TPU v7x, 256 devices: a whole 4x4x8 slice. The times are simulated.
256 devices in a mesh: row: 16 (over z, core), col: 16 (over x, y).
Axes of the slice: x: 4, y: 4, z: 8, core: 2. Of those that a mesh axis runs over, the one named last changes fastest.
Arguments:
- sire_index: int32 [2048], P('row'), may hold values from 0 to 8191
- dam_index: int32 [2048], P('row'), may hold values from -1 to 8191, as said below
- relatives: float32 [8192, 4, 2048], P('row', None, 'col'), may hold values from 0 to 1
- factor_blocks: float32 [6, 2048, 2048], P(None, 'row', 'col'), may hold values from -0.125 to 0.125
- inverses: float32 [4, 2048, 2048], P(None, 'col'), as said below
Outputs:
- relationship: float32 [4, 2048, 2048], P(None, 'col', 'row')
- border: float32 [4, 2048, 2048], P(None, 'col', 'row')
Inputs may be any that keep to these rules, and one draw needn't show every extreme that they name: `dam_index`: -1 marks an unknown dam; every other value is a row of relatives. `inverses`: lower triangular, with diagonal entries of 0.6 to 1.4.
All inputs are finite; a program needn't handle non-finite values.
Results may differ from a plain program's by a relative error of at most 0.0001.
Values sent between devices are 32-bit elements; how exact they have to be, the bound alone decides.
No kernel may reach another device: no remote copies, remote signals or barrier semaphores. Data moves between devices by JAX's collectives and lax.ppermute only.
A program may use at most 64 MiB of HBM per device.

v0:
```python
import jax
import jax.numpy as jnp
from jax import lax
from jax.sharding import PartitionSpec as P


def product(left, right):
    return jnp.dot(left, right, precision=lax.Precision.HIGHEST, preferred_element_type=jnp.float32)


def fetch_rows(stacked):
    return lax.all_gather(stacked, "row", axis=0, tiled=True)


def per_device(sire_index, dam_index, relatives, factor_blocks, inverses):
    calf_dev = sire_index.shape[0]
    old_dev, blocks, block_cols = relatives.shape
    piece = lax.all_gather(relatives, "row", axis=0, tiled=True)
    add_count = piece.shape[0]
    row_ids = lax.iota(jnp.int32, add_count)
    picks = 0.5 * (
        (row_ids[:, None] == sire_index[None, :]).astype(jnp.float32)
        + (row_ids[:, None] == dam_index[None, :]).astype(jnp.float32)
    )
    gathered = piece.reshape(add_count, blocks * block_cols)
    relation = lax.dot_general(
        gathered,
        picks,
        (((0,), (0,)), ((), ())),
        precision=lax.Precision.HIGHEST,
        preferred_element_type=jnp.float32,
    )
    relationship = relation.reshape(blocks, block_cols, calf_dev)
    solved = []
    for target in range(blocks):
        remain = relationship[target]
        if target > 0:
            needed = jnp.stack(
                [factor_blocks[target * (target - 1) // 2 + source] for source in range(target)],
                axis=1,
            )
            whole_rows = fetch_rows(needed).reshape(-1, target * block_cols)
            earlier = jnp.concatenate(solved, axis=0)

            def earlier_terms(start, count, whole_rows=whole_rows, earlier=earlier):
                return product(whole_rows, earlier)

            remain = remain - lax.psum_scatter(
                earlier_terms(jnp.int32(0), block_cols * lax.axis_size("col")),
                "col",
                scatter_dimension=0,
                tiled=True,
            )
        own_inverse = inverses[target]
        solved.append(product(own_inverse, lax.all_gather(remain, "col", axis=0, tiled=True)))
    return (relationship, jnp.stack(solved))


def solution(mesh):
    return jax.shard_map(
        per_device,
        mesh=mesh,
        in_specs=(
            P("row"),
            P("row"),
            P("row", None, "col"),
            P(None, "row", "col"),
            P(None, "col", None),
        ),
        out_specs=(P(None, "col", "row"), P(None, "col", "row")),
        check_vma=False,
    )
```

profile of v0, /device:TPU:8, one launch (start us, length us, event | category | flops | bytes accessed | tf_op | source)
XLA Modules:
  0.0 706.6 jit_solution(13004612064108362385)
XLA Ops:
  7.9 100.2 %all-gather.10.cloned.1.call-done = f32[8192,4,128]{2,1,0:T(4,128)} async-done(((f32[512,4,128]{2,1,0:T(4,128)}), f32[8192,4,128]{2,1,0:T(4,128)}) %all-gather.10.cloned.1.call-update) | async-done | bytes 16777232 | tf_op jit(solution)/shard_map/all_gather | solution.py:18
  108.2 15.4 %fusion.10 = f32[512,128]{0,1:T(8,128)S(1)} fusion(f32[1024,8,4,128]{3,2,1,0:T(4,128)} %bitcast.53, s32[128]{0:T(128)} %param.6, s32[128]{0:T(128)} %param.5), kind=kOutput, calls=%fused_computation.13 | convolution fusion | flops 6448742400 | bytes 17040384 | tf_op jit(solution)/shard_map/dot_general | solution.py:26
  125.0 45.9 %all-gather.12.cloned.1.call-done = f32[2048,128]{0,1:T(8,128)} async-done(((f32[128,128]{0,1:T(8,128)}), f32[2048,128]{0,1:T(8,128)}) %all-gather.12.cloned.1.call-update) | async-done | bytes 1048592 | tf_op jit(solution)/shard_map/all_gather | solution.py:55
  170.9 2.5 fusion.21
  173.5 38.3 %all-gather.24.cloned.1.call-done = f32[1,2048,128]{2,1,0:T(8,128)} async-done(((f32[1,128,128]{2,1,0:T(8,128)}), f32[1,2048,128]{2,1,0:T(8,128)}) %all-gather.24.cloned.1.call-update) | async-done | bytes 1048592 | tf_op jit(solution)/shard_map/all_gather | solution.py:12
  211.7 3.2 convolution_bitcast_fusion
  215.1 76.4 %reduce-scatter.4.cloned.1.call-done = f32[128,128]{0,1:T(8,128)} async-done(((f32[2048,128]{0,1:T(8,128)}), f32[128,128]{0,1:T(8,128)}) %reduce-scatter.4.cloned.1.call-update) | async-done | bytes 65552 | tf_op jit(solution)/shard_map/reduce_scatter | solution.py:48
  291.5 1.5 slice_subtract_fusion.2
  294.0 48.4 %all-gather.14.cloned.1.call-done = f32[2048,128]{0,1:T(8,128)} async-done(((f32[128,128]{0,1:T(8,128)}), f32[2048,128]{0,1:T(8,128)}) %all-gather.14.cloned.1.call-update) | async-done | bytes 1048592 | tf_op jit(solution)/shard_map/all_gather | solution.py:55
  342.4 2.5 fusion.18
  344.9 40.5 %all-gather.16.cloned.1.call-done = f32[2048,2,128]{0,2,1:T(8,128)} async-done(((f32[128,2,128]{0,2,1:T(8,128)}), f32[2048,2,128]{0,2,1:T(8,128)}) %all-gather.16.cloned.1.call-update) | async-done | bytes 2097168 | tf_op jit(solution)/shard_map/all_gather | solution.py:12
  385.4 3.9 fusion.33
  389.4 76.8 %reduce-scatter.6.cloned.1.call-done = f32[128,128]{0,1:T(8,128)} async-done(((f32[2048,128]{0,1:T(8,128)}), f32[128,128]{0,1:T(8,128)}) %reduce-scatter.6.cloned.1.call-update) | async-done | bytes 65552 | tf_op jit(solution)/shard_map/reduce_scatter | solution.py:48
  466.2 1.5 slice_subtract_fusion.1
  469.0 47.9 %all-gather.18.cloned.1.call-done = f32[2048,128]{0,1:T(8,128)} async-done(((f32[128,128]{0,1:T(8,128)}), f32[2048,128]{0,1:T(8,128)}) %all-gather.18.cloned.1.call-update) | async-done | bytes 1048592 | tf_op jit(solution)/shard_map/all_gather | solution.py:55
  516.9 2.5 fusion.16
  519.5 44.8 %all-gather.20.cloned.1.call-done = f32[2048,3,128]{0,2,1:T(8,128)} async-done(((f32[128,3,128]{0,2,1:T(8,128)}), f32[2048,3,128]{0,2,1:T(8,128)}) %all-gather.20.cloned.1.call-update) | async-done | bytes 3145744 | tf_op jit(solution)/shard_map/all_gather | solution.py:12
  564.2 5.0 fusion.27
  569.3 76.4 %reduce-scatter.8.cloned.1.call-done = f32[128,128]{0,1:T(8,128)} async-done(((f32[2048,128]{0,1:T(8,128)}), f32[128,128]{0,1:T(8,128)}) %reduce-scatter.8.cloned.1.call-update) | async-done | bytes 65552 | tf_op jit(solution)/shard_map/reduce_scatter | solution.py:48
  645.8 1.5 slice_subtract_fusion
  647.3 0.8 copy.28
  648.1 48.7 %all-gather.22.cloned.1.call-done = f32[2048,128]{0,1:T(8,128)} async-done(((f32[128,128]{0,1:T(8,128)}), f32[2048,128]{0,1:T(8,128)}) %all-gather.22.cloned.1.call-update) | async-done | bytes 1048592 | tf_op jit(solution)/shard_map/all_gather | solution.py:55
  696.8 2.5 convolution_bitcast_fusion.1
  699.3 0.7 pad_maximum_fusion
  (33 shorter events, 4.6 us)
Async XLA Ops:
  7.2 101.0 %all-gather.10.cloned.1.call-start = ((), (), s32[]{:S(2)}) async-start(), calls=%async_computation.3 | async-start | bytes 17825792 | tf_op jit(solution)/shard_map/all_gather | solution.py:18
  7.9 163.0 %all-gather.12.cloned.1.call-start = ((), (), s32[]{:S(2)}) async-start(), calls=%async_computation.4 | async-start | bytes 1114112 | tf_op jit(solution)/shard_map/all_gather | solution.py:55
  108.2 16.1 %copy-start = (f32[6,128,128]{2,1,0:T(8,128)S(1)}, f32[6,128,128]{2,1,0:T(8,128)}, u32[]{:S(2)}) copy-start(f32[6,128,128]{2,1,0:T(8,128)} %param.8) | copy-start | bytes 1179652
  124.2 87.5 %all-gather.24.cloned.1.call-start = ((), (), s32[]{:S(2)}) async-start(), calls=%async_computation.13 | async-start | bytes 1114112 | tf_op jit(solution)/shard_map/all_gather | solution.py:12
  125.0 166.5 %reduce-scatter.4.cloned.1.call-start = ((), (), s32[]{:S(2)}) async-start(), calls=%async_computation.5 | async-start | bytes 1114112 | tf_op jit(solution)/shard_map/reduce_scatter | solution.py:48
  215.0 127.3 %all-gather.14.cloned.1.call-start = ((), (), s32[]{:S(2)}) async-start(), calls=%async_computation.6 | async-start | bytes 1114112 | tf_op jit(solution)/shard_map/all_gather | solution.py:55
  293.0 92.5 %all-gather.16.cloned.1.call-start = ((), (), s32[]{:S(2)}) async-start(), calls=%async_computation.7 | async-start | bytes 2228224 | tf_op jit(solution)/shard_map/all_gather | solution.py:12
  293.9 172.3 %reduce-scatter.6.cloned.1.call-start = ((), (), s32[]{:S(2)}) async-start(), calls=%async_computation.8 | async-start | bytes 1114112 | tf_op jit(solution)/shard_map/reduce_scatter | solution.py:48
  389.4 127.6 %all-gather.18.cloned.1.call-start = ((), (), s32[]{:S(2)}) async-start(), calls=%async_computation.9 | async-start | bytes 1114112 | tf_op jit(solution)/shard_map/all_gather | solution.py:55
  467.7 96.5 %all-gather.20.cloned.1.call-start = ((), (), s32[]{:S(2)}) async-start(), calls=%async_computation.10 | async-start | bytes 3342336 | tf_op jit(solution)/shard_map/all_gather | solution.py:12
  468.8 177.0 %reduce-scatter.8.cloned.1.call-start = ((), (), s32[]{:S(2)}) async-start(), calls=%async_computation.11 | async-start | bytes 1114112 | tf_op jit(solution)/shard_map/reduce_scatter | solution.py:48
  569.3 127.5 %all-gather.22.cloned.1.call-start = ((), (), s32[]{:S(2)}) async-start(), calls=%async_computation.12 | async-start | bytes 1114112 | tf_op jit(solution)/shard_map/all_gather | solution.py:55
Sparse Core Ops, SparseCore 0:
  9.8 98.2 all-gather.9
  124.4 46.5 all-gather.11
  173.3 38.3 all-gather.23
  215.1 76.2 reduce-scatter.3
  294.6 47.7 all-gather.13
  344.7 40.7 all-gather.15
  389.5 76.6 reduce-scatter.5
  469.2 47.6 all-gather.17
  519.3 44.9 all-gather.19
  569.4 76.2 reduce-scatter.7
  649.0 47.7 all-gather.21
where the time goes:
time: 707 us
  waiting for transfers between devices  645 us (91%)
  matrix products  37.7 us (5%)
  between operations  14 us (2%)
    reduce_scatter x3, waiting for transfers between devices, per_device(): lax.psum_scatter(earlier_terms(jnp.int32(0), block_cols * lax.axis_size('...  230 us
    all_gather x4, waiting for transfers between devices, per_device(): lax.all_gather(remain, 'col', axis=0, tiled=True)  191 us
    all_gather x3, waiting for transfers between devices, fetch_rows(): return lax.all_gather(stacked, 'row', axis=0, tiled=True)  124 us
    all_gather x1, waiting for transfers between devices, per_device(): piece = lax.all_gather(relatives, 'row', axis=0, tiled=True)  100 us
    dot_general x7, matrix products, product(): jnp.dot(left, right, precision=lax.Precision.HIGHEST, preferred_element_t...  22.3 us
    dot_general x1, matrix products, per_device(): lax.dot_general(gathered, picks, (((0,), (0,)), ((), ())), precision=lax....  15.4 us
  transfers between devices with their start and end apart: 11, of which 11 were waited for; matrix products, arithmetic and copies ran while one was open for 2% of the time, Pallas kernels for 0%

commit v1 on v0

v1 whole, which is shorter than its diff:
```python
import jax
import jax.numpy as jnp
from jax import lax
from jax.sharding import Mesh, PartitionSpec as P

ROW = ("z", "core")
COL = ("x", "y")
BLOCKS = 4


def product(left, right):
    return jnp.dot(left, right, precision=lax.Precision.HIGH, preferred_element_type=jnp.float32)


def pieces(value):
    high = lax.reduce_precision(value, 8, 7)
    rest = value - high
    middle = lax.reduce_precision(rest, 8, 7)
    return [part.astype(jnp.bfloat16) for part in (high, middle, rest - middle)]


def gather_col(block):
    copies = jnp.broadcast_to(block[None], (16,) + block.shape)
    return lax.all_to_all(copies, COL, 0, 0, tiled=True).reshape(-1, block.shape[1])


def scatter_sum_col(partial):
    parts = lax.all_to_all(partial, COL, 0, 0, tiled=True)
    return jnp.sum(parts.reshape(16, -1, partial.shape[1]), axis=0)


def per_device(sire_index, dam_index, relatives, factor_blocks, inverses):
    old_dev, blocks, width = relatives.shape
    calf_dev = sire_index.shape[0]
    core = lax.axis_index("core")
    me = lax.axis_index(ROW)

    whole = lax.all_gather(factor_blocks, ROW, axis=1, tiled=True)

    index = lax.all_gather(jnp.stack([sire_index, dam_index]), ROW, axis=0, tiled=False)
    ids = me * old_dev + lax.iota(jnp.int32, old_dev)
    sire = index[:, 0, :, None] == ids
    dam = index[:, 1, :, None] == ids
    picks = 0.5 * (sire.astype(jnp.float32) + dam.astype(jnp.float32))
    picks = picks.astype(jnp.bfloat16).reshape(-1, old_dev)

    def partial(first, count):
        rows = relatives[:, first : first + count, :].reshape(old_dev, count * width)
        total = 0.0
        for piece in pieces(rows):
            total = total + jnp.dot(picks, piece, preferred_element_type=jnp.float32)
        return total.reshape(8, 2, calf_dev, count * width)

    def over_core(terms):
        keep = lax.dynamic_index_in_dim(terms, core, 1, keepdims=False)
        give = lax.dynamic_index_in_dim(terms, 1 - core, 1, keepdims=False)
        return keep + lax.ppermute(give, "core", [(0, 1), (1, 0)])

    first = lax.all_to_all(over_core(partial(0, 1)), "z", 0, 0, tiled=False)
    relation = [jnp.sum(first, axis=0).T]
    later = over_core(partial(1, blocks - 1)).reshape(8 * calf_dev, -1)
    later = lax.psum_scatter(later, "z", scatter_dimension=0, tiled=True)
    for target in range(1, blocks):
        relation.append(later[:, (target - 1) * width : target * width].T)

    solved = []
    for target in range(blocks):
        remain = relation[target]
        if target > 0:
            terms = 0.0
            for source in range(target):
                block = whole[target * (target - 1) // 2 + source]
                terms = terms + product(block, solved[source])
            remain = remain - scatter_sum_col(terms)
        solved.append(product(inverses[target], gather_col(remain)))
    return jnp.stack(relation), jnp.stack(solved)


def solution(mesh):
    fine = Mesh(mesh.devices.reshape(8, 2, 4, 4), ROW + COL)
    return jax.shard_map(
        per_device,
        mesh=fine,
        in_specs=(
            P(ROW),
            P(ROW),
            P(ROW, None, COL),
            P(None, ROW, COL),
            P(None, COL, None),
        ),
        out_specs=(P(None, COL, ROW), P(None, COL, ROW)),
        check_vma=False,
    )
```

time: 707 us -> 235 us (0.33)
  waiting for transfers between devices: 645 us -> 51.5 us
  blocking collectives: 0 us -> 97.3 us
  starting transfers between devices: 0.63 us -> 19.5 us
  matrix products: 37.7 us -> 27.6 us
  local copies, waits for them, and re-layouts: 2.59 us -> 12.1 us
    all_gather x8 -> x1, waiting for transfers between devices: 415 us -> 0.02 us  [per_device(): whole = lax.all_gather(factor_blocks, ROW, axis=1, tiled=True)]
    reduce_scatter x3 -> x1, waiting for transfers between devices: 230 us -> 0.03 us  [per_device(): later = lax.psum_scatter(later, 'z', scatter_dimension=0, tiled=True)]
    all_to_all x0 -> x4, blocking collectives: none -> 77.4 us  [the longest x3 54.9 us: scatter_sum_col(): parts = lax.all_to_all(partial, COL, 0, 0, tiled=True)]
    all_to_all x0 -> x4, waiting for transfers between devices: none -> 48.7 us  [the longest x3 32 us: gather_col(): lax.all_to_all(copies, COL, 0, 0, tiled=True).reshape(-1, block.shape[1])]
    all_gather x0 -> x1, blocking collectives: none -> 20 us  [per_device(): lax.all_gather(jnp.stack([sire_index, dam_index]), ROW, axis=0, tiled=False)]
    all_to_all x0 -> x4, starting transfers between devices: none -> 18.9 us  [the longest x3 14.7 us: gather_col(): lax.all_to_all(copies, COL, 0, 0, tiled=True).reshape(-1, block.shape[1])]
    dot_general x8 -> x16, matrix products: 37.7 us -> 27.6 us  [the longest x10 19.7 us: product(): jnp.dot(left, right, precision=lax.Precision.HIGH, preferred_element_type...]
  transfers between devices with their start and end apart: 11 -> 8, of which waited for: 11 -> 5; matrix products, arithmetic and copies ran while one was open for 2% -> 13% of each run, Pallas kernels for 0% -> 0%
where the time goes in v1:
time: 235 us; the launch traced here: 231 us
  blocking collectives  97.3 us (41%)
  waiting for transfers between devices  51.5 us (22%)
  matrix products  27.6 us (12%)
  starting transfers between devices  19.5 us (8%)
  between operations  15.8 us (7%)
  local copies, waits for them, and re-layouts  12.1 us (5%)
  other arithmetic  7.27 us (3%)
    all_to_all x3, blocking collectives, scatter_sum_col(): parts = lax.all_to_all(partial, COL, 0, 0, tiled=True)  54.9 us
    all_to_all x3, waiting for transfers between devices, gather_col(): lax.all_to_all(copies, COL, 0, 0, tiled=True).reshape(-1, block.shape[1])  32 us
    all_to_all x1, blocking collectives, gather_col(): lax.all_to_all(copies, COL, 0, 0, tiled=True).reshape(-1, block.shape[1])  22.5 us
    all_gather x1, blocking collectives, per_device(): lax.all_gather(jnp.stack([sire_index, dam_index]), ROW, axis=0, tiled=False)  20 us
    dot_general x10, matrix products, product(): jnp.dot(left, right, precision=lax.Precision.HIGH, preferred_element_type...  19.7 us
    all_to_all x1, waiting for transfers between devices, per_device(): first = lax.all_to_all(over_core(partial(0, 1)), 'z', 0, 0, tiled=False)  16.7 us
    all_to_all x3, starting transfers between devices, gather_col(): lax.all_to_all(copies, COL, 0, 0, tiled=True).reshape(-1, block.shape[1])  14.7 us
    dot_general x6, matrix products, partial(): total = total + jnp.dot(picks, piece, preferred_element_type=jnp.float32)  7.87 us
  transfers between devices with their start and end apart: 8, of which 5 were waited for; matrix products, arithmetic and copies ran while one was open for 13% of the time, Pallas kernels for 0%

profile of v1, /device:TPU:8, one launch (start us, length us, event | category | flops | bytes accessed | tf_op | source)
XLA Modules:
  0.0 231.1 jit_solution(14973829101370196413)
XLA Ops:
  10.6 20.0 %all-gather.1 = s32[16,2,128]{2,1,0:T(2,128)S(1)} all-gather(s32[1,2,128]{2,1,0:T(2,128)S(1)} %add_bitcast_fusion), channel_id=2, replica_groups=mesh['z'=8,'core'=2,'x'=4,'y'=4] {'z','core'}, dimensions={0}, use_global_device_ids=true | all-gather | bytes 17408 | tf_op jit(solution)/shard_map/all_gather | solution.py:40
  43.8 2.0 collective-permute-done
  45.9 2.1 bitcast_add_fusion.1
  47.9 4.1 %all-to-all-start = ((f32[8,128,128]{2,1,0:T(8,128)}), f32[8,128,128]{2,1,0:T(8,128)}, u32[]{:S(2)}, u32[]{:S(2)}) async-start(f32[8,128,128]{2,1,0:T(8,128)} %bitcast_add_fusion.1), calls=%async_computation | async-start | bytes 1048576 | tf_op jit(solution)/shard_map/all_to_all | solution.py:59
  52.2 2.9 %bitcast_add_fusion = f32[8,128,384]{2,1,0:T(8,128)} fusion(f32[8,128,384]{2,1,0:T(8,128)} %collective-permute-done.1, f32[8,2,128,384]{3,2,1,0:T(8,128)S(1)} %bitcast.126, s32[]{:T(128)S(6)} %select_n.10), kind=kLoop, calls=%fused_computation.34 | loop fusion | flops 393216 | bytes 4718596 | tf_op jit(solution)/shard_map/add | solution.py:57
  55.0 16.7 %all-to-all-done = f32[8,128,128]{2,1,0:T(8,128)} async-done(((f32[8,128,128]{2,1,0:T(8,128)}), f32[8,128,128]{2,1,0:T(8,128)}, u32[]{:S(2)}, u32[]{:S(2)}) %all-to-all-start) | async-done | bytes 524320 | tf_op jit(solution)/shard_map/all_to_all | solution.py:59
  73.0 22.5 %all_to_all.52 = f32[16,128,128]{2,1,0:T(8,128)S(1)} all-to-all(f32[16,128,128]{2,1,0:T(8,128)S(1)} %broadcast_in_dim.8), channel_id=1, replica_groups=mesh['z'=8,'core'=2,'x'=4,'y'=4] {'x','y'}, dimensions={0} | all-to-all | bytes 2097152 | tf_op jit(solution)/shard_map/all_to_all | solution.py:24
  95.5 2.2 fusion.36
  99.7 19.9 %all_to_all.53 = f32[16,128,128]{1,2,0:T(8,128)S(1)} all-to-all(f32[16,128,128]{1,2,0:T(8,128)S(1)} %bitcast.132), channel_id=1, replica_groups=mesh['z'=8,'core'=2,'x'=4,'y'=4] {'x','y'}, dimensions={0} | all-to-all | bytes 2097152 | tf_op jit(solution)/shard_map/all_to_all | solution.py:28
  121.7 4.9 %all-to-all-start.3 = ((f32[16,128,128]{2,1,0:T(8,128)}), f32[16,128,128]{2,1,0:T(8,128)S(1)}, u32[]{:S(2)}, u32[]{:S(2)}) async-start(f32[16,128,128]{2,1,0:T(8,128)} %broadcast_in_dim.9), calls=%async_computation.4 | async-start | bytes 2097152 | tf_op jit(solution)/shard_map/all_to_all | solution.py:24
  126.6 1.8 fusion.30
  128.4 12.0 %all-to-all-done.3 = f32[16,128,128]{2,1,0:T(8,128)S(1)} async-done(((f32[16,128,128]{2,1,0:T(8,128)}), f32[16,128,128]{2,1,0:T(8,128)S(1)}, u32[]{:S(2)}, u32[]{:S(2)}) %all-to-all-start.3) | async-done | bytes 1048608 | tf_op jit(solution)/shard_map/all_to_all | solution.py:24
  140.5 2.2 fusion.34
  142.7 1.8 fusion.27
  144.7 18.7 %all_to_all.54 = f32[16,128,128]{1,2,0:T(8,128)S(1)} all-to-all(f32[16,128,128]{1,2,0:T(8,128)S(1)} %bitcast.133), channel_id=1, replica_groups=mesh['z'=8,'core'=2,'x'=4,'y'=4] {'x','y'}, dimensions={0} | all-to-all | bytes 2097152 | tf_op jit(solution)/shard_map/all_to_all | solution.py:28
  164.6 4.9 %all-to-all-start.5 = ((f32[16,128,128]{2,1,0:T(8,128)}), f32[16,128,128]{2,1,0:T(8,128)S(1)}, u32[]{:S(2)}, u32[]{:S(2)}) async-start(f32[16,128,128]{2,1,0:T(8,128)} %broadcast_in_dim.10), calls=%async_computation.6 | async-start | bytes 2097152 | tf_op jit(solution)/shard_map/all_to_all | solution.py:24
  171.3 1.8 convolution_add_fusion.3
  173.1 9.2 %all-to-all-done.5 = f32[16,128,128]{2,1,0:T(8,128)S(1)} async-done(((f32[16,128,128]{2,1,0:T(8,128)}), f32[16,128,128]{2,1,0:T(8,128)S(1)}, u32[]{:S(2)}, u32[]{:S(2)}) %all-to-all-start.5) | async-done | bytes 1048608 | tf_op jit(solution)/shard_map/all_to_all | solution.py:24
  182.3 2.2 fusion.32
  184.6 1.8 fusion.28
  186.5 16.3 %all_to_all.55 = f32[16,128,128]{1,2,0:T(8,128)S(1)} all-to-all(f32[16,128,128]{1,2,0:T(8,128)S(1)} %bitcast.134), channel_id=1, replica_groups=mesh['z'=8,'core'=2,'x'=4,'y'=4] {'x','y'}, dimensions={0} | all-to-all | bytes 2097152 | tf_op jit(solution)/shard_map/all_to_all | solution.py:28
  204.0 4.9 %all-to-all-start.7 = ((f32[16,128,128]{2,1,0:T(8,128)}), f32[16,128,128]{2,1,0:T(8,128)S(1)}, u32[]{:S(2)}, u32[]{:S(2)}) async-start(f32[16,128,128]{2,1,0:T(8,128)} %broadcast_in_dim.11), calls=%async_computation.8 | async-start | bytes 2097152 | tf_op jit(solution)/shard_map/all_to_all | solution.py:24
  209.8 10.7 %all-to-all-done.7 = f32[16,128,128]{2,1,0:T(8,128)S(1)} async-done(((f32[16,128,128]{2,1,0:T(8,128)}), f32[16,128,128]{2,1,0:T(8,128)S(1)}, u32[]{:S(2)}, u32[]{:S(2)}) %all-to-all-start.7) | async-done | bytes 1048608 | tf_op jit(solution)/shard_map/all_to_all | solution.py:24
  220.6 2.2 convolution_bitcast_fusion.1
  (57 shorter events, 27.3 us)
Async XLA Ops:
  8.0 2.6 %copy-start.3 = (s32[128]{0:T(128)S(1)}, s32[128]{0:T(128)}, u32[]{:S(2)}) copy-start(s32[128]{0:T(128)} %param.5) | copy-start | bytes 1540
  8.0 2.6 %copy-start.2 = (s32[128]{0:T(128)S(1)}, s32[128]{0:T(128)}, u32[]{:S(2)}) copy-start(s32[128]{0:T(128)} %param.6) | copy-start | bytes 1540
  8.0 89.8 %all-gather.4.cloned.1.call-start = ((), (), s32[]{:S(2)}) async-start(), calls=%async_computation.10 | async-start | bytes 6684672 | tf_op jit(solution)/shard_map/all_gather | solution.py:38
  36.7 15.5 %collective-permute-start.1 = (f32[8,128,384]{2,1,0:T(8,128)}, f32[8,128,384]{2,1,0:T(8,128)}, u32[]{:S(2)}, u32[]{:S(2)}) collective-permute-start(f32[8,128,384]{2,1,0:T(8,128)} %dynamic-slice_bitcast_fusion), channel_id=1, source_target_pairs={{0,16},{16,0},{1,17},{17,1},{2,18},{18,2},{3,19},{19,3},{4,20},{20... | collective-permute-start | bytes 4718600 | tf_op jit(solution)/shard_map/ppermute | solution.py:57
  41.8 1.0 copy-start
  43.6 2.3 collective-permute-start
  47.9 23.8 %all-to-all-start = ((f32[8,128,128]{2,1,0:T(8,128)}), f32[8,128,128]{2,1,0:T(8,128)}, u32[]{:S(2)}, u32[]{:S(2)}) async-start(f32[8,128,128]{2,1,0:T(8,128)} %bitcast_add_fusion.1), calls=%async_computation | async-start | bytes 1048576 | tf_op jit(solution)/shard_map/all_to_all | solution.py:59
  52.1 67.6 %reduce-scatter.2.cloned.1.call-start = ((), (), s32[]{:S(2)}) async-start(), calls=%async_computation.9 | async-start | bytes 1769472 | tf_op jit(solution)/shard_map/reduce_scatter | solution.py:62
  121.7 18.7 %all-to-all-start.3 = ((f32[16,128,128]{2,1,0:T(8,128)}), f32[16,128,128]{2,1,0:T(8,128)S(1)}, u32[]{:S(2)}, u32[]{:S(2)}) async-start(f32[16,128,128]{2,1,0:T(8,128)} %broadcast_in_dim.9), calls=%async_computation.4 | async-start | bytes 2097152 | tf_op jit(solution)/shard_map/all_to_all | solution.py:24
  142.7 20.7 %copy-start.1 = (f32[128,384]{1,0:T(8,128)S(1)}, f32[128,384]{1,0:T(8,128)}, u32[]{:S(2)}) copy-start(f32[128,384]{1,0:T(8,128)} %reduce-scatter.2.cloned.1.call-done) | copy-start | bytes 589828
  164.6 17.7 %all-to-all-start.5 = ((f32[16,128,128]{2,1,0:T(8,128)}), f32[16,128,128]{2,1,0:T(8,128)S(1)}, u32[]{:S(2)}, u32[]{:S(2)}) async-start(f32[16,128,128]{2,1,0:T(8,128)} %broadcast_in_dim.10), calls=%async_computation.6 | async-start | bytes 2097152 | tf_op jit(solution)/shard_map/all_to_all | solution.py:24
  204.0 16.5 %all-to-all-start.7 = ((f32[16,128,128]{2,1,0:T(8,128)}), f32[16,128,128]{2,1,0:T(8,128)S(1)}, u32[]{:S(2)}, u32[]{:S(2)}) async-start(f32[16,128,128]{2,1,0:T(8,128)} %broadcast_in_dim.11), calls=%async_computation.8 | async-start | bytes 2097152 | tf_op jit(solution)/shard_map/all_to_all | solution.py:24
Sparse Core Ops, SparseCore 0:
  10.7 54.2 all-gather.3
Sparse Core Ops, SparseCore 1:
  55.1 41.9 reduce-scatter.1

commit v2 on v1

v2 whole, which is shorter than its diff:
```python
import functools

import jax
import jax.numpy as jnp
from jax import lax
from jax.experimental import pallas as pl
from jax.experimental.pallas import tpu as pltpu
from jax.sharding import Mesh, PartitionSpec as P

ROW = ("z", "core")
COL = ("x", "y")
OLD = 512
SIDE = 128
GROUP = 16
LIMIT = 24 << 20
F32 = jnp.float32
BF16 = jnp.bfloat16
SMEM = pl.BlockSpec(memory_space=pltpu.SMEM)
VMEM = pl.BlockSpec(memory_space=pltpu.VMEM)
PARAMS = pltpu.CompilerParams(vmem_limit_bytes=LIMIT)


def pieces(value):
    high = lax.reduce_precision(value, 8, 7)
    rest = value - high
    middle = lax.reduce_precision(rest, 8, 7)
    return [part.astype(BF16) for part in (high, middle, rest - middle)]


def halves(value):
    high = value.astype(BF16)
    return high, (value - high.astype(F32)).astype(BF16)


def select_kernel(count, here, index, rows, after, keep, give):
    core, base = here[2], here[3]
    ids = lax.broadcasted_iota(jnp.int32, (OLD, SIDE), 0) + base

    def picks(owner):
        pair = index[owner]
        sire = jnp.where(ids == pair[0:1, :], 0.5, 0.0)
        dam = jnp.where(ids == pair[1:2, :], 0.5, 0.0)
        return (sire + dam).astype(BF16)

    @pl.loop(0, 8)
    def _(z):
        both = jnp.concatenate([picks(2 * z + core), picks(2 * z + 1 - core)], axis=1)
        size = count * SIDE
        total = jnp.dot(rows[:size], both, preferred_element_type=F32)
        for piece in (1, 2):
            total += jnp.dot(rows[piece * size : (piece + 1) * size], both, preferred_element_type=F32)
        keep[z] = total[:, :SIDE]
        give[z] = total[:, SIDE:]


def select(count, here, index, rows, after):
    shape = jax.ShapeDtypeStruct((8, count * SIDE, SIDE), F32)
    return pl.pallas_call(
        functools.partial(select_kernel, count),
        out_shape=(shape, shape),
        in_specs=[SMEM, VMEM, VMEM, pl.BlockSpec(memory_space=pl.ANY)],
        out_specs=(VMEM, VMEM),
        cost_estimate=pl.CostEstimate(
            flops=2 * 3 * count * SIDE * OLD * 2048, bytes_accessed=count << 20, transcendentals=0
        ),
        compiler_params=PARAMS,
        name="select",
    )(here, index, rows, after)


def remain_kernel(minus, *refs):
    terms = refs[0]
    total = terms[0]
    for part in range(1, terms.shape[0]):
        total += terms[part]
    if minus:
        total = refs[1][0] - total
    else:
        refs[1][...] = total
    for owner in range(GROUP):
        refs[2][owner] = total


def spread(terms, minuend=None, block=0):
    copies = jax.ShapeDtypeStruct((GROUP, SIDE, SIDE), F32)
    copies_spec = pl.BlockSpec(copies.shape, lambda i: (0, 0, 0))
    terms_spec = pl.BlockSpec(terms.shape, lambda i: (0, 0, 0))
    if minuend is None:
        return pl.pallas_call(
            functools.partial(remain_kernel, False),
            out_shape=(jax.ShapeDtypeStruct((SIDE, SIDE), F32), copies),
            grid=(1,),
            in_specs=[terms_spec],
            out_specs=(pl.BlockSpec((SIDE, SIDE), lambda i: (0, 0)), copies_spec),
            compiler_params=PARAMS,
            name="sum_first",
        )(terms)
    return pl.pallas_call(
        functools.partial(remain_kernel, True),
        out_shape=copies,
        grid=(1,),
        in_specs=[terms_spec, pl.BlockSpec((1, SIDE, SIDE), lambda i: (block, 0, 0))],
        out_specs=copies_spec,
        compiler_params=PARAMS,
        name="subtract",
    )(terms, minuend)


def solve_kernel(target, last, *refs):
    whole, inverse = refs[0], refs[1]
    factors = refs[2 : 2 + (0 if last else target + 1)]
    before = refs[2 + len(factors) : 2 + len(factors) + (0 if last else target)]
    solved = refs[2 + len(factors) + len(before)]
    high, low = halves(whole[...].reshape(GROUP * SIDE, SIDE))
    left, left_low = halves(inverse[0])
    wide = jnp.dot(left, jnp.concatenate([high, low], axis=1), preferred_element_type=F32)
    own = wide[:, :SIDE] + wide[:, SIDE:] + jnp.dot(left_low, high, preferred_element_type=F32)
    solved[...] = own
    if last:
        return
    terms = refs[-1]
    rights = [one[...] for one in before] + [own]
    for first in range(0, target + 1, 2):
        some = range(first, min(first + 2, target + 1))
        right = jnp.concatenate([rights[source] for source in some], axis=0)
        high, low = halves(right)
        right = jnp.concatenate([high, low], axis=1)
        for part in range(4):
            rows = pl.ds(part * 4 * SIDE, 4 * SIDE)
            left = jnp.concatenate([factors[source][0, rows] for source in some], axis=1)
            left, left_low = halves(left)
            wide = jnp.dot(left, right, preferred_element_type=F32)
            term = wide[:, :SIDE] + wide[:, SIDE:] + jnp.dot(left_low, high, preferred_element_type=F32)
            term = term.reshape(4, SIDE, SIDE)
            if first == 0:
                terms[pl.ds(part * 4, 4)] = term
            else:
                terms[pl.ds(part * 4, 4)] += term


def solve(target, whole, inverses, factor, before):
    last = target + 1 == inverses.shape[0]
    count = 0 if last else target + 1
    first = target * (target + 1) // 2
    one = jax.ShapeDtypeStruct((SIDE, SIDE), F32)
    one_spec = pl.BlockSpec(one.shape, lambda i: (0, 0))
    group = jax.ShapeDtypeStruct((GROUP, SIDE, SIDE), F32)
    group_spec = pl.BlockSpec(group.shape, lambda i: (0, 0, 0))
    out = pl.pallas_call(
        functools.partial(solve_kernel, target, last),
        out_shape=(one,) if last else (one, group),
        grid=(1,),
        in_specs=[group_spec, pl.BlockSpec((1, SIDE, GROUP * SIDE), lambda i: (target, 0, 0))]
        + [pl.BlockSpec((1, GROUP * SIDE, SIDE), lambda i, at=first + k: (at, 0, 0)) for k in range(count)]
        + [one_spec] * (0 if last else target),
        out_specs=(one_spec,) if last else (one_spec, group_spec),
        compiler_params=PARAMS,
        name="solve",
    )(whole, inverses, *[factor] * count, *([] if last else before))
    return (out[0], None) if last else out


def to_group(parts):
    return lax.all_to_all(parts, COL, 0, 0)


def per_device(sire_index, dam_index, relatives, factor_blocks, inverses):
    old_dev, blocks, _ = relatives.shape
    here = jnp.stack([jnp.int32(0), jnp.int32(0), lax.axis_index("core"), lax.axis_index(ROW) * old_dev])
    here = here.astype(jnp.int32)
    swap = [(0, 1), (1, 0)]

    factor = lax.all_gather(factor_blocks, ROW, axis=1, tiled=True)
    factor = pltpu.with_memory_space_constraint(factor, pltpu.HBM)
    inverses = pltpu.with_memory_space_constraint(inverses, pltpu.HBM)

    pair = jnp.stack([sire_index, dam_index])
    index = lax.all_to_all(jnp.broadcast_to(pair[None], (GROUP, 2, SIDE)), ROW, 0, 0)

    def rows_of(first, count):
        rows = relatives[:, first : first + count, :].reshape(old_dev, count * SIDE).T
        return jnp.concatenate(pieces(rows))

    keep, give = select(1, here, index, rows_of(0, 1), here)
    first_terms = keep + lax.ppermute(give, "core", swap)
    relation0, copies = spread(lax.all_to_all(first_terms, "z", 0, 0))

    keep, give = select(blocks - 1, here, index, rows_of(1, blocks - 1), first_terms)
    terms = keep + lax.ppermute(give, "core", swap)
    later = lax.psum_scatter(terms.reshape(-1, SIDE), "z", scatter_dimension=0, tiled=True)
    later = later.reshape(blocks - 1, SIDE, SIDE)

    solved = []
    for target in range(blocks):
        if target > 0:
            copies = spread(to_group(terms), later, target - 1)
        own, terms = solve(target, to_group(copies), inverses, factor, solved)
        solved.append(own)
    relationship = jnp.concatenate([relation0[None], later])
    return relationship, jnp.stack(solved)


def solution(mesh):
    fine = Mesh(mesh.devices.reshape(8, 2, 4, 4), ROW + COL)
    return jax.shard_map(
        per_device,
        mesh=fine,
        in_specs=(
            P(ROW),
            P(ROW),
            P(ROW, None, COL),
            P(None, ROW, COL),
            P(None, COL, None),
        ),
        out_specs=(P(None, COL, ROW), P(None, COL, ROW)),
        check_vma=False,
    )
```

time: 235 us -> 220 us (0.936); the launches traced: 231 us -> 219 us
  matrix products: 27.6 us -> 0 us
  blocking collectives: 97.3 us -> 119 us
  Pallas kernels: 0 us -> 21.6 us
  waiting for transfers between devices: 51.5 us -> 36.2 us
  local copies, waits for them, and re-layouts: 12.1 us -> 3.65 us
  other arithmetic: 7.27 us -> 3.97 us
    all_to_all x4 -> x6, blocking collectives: 77.4 us -> 119 us  [the longest x5 92.6 us: to_group(): return lax.all_to_all(parts, COL, 0, 0)]
    dot_general x16 -> x0, matrix products: 27.6 us -> none  [the longest x10 19.7 us: product(): jnp.dot(left, right, precision=lax.Precision.HIGH, preferred_element_type...]
    pallas_call x0 -> x10, Pallas kernels: none -> 21.6 us  [the longest x4 11.8 us: solve(): pl.pallas_call(functools.partial(solve_kernel, target, last), out_shape=(...]
    all_gather x1 -> x0, blocking collectives: 20 us -> none  [per_device(): lax.all_gather(jnp.stack([sire_index, dam_index]), ROW, axis=0, tiled=False)]
    all_to_all x4 -> x3, waiting for transfers between devices: 48.7 us -> 30.7 us  [the longest x2 25.5 us: to_group(): return lax.all_to_all(parts, COL, 0, 0)]
    add x3 -> x2, other arithmetic: 4.93 us -> 1.43 us  [the longest x1 1.36 us: per_device(): terms = keep + lax.ppermute(give, 'core', swap)]
    ppermute x2, waiting for transfers between devices: 2.04 us -> 4.81 us  [the longest x1 3.27 us: per_device(): terms = keep + lax.ppermute(give, 'core', swap)]
    broadcast_in_dim x4 -> x1, local copies, waits for them, and re-layouts: 3.38 us -> 0.61 us  [per_device(): jnp.broadcast_to(pair[None], (GROUP, 2, SIDE))]
  transfers between devices with their start and end apart: 8 -> 7, of which waited for: 5 -> 5; matrix products, arithmetic and copies ran while one was open for 13% -> 3% of each run, Pallas kernels for 0% -> 5%
where the time goes in v2:
time: 220 us; the launch traced here: 219 us
  blocking collectives  119 us (54%)
  waiting for transfers between devices  36.2 us (16%)
  Pallas kernels  21.6 us (10%)
  starting transfers between devices  18.9 us (9%)
  between operations  15.6 us (7%)
  other arithmetic  3.97 us (2%)
  local copies, waits for them, and re-layouts  3.65 us (2%)
    all_to_all x5, blocking collectives, to_group(): return lax.all_to_all(parts, COL, 0, 0)  92.6 us
    all_to_all x1, blocking collectives, per_device(): relation0, copies = spread(lax.all_to_all(first_terms, 'z', 0, 0))  26.4 us
    all_to_all x2, waiting for transfers between devices, to_group(): return lax.all_to_all(parts, COL, 0, 0)  25.5 us
    pallas_call x4, Pallas kernels, solve(): pl.pallas_call(functools.partial(solve_kernel, target, last), out_shape=(...  11.8 us
    all_to_all x2, starting transfers between devices, to_group(): return lax.all_to_all(parts, COL, 0, 0)  9.83 us
    all_to_all x1, starting transfers between devices, per_device(): lax.all_to_all(jnp.broadcast_to(pair[None], (GROUP, 2, SIDE)), ROW, 0, 0)  8.57 us
    pallas_call x2, Pallas kernels, select(): pl.pallas_call(functools.partial(select_kernel, count), out_shape=(shape,...  8.27 us
    all_to_all x1, waiting for transfers between devices, per_device(): lax.all_to_all(jnp.broadcast_to(pair[None], (GROUP, 2, SIDE)), ROW, 0, 0)  5.24 us
  transfers between devices with their start and end apart: 7, of which 5 were waited for; matrix products, arithmetic and copies ran while one was open for 3% of the time, Pallas kernels for 5%

profile of v2, /device:TPU:8, one launch (start us, length us, event | category | flops | bytes accessed | tf_op | source)
XLA Modules:
  0.0 219.0 jit_solution(6681439813823876035)
XLA Ops:
  10.0 8.6 %all-to-all-start = ((s32[16,2,128]{2,1,0:T(2,128)}), s32[16,2,128]{2,1,0:T(2,128)S(1)}, u32[]{:S(2)}, u32[]{:S(2)}) async-start(s32[16,2,128]{2,1,0:T(2,128)} %broadcast_in_dim.4), calls=%async_computation | async-start | bytes 32768 | tf_op jit(solution)/shard_map/all_to_all | solution.py:178
  18.7 1.4 slice.6
  21.0 5.2 %all-to-all-done.index = s32[16,2,128]{2,1,0:T(2,128)S(1)} async-done(((s32[16,2,128]{2,1,0:T(2,128)}), s32[16,2,128]{2,1,0:T(2,128)S(1)}, u32[]{:S(2)}, u32[]{:S(2)}) %all-to-all-start) | async-done | bytes 16416 | tf_op jit(solution)/shard_map/all_to_all | solution.py:178
  26.2 3.3 %select.2 = (f32[8,128,128]{2,1,0:T(8,128)S(1)}, f32[8,128,128]{2,1,0:T(8,128)S(1)}) custom-call(s32[4]{0:T(128)S(1)} %pad_add_fusion.1.here.after, s32[16,2,128]{2,1,0:T(2,128)S(1)} %all-to-all-done.index, bf16[384,512]{1,0:T(8,128)(2,1)S(1)} %pad_maximum_fusion.1.rows, s32[4]{0:T(128)S(1)} %pad_add_fusion.1.here.after), custom_call_target="tpu_custom_call" | custom-call | flops 805306368 | bytes 1048576 | tf_op jit(solution)/shard_map/select/pallas_call | solution.py:58
  30.0 1.5 collective-permute-done
  31.6 4.9 %select.3 = (f32[8,384,128]{2,1,0:T(8,128)S(1)}, f32[8,384,128]{2,1,0:T(8,128)S(1)}) custom-call(s32[4]{0:T(128)S(1)} %pad_add_fusion.1.here.after, s32[16,2,128]{2,1,0:T(2,128)S(1)} %all-to-all-done.index, bf16[1152,512]{1,0:T(8,128)(2,1)S(1)} %pad_maximum_fusion.rows, f32[8,128,128]{2,1,0:T(8,128)S(1)} %add.12.after), custom_call_target="tpu_custom_call" | custom-call | flops 2415919104 | bytes 3145728 | tf_op jit(solution)/shard_map/select/pallas_call | solution.py:58
  36.8 3.3 %collective-permute-done.1 = f32[8,384,128]{2,1,0:T(8,128)S(1)} collective-permute-done((f32[8,384,128]{2,1,0:T(8,128)S(1)}, f32[8,384,128]{2,1,0:T(8,128)S(1)}, u32[]{:S(2)}, u32[]{:S(2)}) %collective-permute-start.1) | collective-permute-done | bytes 1572896 | tf_op jit(solution)/shard_map/ppermute | solution.py:189
  40.1 1.4 add.13
  41.5 26.4 %all_to_all.45.refs_0_ = f32[8,128,128]{2,1,0:T(8,128)S(1)} all-to-all(f32[8,128,128]{2,1,0:T(8,128)S(1)} %add.12.after), channel_id=1, replica_groups=mesh['z'=8,'core'=2,'x'=4,'y'=4] {'z'}, dimensions={0} | all-to-all | bytes 1048576 | tf_op jit(solution)/shard_map/all_to_all | solution.py:186
  68.0 22.7 %all_to_all.46.refs_0_ = f32[16,128,128]{2,1,0:T(8,128)S(1)} all-to-all(f32[16,128,128]{2,1,0:T(8,128)S(1)} %get-tuple-element.19), channel_id=1, replica_groups=mesh['z'=8,'core'=2,'x'=4,'y'=4] {'x','y'}, dimensions={0} | all-to-all | bytes 2097152 | tf_op jit(solution)/shard_map/all_to_all | solution.py:164
  90.8 3.6 %solve.4 = (f32[128,128]{1,0:T(8,128)S(1)}, f32[16,128,128]{2,1,0:T(8,128)}) custom-call(f32[16,128,128]{2,1,0:T(8,128)S(1)} %all_to_all.46.refs_0_, f32[4,128,2048]{2,1,0:T(8,128)} %refs_1_.7, f32[6,2048,128]{2,1,0:T(8,128)} %all-gather.2.cloned.1.call-done.refs_2_.refs_3_.refs_4_), custom_call_target="tpu_custom_call" | custom-call | tf_op jit(solution)/shard_map/solve/pallas_call | solution.py:149
  94.4 4.9 %all-to-all-start.3 = ((f32[16,128,128]{2,1,0:T(8,128)}), f32[16,128,128]{2,1,0:T(8,128)S(1)}, u32[]{:S(2)}, u32[]{:S(2)}) async-start(f32[16,128,128]{2,1,0:T(8,128)} %get-tuple-element.21), calls=%async_computation.4 | async-start | bytes 2097152 | tf_op jit(solution)/shard_map/all_to_all | solution.py:164
  99.3 14.5 %all-to-all-done.3.refs_0_ = f32[16,128,128]{2,1,0:T(8,128)S(1)} async-done(((f32[16,128,128]{2,1,0:T(8,128)}), f32[16,128,128]{2,1,0:T(8,128)S(1)}, u32[]{:S(2)}, u32[]{:S(2)}) %all-to-all-start.3) | async-done | bytes 1048608 | tf_op jit(solution)/shard_map/all_to_all | solution.py:164
  113.9 0.9 copy-done
  114.9 19.1 %all_to_all.47.refs_0_ = f32[16,128,128]{2,1,0:T(8,128)S(1)} all-to-all(f32[16,128,128]{2,1,0:T(8,128)S(1)} %subtract.3), channel_id=1, replica_groups=mesh['z'=8,'core'=2,'x'=4,'y'=4] {'x','y'}, dimensions={0} | all-to-all | bytes 2097152 | tf_op jit(solution)/shard_map/all_to_all | solution.py:164
  134.0 3.0 %solve.5 = (f32[128,128]{1,0:T(8,128)S(1)}, f32[16,128,128]{2,1,0:T(8,128)S(1)}) custom-call(f32[16,128,128]{2,1,0:T(8,128)S(1)} %all_to_all.47.refs_0_, f32[4,128,2048]{2,1,0:T(8,128)} %refs_1_.7, f32[6,2048,128]{2,1,0:T(8,128)} %all-gather.2.cloned.1.call-done.refs_2_.refs_3_.refs_4_, f32[6,2048,128]{2,1,0:T(8,128)} %all-gather.2.cloned.1.call-done.refs_2_.refs_3_.refs_4_, ...), custom_call_target="tpu_custom_call" | custom-call | tf_op jit(solution)/shard_map/solve/pallas_call | solution.py:149
  137.0 18.0 %all_to_all.48.refs_0_ = f32[16,128,128]{2,1,0:T(8,128)S(1)} all-to-all(f32[16,128,128]{2,1,0:T(8,128)S(1)} %get-tuple-element.23), channel_id=1, replica_groups=mesh['z'=8,'core'=2,'x'=4,'y'=4] {'x','y'}, dimensions={0} | all-to-all | bytes 2097152 | tf_op jit(solution)/shard_map/all_to_all | solution.py:164
  155.1 16.6 %all_to_all.49.refs_0_ = f32[16,128,128]{2,1,0:T(8,128)S(1)} all-to-all(f32[16,128,128]{2,1,0:T(8,128)S(1)} %subtract.4), channel_id=1, replica_groups=mesh['z'=8,'core'=2,'x'=4,'y'=4] {'x','y'}, dimensions={0} | all-to-all | bytes 2097152 | tf_op jit(solution)/shard_map/all_to_all | solution.py:164
  171.7 3.6 %solve.6 = (f32[128,128]{1,0:T(8,128)S(1)}, f32[16,128,128]{2,1,0:T(8,128)S(1)}) custom-call(f32[16,128,128]{2,1,0:T(8,128)S(1)} %all_to_all.49.refs_0_, f32[4,128,2048]{2,1,0:T(8,128)} %refs_1_.7, f32[6,2048,128]{2,1,0:T(8,128)} %all-gather.2.cloned.1.call-done.refs_2_.refs_3_.refs_4_, f32[6,2048,128]{2,1,0:T(8,128)} %all-gather.2.cloned.1.call-done.refs_2_.refs_3_.refs_4_, ...), custom_call_target="tpu_custom_call" | custom-call | tf_op jit(solution)/shard_map/solve/pallas_call | solution.py:149
  175.3 16.2 %all_to_all.50.refs_0_ = f32[16,128,128]{2,1,0:T(8,128)S(1)} all-to-all(f32[16,128,128]{2,1,0:T(8,128)S(1)} %get-tuple-element.25), channel_id=1, replica_groups=mesh['z'=8,'core'=2,'x'=4,'y'=4] {'x','y'}, dimensions={0} | all-to-all | bytes 2097152 | tf_op jit(solution)/shard_map/all_to_all | solution.py:164
  191.5 1.1 subtract.5
  192.6 4.9 %all-to-all-start.8 = ((f32[16,128,128]{2,1,0:T(8,128)}), f32[16,128,128]{2,1,0:T(8,128)S(1)}, u32[]{:S(2)}, u32[]{:S(2)}) async-start(f32[16,128,128]{2,1,0:T(8,128)} %subtract.5), calls=%async_computation.9 | async-start | bytes 2097152 | tf_op jit(solution)/shard_map/all_to_all | solution.py:164
  198.2 10.9 %all-to-all-done.8.refs_0_ = f32[16,128,128]{2,1,0:T(8,128)S(1)} async-done(((f32[16,128,128]{2,1,0:T(8,128)}), f32[16,128,128]{2,1,0:T(8,128)S(1)}, u32[]{:S(2)}, u32[]{:S(2)}) %all-to-all-start.8) | async-done | bytes 1048608 | tf_op jit(solution)/shard_map/all_to_all | solution.py:164
  209.1 1.7 solve.7
  (30 shorter events, 5.5 us)
Async XLA Ops:
  8.0 12.4 %copy-start.2 = (f32[512,4,128]{2,1,0:T(4,128)S(1)}, f32[512,4,128]{2,1,0:T(4,128)}, u32[]{:S(2)}) copy-start(f32[512,4,128]{2,1,0:T(4,128)} %param.7) | copy-start | bytes 3145732
  8.0 82.8 %all-gather.2.cloned.1.call-start = ((), (), s32[]{:S(2)}) async-start(), calls=%async_computation.11 | async-start | bytes 6684672 | tf_op jit(solution)/shard_map/all_gather | solution.py:173
  10.0 16.2 %all-to-all-start = ((s32[16,2,128]{2,1,0:T(2,128)}), s32[16,2,128]{2,1,0:T(2,128)S(1)}, u32[]{:S(2)}, u32[]{:S(2)}) async-start(s32[16,2,128]{2,1,0:T(2,128)} %broadcast_in_dim.4), calls=%async_computation | async-start | bytes 32768 | tf_op jit(solution)/shard_map/all_to_all | solution.py:178
  18.6 80.7 %reduce-scatter.2.cloned.1.call-start = ((), (), s32[]{:S(2)}) async-start(), calls=%async_computation.10 | async-start | bytes 1769472 | tf_op jit(solution)/shard_map/reduce_scatter | solution.py:190
  29.6 2.0 collective-permute-start
  36.6 3.5 %collective-permute-start.1 = (f32[8,384,128]{2,1,0:T(8,128)S(1)}, f32[8,384,128]{2,1,0:T(8,128)S(1)}, u32[]{:S(2)}, u32[]{:S(2)}) collective-permute-start(f32[8,384,128]{2,1,0:T(8,128)S(1)} %get-tuple-element.18), channel_id=1, source_target_pairs={{0,16},{16,0},{1,17},{17,1},{2,18},{18,2},{3,19},{19,3},{4,20},{20... | collective-permute-start | bytes 4718600 | tf_op jit(solution)/shard_map/ppermute | solution.py:189
  94.4 19.5 %all-to-all-start.3 = ((f32[16,128,128]{2,1,0:T(8,128)}), f32[16,128,128]{2,1,0:T(8,128)S(1)}, u32[]{:S(2)}, u32[]{:S(2)}) async-start(f32[16,128,128]{2,1,0:T(8,128)} %get-tuple-element.21), calls=%async_computation.4 | async-start | bytes 2097152 | tf_op jit(solution)/shard_map/all_to_all | solution.py:164
  113.9 0.9 copy-start
  137.0 18.0 %copy-start.1 = (f32[384,128]{1,0:T(8,128)S(1)}, f32[384,128]{1,0:T(8,128)}, u32[]{:S(2)}) copy-start(f32[384,128]{1,0:T(8,128)} %reduce-scatter.2.cloned.1.call-done) | copy-start | bytes 589828
  192.6 16.5 %all-to-all-start.8 = ((f32[16,128,128]{2,1,0:T(8,128)}), f32[16,128,128]{2,1,0:T(8,128)S(1)}, u32[]{:S(2)}, u32[]{:S(2)}) async-start(f32[16,128,128]{2,1,0:T(8,128)} %subtract.5), calls=%async_computation.9 | async-start | bytes 2097152 | tf_op jit(solution)/shard_map/all_to_all | solution.py:164
Sparse Core Ops, SparseCore 0:
  10.7 64.8 all-gather.1
Sparse Core Ops, SparseCore 1:
  41.6 50.1 reduce-scatter.1

commit v3 on v2

--- a/solution.py
+++ b/solution.py
@@ -68,66 +68,79 @@
     )(here, index, rows, after)
 
 
-def remain_kernel(minus, *refs):
+def remain_kernel(block, *refs):
     terms = refs[0]
     total = terms[0]
     for part in range(1, terms.shape[0]):
         total += terms[part]
-    if minus:
-        total = refs[1][0] - total
+    if block is None:
+        refs[1][...] = total
     else:
-        refs[1][...] = total
+        total = refs[1][block] - total
     for owner in range(GROUP):
         refs[2][owner] = total
 
 
-def spread(terms, minuend=None, block=0):
+def spread(terms, minuend=None, block=None):
     copies = jax.ShapeDtypeStruct((GROUP, SIDE, SIDE), F32)
-    copies_spec = pl.BlockSpec(copies.shape, lambda i: (0, 0, 0))
-    terms_spec = pl.BlockSpec(terms.shape, lambda i: (0, 0, 0))
     if minuend is None:
         return pl.pallas_call(
-            functools.partial(remain_kernel, False),
+            functools.partial(remain_kernel, None),
             out_shape=(jax.ShapeDtypeStruct((SIDE, SIDE), F32), copies),
-            grid=(1,),
-            in_specs=[terms_spec],
-            out_specs=(pl.BlockSpec((SIDE, SIDE), lambda i: (0, 0)), copies_spec),
+            in_specs=[VMEM],
+            out_specs=(VMEM, VMEM),
             compiler_params=PARAMS,
             name="sum_first",
         )(terms)
     return pl.pallas_call(
-        functools.partial(remain_kernel, True),
+        functools.partial(remain_kernel, block),
         out_shape=copies,
-        grid=(1,),
-        in_specs=[terms_spec, pl.BlockSpec((1, SIDE, SIDE), lambda i: (block, 0, 0))],
-        out_specs=copies_spec,
+        in_specs=[VMEM, VMEM],
+        out_specs=VMEM,
         compiler_params=PARAMS,
         name="subtract",
     )(terms, minuend)
 
 
-def solve_kernel(target, last, *refs):
-    whole, inverse = refs[0], refs[1]
-    factors = refs[2 : 2 + (0 if last else target + 1)]
-    before = refs[2 + len(factors) : 2 + len(factors) + (0 if last else target)]
-    solved = refs[2 + len(factors) + len(before)]
+def solve_kernel(target, last, places, *refs):
+    whole, inverse_ref = refs[0], refs[1]
+    count = 0 if last else target + 1
+    factors = refs[2 : 2 + count]
+    before = refs[2 + count : 2 + count + target]
+    solved = refs[2 + count + target]
+    held_inverse, held, sems = refs[-3:]
+    fetch = pltpu.make_async_copy(inverse_ref.at[target], held_inverse, sems.at[0])
+    fetch.start()
+    copies = []
+    for source in range(count):
+        copy = pltpu.make_async_copy(factors[source].at[places[source]], held.at[source], sems.at[source + 1])
+        copy.start()
+        copies.append(copy)
+
     high, low = halves(whole[...].reshape(GROUP * SIDE, SIDE))
-    left, left_low = halves(inverse[0])
-    wide = jnp.dot(left, jnp.concatenate([high, low], axis=1), preferred_element_type=F32)
+    right = jnp.concatenate([high, low], axis=1)
+    fetch.wait()
+    left, left_low = halves(held_inverse[...])
+    wide = jnp.dot(left, right, preferred_element_type=F32)
     own = wide[:, :SIDE] + wide[:, SIDE:] + jnp.dot(left_low, high, preferred_element_type=F32)
+    if last:
+        for source in range(target):
+            solved[source] = before[source][...]
+        solved[target] = own
+        return
     solved[...] = own
-    if last:
-        return
-    terms = refs[-1]
+    terms = refs[-4]
     rights = [one[...] for one in before] + [own]
-    for first in range(0, target + 1, 2):
-        some = range(first, min(first + 2, target + 1))
+    for first in range(0, count, 2):
+        some = range(first, min(first + 2, count))
         right = jnp.concatenate([rights[source] for source in some], axis=0)
         high, low = halves(right)
         right = jnp.concatenate([high, low], axis=1)
+        for source in some:
+            copies[source].wait()
         for part in range(4):
             rows = pl.ds(part * 4 * SIDE, 4 * SIDE)
-            left = jnp.concatenate([factors[source][0, rows] for source in some], axis=1)
+            left = jnp.concatenate([held[source, rows] for source in some], axis=1)
             left, left_low = halves(left)
             wide = jnp.dot(left, right, preferred_element_type=F32)
             term = wide[:, :SIDE] + wide[:, SIDE:] + jnp.dot(left_low, high, preferred_element_type=F32)
@@ -138,26 +151,44 @@
                 terms[pl.ds(part * 4, 4)] += term
 
 
-def solve(target, whole, inverses, factor, before):
+def solve(target, whole, inverses, factors, before):
     last = target + 1 == inverses.shape[0]
-    count = 0 if last else target + 1
-    first = target * (target + 1) // 2
+    count = len(factors)
     one = jax.ShapeDtypeStruct((SIDE, SIDE), F32)
-    one_spec = pl.BlockSpec(one.shape, lambda i: (0, 0))
-    group = jax.ShapeDtypeStruct((GROUP, SIDE, SIDE), F32)
-    group_spec = pl.BlockSpec(group.shape, lambda i: (0, 0, 0))
+    out_shape = (one, jax.ShapeDtypeStruct((GROUP, SIDE, SIDE), F32))
+    if last:
+        out_shape = (jax.ShapeDtypeStruct((target + 1, SIDE, SIDE), F32),)
+    hbm = pl.BlockSpec(memory_space=pltpu.HBM)
     out = pl.pallas_call(
-        functools.partial(solve_kernel, target, last),
-        out_shape=(one,) if last else (one, group),
-        grid=(1,),
-        in_specs=[group_spec, pl.BlockSpec((1, SIDE, GROUP * SIDE), lambda i: (target, 0, 0))]
-        + [pl.BlockSpec((1, GROUP * SIDE, SIDE), lambda i, at=first + k: (at, 0, 0)) for k in range(count)]
-        + [one_spec] * (0 if last else target),
-        out_specs=(one_spec,) if last else (one_spec, group_spec),
+        functools.partial(solve_kernel, target, last, tuple(block for _, block in factors)),
+        out_shape=out_shape,
+        in_specs=[VMEM, hbm] + [hbm] * count + [VMEM] * target,
+        out_specs=(VMEM,) * len(out_shape),
+        scratch_shapes=[
+            pltpu.VMEM((SIDE, GROUP * SIDE), F32),
+            pltpu.VMEM((max(count, 1), GROUP * SIDE, SIDE), F32),
+            pltpu.SemaphoreType.DMA((count + 1,)),
+        ],
         compiler_params=PARAMS,
         name="solve",
-    )(whole, inverses, *[factor] * count, *([] if last else before))
+    )(whole, inverses, *[array for array, _ in factors], *before)
     return (out[0], None) if last else out
+
+
+def hold_kernel(blocks, after, out):
+    out[...] = blocks[1:]
+
+
+def hold(blocks, after):
+    shape = jax.ShapeDtypeStruct((blocks.shape[0] - 1,) + blocks.shape[1:], F32)
+    return pl.pallas_call(
+        hold_kernel,
+        out_shape=shape,
+        in_specs=[VMEM, pl.BlockSpec(memory_space=pl.ANY)],
+        out_specs=VMEM,
+        compiler_params=PARAMS,
+        name="hold",
+    )(blocks, after)
 
 
 def to_group(parts):
@@ -170,8 +201,10 @@
     here = here.astype(jnp.int32)
     swap = [(0, 1), (1, 0)]
 
-    factor = lax.all_gather(factor_blocks, ROW, axis=1, tiled=True)
-    factor = pltpu.with_memory_space_constraint(factor, pltpu.HBM)
+    def gathered(some):
+        return pltpu.with_memory_space_constraint(lax.all_gather(some, ROW, axis=1, tiled=True), pltpu.HBM)
+
+    start = gathered(factor_blocks[:1])
     inverses = pltpu.with_memory_space_constraint(inverses, pltpu.HBM)
 
     pair = jnp.stack([sire_index, dam_index])
@@ -184,6 +217,8 @@
     keep, give = select(1, here, index, rows_of(0, 1), here)
     first_terms = keep + lax.ppermute(give, "core", swap)
     relation0, copies = spread(lax.all_to_all(first_terms, "z", 0, 0))
+
+    rest = gathered(hold(factor_blocks, relation0))
 
     keep, give = select(blocks - 1, here, index, rows_of(1, blocks - 1), first_terms)
     terms = keep + lax.ppermute(give, "core", swap)
@@ -194,10 +229,16 @@
     for target in range(blocks):
         if target > 0:
             copies = spread(to_group(terms), later, target - 1)
-        own, terms = solve(target, to_group(copies), inverses, factor, solved)
+        first = target * (target + 1) // 2
+        factors = [(rest, first + source - 1) for source in range(target + 1)]
+        if target == 0:
+            factors = [(start, 0)]
+        if target + 1 == blocks:
+            factors = []
+        own, terms = solve(target, to_group(copies), inverses, factors, solved)
         solved.append(own)
     relationship = jnp.concatenate([relation0[None], later])
-    return relationship, jnp.stack(solved)
+    return relationship, solved[-1]
 
 
 def solution(mesh):

time: 220 us -> 214 us (0.973)
  blocking collectives: 119 us -> 110 us
  starting transfers between devices: 18.9 us -> 21.6 us
    all_to_all x5, blocking collectives: 92.6 us -> 85.8 us  [to_group(): return lax.all_to_all(parts, COL, 0, 0)]
    all_to_all x2, starting transfers between devices: 9.83 us -> 12.5 us  [to_group(): return lax.all_to_all(parts, COL, 0, 0)]
    all_to_all x1, blocking collectives: 26.4 us -> 24 us  [per_device(): relation0, copies = spread(lax.all_to_all(first_terms, 'z', 0, 0))]
    pallas_call x8 -> x9, Pallas kernels: 13.3 us -> 13.8 us  [the longest x4 10.4 us: solve(): pl.pallas_call(functools.partial(solve_kernel, target, last, tuple((block...]
  transfers between devices with their start and end apart: 7 -> 8, of which waited for: 5 -> 5; matrix products, arithmetic and copies ran while one was open for 3% -> 3% of each run, Pallas kernels for 5% -> 6%
where the time goes in v3:
time: 214 us; the launch traced here: 213 us
  blocking collectives  110 us (51%)
  waiting for transfers between devices  35.8 us (17%)
  Pallas kernels  22 us (10%)
  starting transfers between devices  21.6 us (10%)
  between operations  15.7 us (7%)
  local copies, waits for them, and re-layouts  5.13 us (2%)
  other arithmetic  3.34 us (2%)
    all_to_all x5, blocking collectives, to_group(): return lax.all_to_all(parts, COL, 0, 0)  85.8 us
    all_to_all x2, waiting for transfers between devices, to_group(): return lax.all_to_all(parts, COL, 0, 0)  27.2 us
    all_to_all x1, blocking collectives, per_device(): relation0, copies = spread(lax.all_to_all(first_terms, 'z', 0, 0))  24 us
    all_to_all x2, starting transfers between devices, to_group(): return lax.all_to_all(parts, COL, 0, 0)  12.5 us
    pallas_call x4, Pallas kernels, solve(): pl.pallas_call(functools.partial(solve_kernel, target, last, tuple((block...  10.4 us
    all_to_all x1, starting transfers between devices, per_device(): lax.all_to_all(jnp.broadcast_to(pair[None], (GROUP, 2, SIDE)), ROW, 0, 0)  8.57 us
    pallas_call x2, Pallas kernels, select(): pl.pallas_call(functools.partial(select_kernel, count), out_shape=(shape,...  8.27 us
  transfers between devices with their start and end apart: 8, of which 5 were waited for; matrix products, arithmetic and copies ran while one was open for 3% of the time, Pallas kernels for 6%

profile of v3, /device:TPU:8, one launch (start us, length us, event | category | flops | bytes accessed | tf_op | source)
XLA Modules:
  0.0 213.4 jit_solution(5128250307099804230)
XLA Ops:
  9.4 8.6 %all-to-all-start = ((s32[16,2,128]{2,1,0:T(2,128)}), s32[16,2,128]{2,1,0:T(2,128)S(1)}, u32[]{:S(2)}, u32[]{:S(2)}) async-start(s32[16,2,128]{2,1,0:T(2,128)} %broadcast_in_dim.4), calls=%async_computation | async-start | bytes 32768 | tf_op jit(solution)/shard_map/all_to_all | solution.py:211
  18.0 1.5 slice.11
  19.6 1.4 slice.9
  21.9 3.7 %all-to-all-done.index = s32[16,2,128]{2,1,0:T(2,128)S(1)} async-done(((s32[16,2,128]{2,1,0:T(2,128)}), s32[16,2,128]{2,1,0:T(2,128)S(1)}, u32[]{:S(2)}, u32[]{:S(2)}) %all-to-all-start) | async-done | bytes 16416 | tf_op jit(solution)/shard_map/all_to_all | solution.py:211
  25.6 3.3 %select.2 = (f32[8,128,128]{2,1,0:T(8,128)S(1)}, f32[8,128,128]{2,1,0:T(8,128)S(1)}) custom-call(s32[4]{0:T(128)S(1)} %pad_add_fusion.1.here.after, s32[16,2,128]{2,1,0:T(2,128)S(1)} %all-to-all-done.index, bf16[384,512]{1,0:T(8,128)(2,1)S(1)} %pad_maximum_fusion.1.rows, s32[4]{0:T(128)S(1)} %pad_add_fusion.1.here.after), custom_call_target="tpu_custom_call" | custom-call | flops 805306368 | bytes 1048576 | tf_op jit(solution)/shard_map/select/pallas_call | solution.py:58
  29.4 1.5 collective-permute-done
  31.0 4.9 %select.3 = (f32[8,384,128]{2,1,0:T(8,128)S(1)}, f32[8,384,128]{2,1,0:T(8,128)S(1)}) custom-call(s32[4]{0:T(128)S(1)} %pad_add_fusion.1.here.after, s32[16,2,128]{2,1,0:T(2,128)S(1)} %all-to-all-done.index, bf16[1152,512]{1,0:T(8,128)(2,1)S(1)} %pad_maximum_fusion.rows, f32[8,128,128]{2,1,0:T(8,128)S(1)} %add.12.after), custom_call_target="tpu_custom_call" | custom-call | flops 2415919104 | bytes 3145728 | tf_op jit(solution)/shard_map/select/pallas_call | solution.py:58
  36.2 3.3 %collective-permute-done.1 = f32[8,384,128]{2,1,0:T(8,128)S(1)} collective-permute-done((f32[8,384,128]{2,1,0:T(8,128)S(1)}, f32[8,384,128]{2,1,0:T(8,128)S(1)}, u32[]{:S(2)}, u32[]{:S(2)}) %collective-permute-start.1) | collective-permute-done | bytes 1572896 | tf_op jit(solution)/shard_map/ppermute | solution.py:224
  39.4 1.4 add.13
  40.9 24.0 %all_to_all.45.refs_0_ = f32[8,128,128]{2,1,0:T(8,128)S(1)} all-to-all(f32[8,128,128]{2,1,0:T(8,128)S(1)} %add.12.after), channel_id=1, replica_groups=mesh['z'=8,'core'=2,'x'=4,'y'=4] {'z'}, dimensions={0} | all-to-all | bytes 1048576 | tf_op jit(solution)/shard_map/all_to_all | solution.py:219
  64.9 1.2 sum_first.1
  66.8 7.6 %all-to-all-start.2 = ((f32[16,128,128]{2,1,0:T(8,128)}), f32[16,128,128]{2,1,0:T(8,128)S(1)}, u32[]{:S(2)}, u32[]{:S(2)}) async-start(f32[16,128,128]{2,1,0:T(8,128)} %get-tuple-element.19), calls=%async_computation.3 | async-start | bytes 2097152 | tf_op jit(solution)/shard_map/all_to_all | solution.py:195
  74.5 16.3 %all-to-all-done.2.refs_0_ = f32[16,128,128]{2,1,0:T(8,128)S(1)} async-done(((f32[16,128,128]{2,1,0:T(8,128)}), f32[16,128,128]{2,1,0:T(8,128)S(1)}, u32[]{:S(2)}, u32[]{:S(2)}) %all-to-all-start.2) | async-done | bytes 1048608 | tf_op jit(solution)/shard_map/all_to_all | solution.py:195
  90.8 2.3 %solve.4 = (f32[128,128]{1,0:T(8,128)S(1)}, f32[16,128,128]{2,1,0:T(8,128)S(1)}) custom-call(f32[16,128,128]{2,1,0:T(8,128)S(1)} %all-to-all-done.2.refs_0_, f32[4,128,2048]{2,1,0:T(8,128)} %refs_1_.7, f32[1,2048,128]{2,1,0:T(8,128)} %all-gather.3.cloned.1.call-done.refs_2_), custom_call_target="tpu_custom_call" | custom-call | tf_op jit(solution)/shard_map/solve/pallas_call | solution.py:162
  93.1 18.7 %all_to_all.46.refs_0_ = f32[16,128,128]{2,1,0:T(8,128)S(1)} all-to-all(f32[16,128,128]{2,1,0:T(8,128)S(1)} %get-tuple-element.20), channel_id=1, replica_groups=mesh['z'=8,'core'=2,'x'=4,'y'=4] {'x','y'}, dimensions={0} | all-to-all | bytes 2097152 | tf_op jit(solution)/shard_map/all_to_all | solution.py:195
  112.9 18.0 %all_to_all.47.refs_0_ = f32[16,128,128]{2,1,0:T(8,128)S(1)} all-to-all(f32[16,128,128]{2,1,0:T(8,128)S(1)} %subtract.3), channel_id=1, replica_groups=mesh['z'=8,'core'=2,'x'=4,'y'=4] {'x','y'}, dimensions={0} | all-to-all | bytes 2097152 | tf_op jit(solution)/shard_map/all_to_all | solution.py:195
  130.8 2.6 %solve.5 = (f32[128,128]{1,0:T(8,128)S(1)}, f32[16,128,128]{2,1,0:T(8,128)S(1)}) custom-call(f32[16,128,128]{2,1,0:T(8,128)S(1)} %all_to_all.47.refs_0_, f32[4,128,2048]{2,1,0:T(8,128)} %refs_1_.7, f32[5,2048,128]{2,1,0:T(8,128)} %all-gather.5.cloned.1.call-done.refs_2_.refs_3_.refs_4_, f32[5,2048,128]{2,1,0:T(8,128)} %all-gather.5.cloned.1.call-done.refs_2_.refs_3_.refs_4_, ...), custom_call_target="tpu_custom_call" | custom-call | tf_op jit(solution)/shard_map/solve/pallas_call | solution.py:162
  133.4 16.8 %all_to_all.48.refs_0_ = f32[16,128,128]{2,1,0:T(8,128)S(1)} all-to-all(f32[16,128,128]{2,1,0:T(8,128)S(1)} %get-tuple-element.22), channel_id=1, replica_groups=mesh['z'=8,'core'=2,'x'=4,'y'=4] {'x','y'}, dimensions={0} | all-to-all | bytes 2097152 | tf_op jit(solution)/shard_map/all_to_all | solution.py:195
  150.4 16.2 %all_to_all.49.refs_0_ = f32[16,128,128]{2,1,0:T(8,128)S(1)} all-to-all(f32[16,128,128]{2,1,0:T(8,128)S(1)} %subtract.4), channel_id=1, replica_groups=mesh['z'=8,'core'=2,'x'=4,'y'=4] {'x','y'}, dimensions={0} | all-to-all | bytes 2097152 | tf_op jit(solution)/shard_map/all_to_all | solution.py:195
  166.5 3.2 %solve.6 = (f32[128,128]{1,0:T(8,128)S(1)}, f32[16,128,128]{2,1,0:T(8,128)S(1)}) custom-call(f32[16,128,128]{2,1,0:T(8,128)S(1)} %all_to_all.49.refs_0_, f32[4,128,2048]{2,1,0:T(8,128)} %refs_1_.7, f32[5,2048,128]{2,1,0:T(8,128)} %all-gather.5.cloned.1.call-done.refs_2_.refs_3_.refs_4_, f32[5,2048,128]{2,1,0:T(8,128)} %all-gather.5.cloned.1.call-done.refs_2_.refs_3_.refs_4_, ...), custom_call_target="tpu_custom_call" | custom-call | tf_op jit(solution)/shard_map/solve/pallas_call | solution.py:162
  169.7 16.2 %all_to_all.50.refs_0_ = f32[16,128,128]{2,1,0:T(8,128)S(1)} all-to-all(f32[16,128,128]{2,1,0:T(8,128)S(1)} %get-tuple-element.24), channel_id=1, replica_groups=mesh['z'=8,'core'=2,'x'=4,'y'=4] {'x','y'}, dimensions={0} | all-to-all | bytes 2097152 | tf_op jit(solution)/shard_map/all_to_all | solution.py:195
  187.0 4.9 %all-to-all-start.8 = ((f32[16,128,128]{2,1,0:T(8,128)}), f32[16,128,128]{2,1,0:T(8,128)S(1)}, u32[]{:S(2)}, u32[]{:S(2)}) async-start(f32[16,128,128]{2,1,0:T(8,128)} %subtract.5), calls=%async_computation.9 | async-start | bytes 2097152 | tf_op jit(solution)/shard_map/all_to_all | solution.py:195
  192.6 10.9 %all-to-all-done.8.refs_0_ = f32[16,128,128]{2,1,0:T(8,128)S(1)} async-done(((f32[16,128,128]{2,1,0:T(8,128)}), f32[16,128,128]{2,1,0:T(8,128)S(1)}, u32[]{:S(2)}, u32[]{:S(2)}) %all-to-all-start.8) | async-done | bytes 1048608 | tf_op jit(solution)/shard_map/all_to_all | solution.py:195
  203.5 2.4 %solve.7 = f32[4,128,128]{2,1,0:T(8,128)} custom-call(f32[16,128,128]{2,1,0:T(8,128)S(1)} %all-to-all-done.8.refs_0_, f32[4,128,2048]{2,1,0:T(8,128)} %refs_1_.7, f32[128,128]{1,0:T(8,128)S(1)} %get-tuple-element.21.refs_4_.refs_5_.refs_2_, f32[128,128]{1,0:T(8,128)S(1)} %get-tuple-element.23.refs_6_.refs_3_, f32[128,128]{1,0:T(8,128)S(1)} %get-tuple-element.25.refs_4_), custom_call_target="tpu_custom_call" | custom-call | tf_op jit(solution)/shard_map/solve/pallas_call | solution.py:162
  (36 shorter events, 7.0 us)
Async XLA Ops:
  8.0 13.3 %copy-start.3 = (f32[512,4,128]{2,1,0:T(4,128)S(1)}, f32[512,4,128]{2,1,0:T(4,128)}, u32[]{:S(2)}) copy-start(f32[512,4,128]{2,1,0:T(4,128)} %param.7) | copy-start | bytes 3145732
  9.4 16.2 %all-to-all-start = ((s32[16,2,128]{2,1,0:T(2,128)}), s32[16,2,128]{2,1,0:T(2,128)S(1)}, u32[]{:S(2)}, u32[]{:S(2)}) async-start(s32[16,2,128]{2,1,0:T(2,128)} %broadcast_in_dim.4), calls=%async_computation | async-start | bytes 32768 | tf_op jit(solution)/shard_map/all_to_all | solution.py:211
  18.0 56.5 %all-gather.3.cloned.1.call-start = ((), (), s32[]{:S(2)}) async-start(), calls=%async_computation.11 | async-start | bytes 1114112 | tf_op jit(solution)/shard_map/all_gather | solution.py:205
  19.5 92.3 %reduce-scatter.2.cloned.1.call-start = ((), (), s32[]{:S(2)}) async-start(), calls=%async_computation.10 | async-start | bytes 1769472 | tf_op jit(solution)/shard_map/reduce_scatter | solution.py:225
  28.9 2.0 collective-permute-start
  36.0 3.5 %collective-permute-start.1 = (f32[8,384,128]{2,1,0:T(8,128)S(1)}, f32[8,384,128]{2,1,0:T(8,128)S(1)}, u32[]{:S(2)}, u32[]{:S(2)}) collective-permute-start(f32[8,384,128]{2,1,0:T(8,128)S(1)} %get-tuple-element.18), channel_id=1, source_target_pairs={{0,16},{16,0},{1,17},{17,1},{2,18},{18,2},{3,19},{19,3},{4,20},{20... | collective-permute-start | bytes 4718600 | tf_op jit(solution)/shard_map/ppermute | solution.py:224
  40.8 25.2 %copy-start.2 = (f32[6,128,128]{2,1,0:T(8,128)S(1)}, f32[6,128,128]{2,1,0:T(8,128)}, u32[]{:S(2)}) copy-start(f32[6,128,128]{2,1,0:T(8,128)} %blocks.1) | copy-start | bytes 1179652
  40.8 90.0 %all-gather.5.cloned.1.call-start = ((), (), s32[]{:S(2)}) async-start(), calls=%async_computation.12 | async-start | bytes 5570560 | tf_op jit(solution)/shard_map/all_gather | solution.py:205
  66.8 23.9 %all-to-all-start.2 = ((f32[16,128,128]{2,1,0:T(8,128)}), f32[16,128,128]{2,1,0:T(8,128)S(1)}, u32[]{:S(2)}, u32[]{:S(2)}) async-start(f32[16,128,128]{2,1,0:T(8,128)} %get-tuple-element.19), calls=%async_computation.3 | async-start | bytes 2097152 | tf_op jit(solution)/shard_map/all_to_all | solution.py:195
  111.8 0.9 copy-start
  133.4 16.8 %copy-start.1 = (f32[384,128]{1,0:T(8,128)S(1)}, f32[384,128]{1,0:T(8,128)}, u32[]{:S(2)}) copy-start(f32[384,128]{1,0:T(8,128)} %reduce-scatter.2.cloned.1.call-done) | copy-start | bytes 589828
  187.0 16.5 %all-to-all-start.8 = ((f32[16,128,128]{2,1,0:T(8,128)}), f32[16,128,128]{2,1,0:T(8,128)S(1)}, u32[]{:S(2)}, u32[]{:S(2)}) async-start(f32[16,128,128]{2,1,0:T(8,128)} %subtract.5), calls=%async_computation.9 | async-start | bytes 2097152 | tf_op jit(solution)/shard_map/all_to_all | solution.py:195
Sparse Core Ops, SparseCore 0:
  21.2 46.4 all-gather.2
  69.6 44.1 all-gather.4
Sparse Core Ops, SparseCore 1:
  40.9 43.3 reduce-scatter.1

commit v4 on v3

--- a/solution.py
+++ b/solution.py
@@ -191,6 +191,29 @@
     )(blocks, after)
 
 
+def add_kernel(one, other, after, first, rest):
+    first[...] = one[:, :SIDE] + other[:, :SIDE]
+    rest[...] = one[:, SIDE:] + other[:, SIDE:]
+
+
+def add(one, other, after):
+    rest = (one.shape[0], one.shape[1] - SIDE, SIDE)
+    return pl.pallas_call(
+        add_kernel,
+        out_shape=(jax.ShapeDtypeStruct((one.shape[0], SIDE, SIDE), F32), jax.ShapeDtypeStruct(rest, F32)),
+        in_specs=[VMEM, VMEM, pl.BlockSpec(memory_space=pl.ANY)],
+        out_specs=(VMEM, VMEM),
+        compiler_params=PARAMS,
+        name="add",
+    )(one, other, after)
+
+
+def pair_kernel(sire, dam, out):
+    for owner in range(GROUP):
+        out[owner, 0:1] = sire[...]
+        out[owner, 1:2] = dam[...]
+
+
 def to_group(parts):
     return lax.all_to_all(parts, COL, 0, 0)
 
@@ -207,8 +230,15 @@
     start = gathered(factor_blocks[:1])
     inverses = pltpu.with_memory_space_constraint(inverses, pltpu.HBM)
 
-    pair = jnp.stack([sire_index, dam_index])
-    index = lax.all_to_all(jnp.broadcast_to(pair[None], (GROUP, 2, SIDE)), ROW, 0, 0)
+    pair = pl.pallas_call(
+        pair_kernel,
+        out_shape=jax.ShapeDtypeStruct((GROUP, 2, SIDE), jnp.int32),
+        in_specs=[VMEM, VMEM],
+        out_specs=VMEM,
+        compiler_params=PARAMS,
+        name="pair",
+    )(sire_index[None], dam_index[None])
+    index = lax.all_to_all(pair, ROW, 0, 0)
 
     def rows_of(first, count):
         rows = relatives[:, first : first + count, :].reshape(old_dev, count * SIDE).T
@@ -221,14 +251,15 @@
     rest = gathered(hold(factor_blocks, relation0))
 
     keep, give = select(blocks - 1, here, index, rows_of(1, blocks - 1), first_terms)
-    terms = keep + lax.ppermute(give, "core", swap)
-    later = lax.psum_scatter(terms.reshape(-1, SIDE), "z", scatter_dimension=0, tiled=True)
-    later = later.reshape(blocks - 1, SIDE, SIDE)
+    parts = add(keep, lax.ppermute(give, "core", swap), relation0)
+    parts = [lax.psum_scatter(part.reshape(-1, SIDE), "z", scatter_dimension=0, tiled=True) for part in parts]
+    later = [part.reshape(-1, SIDE, SIDE) for part in parts]
+    minuends = [(later[0], 0), (later[1], 0), (later[1], 1)]
 
     solved = []
     for target in range(blocks):
         if target > 0:
-            copies = spread(to_group(terms), later, target - 1)
+            copies = spread(to_group(terms), *minuends[target - 1])
         first = target * (target + 1) // 2
         factors = [(rest, first + source - 1) for source in range(target + 1)]
         if target == 0:
@@ -237,7 +268,7 @@
             factors = []
         own, terms = solve(target, to_group(copies), inverses, factors, solved)
         solved.append(own)
-    relationship = jnp.concatenate([relation0[None], later])
+    relationship = jnp.concatenate([relation0[None], *later])
     return relationship, solved[-1]
 
 

time: 214 us -> 221 us (1.033)
  blocking collectives: 110 us -> 79.3 us
  waiting for transfers between devices: 35.8 us -> 59.5 us
  starting transfers between devices: 21.6 us -> 31.4 us
  Pallas kernels: 22 us -> 26.1 us
    all_to_all x5 -> x3, blocking collectives: 85.8 us -> 55.7 us  [to_group(): return lax.all_to_all(parts, COL, 0, 0)]
    all_to_all x2 -> x4, waiting for transfers between devices: 27.2 us -> 40.7 us  [to_group(): return lax.all_to_all(parts, COL, 0, 0)]
    reduce_scatter x1 -> x2, waiting for transfers between devices: 0.01 us -> 13 us  [per_device(): lax.psum_scatter(part.reshape(-1, SIDE), 'z', scatter_dimension=0, tiled=...]
    all_to_all x2 -> x4, starting transfers between devices: 12.5 us -> 22.3 us  [to_group(): return lax.all_to_all(parts, COL, 0, 0)]
    ppermute x1, waiting for transfers between devices: 3.27 us -> 0.01 us  [per_device(): parts = add(keep, lax.ppermute(give, 'core', swap), relation0)]
  transfers between devices with their start and end apart: 8 -> 11, of which waited for: 5 -> 8; matrix products, arithmetic and copies ran while one was open for 3% -> 2% of each run, Pallas kernels for 6% -> 9%
where the time goes in v4:
time: 221 us; the launch traced here: 220 us
  blocking collectives  79.3 us (36%)
  waiting for transfers between devices  59.5 us (27%)
  starting transfers between devices  31.4 us (14%)
  Pallas kernels  26.1 us (12%)
  between operations  15.7 us (7%)
  local copies, waits for them, and re-layouts  6.64 us (3%)
    all_to_all x3, blocking collectives, to_group(): return lax.all_to_all(parts, COL, 0, 0)  55.7 us
    all_to_all x4, waiting for transfers between devices, to_group(): return lax.all_to_all(parts, COL, 0, 0)  40.7 us
    all_to_all x1, blocking collectives, per_device(): relation0, copies = spread(lax.all_to_all(first_terms, 'z', 0, 0))  23.6 us
    all_to_all x4, starting transfers between devices, to_group(): return lax.all_to_all(parts, COL, 0, 0)  22.3 us
    reduce_scatter x2, waiting for transfers between devices, per_device(): lax.psum_scatter(part.reshape(-1, SIDE), 'z', scatter_dimension=0, tiled=...  13 us
    pallas_call x4, Pallas kernels, solve(): pl.pallas_call(functools.partial(solve_kernel, target, last, tuple((block...  12.6 us
    all_to_all x1, starting transfers between devices, per_device(): index = lax.all_to_all(pair, ROW, 0, 0)  8.57 us
    pallas_call x2, Pallas kernels, select(): pl.pallas_call(functools.partial(select_kernel, count), out_shape=(shape,...  8.29 us
  transfers between devices with their start and end apart: 11, of which 8 were waited for; matrix products, arithmetic and copies ran while one was open for 2% of the time, Pallas kernels for 9%

profile of v4, /device:TPU:8, one launch (start us, length us, event | category | flops | bytes accessed | tf_op | source)
XLA Modules:
  0.0 219.9 jit_solution(5624915906205077823)
XLA Ops:
  9.9 8.6 %all-to-all-start = ((s32[16,2,128]{2,1,0:T(2,128)}), s32[16,2,128]{2,1,0:T(2,128)S(1)}, u32[]{:S(2)}, u32[]{:S(2)}) async-start(s32[16,2,128]{2,1,0:T(2,128)} %pair.1), calls=%async_computation | async-start | bytes 32768 | tf_op jit(solution)/shard_map/all_to_all | solution.py:241
  18.6 1.5 slice.11
  22.4 3.7 %all-to-all-done.index = s32[16,2,128]{2,1,0:T(2,128)S(1)} async-done(((s32[16,2,128]{2,1,0:T(2,128)}), s32[16,2,128]{2,1,0:T(2,128)S(1)}, u32[]{:S(2)}, u32[]{:S(2)}) %all-to-all-start) | async-done | bytes 16416 | tf_op jit(solution)/shard_map/all_to_all | solution.py:241
  26.1 3.3 %select.2 = (f32[8,128,128]{2,1,0:T(8,128)S(1)}, f32[8,128,128]{2,1,0:T(8,128)S(1)}) custom-call(s32[4]{0:T(128)S(1)} %pad_add_fusion.here.after, s32[16,2,128]{2,1,0:T(2,128)S(1)} %all-to-all-done.index, bf16[384,512]{1,0:T(8,128)(2,1)S(1)} %pad_maximum_fusion.1.rows, s32[4]{0:T(128)S(1)} %pad_add_fusion.here.after), custom_call_target="tpu_custom_call" | custom-call | flops 805306368 | bytes 1048576 | tf_op jit(solution)/shard_map/select/pallas_call | solution.py:58
  29.9 1.5 collective-permute-done
  31.5 5.0 %select.3 = (f32[8,384,128]{2,1,0:T(8,128)S(1)}, f32[8,384,128]{2,1,0:T(8,128)S(1)}) custom-call(s32[4]{0:T(128)S(1)} %pad_add_fusion.here.after, s32[16,2,128]{2,1,0:T(2,128)S(1)} %all-to-all-done.index, bf16[1152,512]{1,0:T(8,128)(2,1)S(1)} %pad_maximum_fusion.rows, f32[8,128,128]{2,1,0:T(8,128)S(1)} %add.12.after), custom_call_target="tpu_custom_call" | custom-call | flops 2415919104 | bytes 3145728 | tf_op jit(solution)/shard_map/select/pallas_call | solution.py:58
  36.7 23.6 %all_to_all.45.refs_0_ = f32[8,128,128]{2,1,0:T(8,128)S(1)} all-to-all(f32[8,128,128]{2,1,0:T(8,128)S(1)} %add.12.after), channel_id=1, replica_groups=mesh['z'=8,'core'=2,'x'=4,'y'=4] {'z'}, dimensions={0} | all-to-all | bytes 1048576 | tf_op jit(solution)/shard_map/all_to_all | solution.py:249
  63.7 7.4 %all-to-all-start.2 = ((f32[16,128,128]{2,1,0:T(8,128)}), f32[16,128,128]{2,1,0:T(8,128)S(1)}, u32[]{:S(2)}, u32[]{:S(2)}) async-start(f32[16,128,128]{2,1,0:T(8,128)} %get-tuple-element.23), calls=%async_computation.4 | async-start | bytes 2097152 | tf_op jit(solution)/shard_map/all_to_all | solution.py:218
  71.2 14.8 %all-to-all-done.2.refs_0_ = f32[16,128,128]{2,1,0:T(8,128)S(1)} async-done(((f32[16,128,128]{2,1,0:T(8,128)}), f32[16,128,128]{2,1,0:T(8,128)S(1)}, u32[]{:S(2)}, u32[]{:S(2)}) %all-to-all-start.2) | async-done | bytes 1048608 | tf_op jit(solution)/shard_map/all_to_all | solution.py:218
  86.0 3.4 %solve.4 = (f32[128,128]{1,0:T(8,128)S(1)}, f32[16,128,128]{2,1,0:T(8,128)}) custom-call(f32[16,128,128]{2,1,0:T(8,128)S(1)} %all-to-all-done.2.refs_0_, f32[4,128,2048]{2,1,0:T(8,128)} %refs_1_.7, f32[1,2048,128]{2,1,0:T(8,128)} %all-gather.3.cloned.1.call-done.refs_2_), custom_call_target="tpu_custom_call" | custom-call | tf_op jit(solution)/shard_map/solve/pallas_call | solution.py:162
  89.4 4.9 %all-to-all-start.3 = ((f32[16,128,128]{2,1,0:T(8,128)}), f32[16,128,128]{2,1,0:T(8,128)S(1)}, u32[]{:S(2)}, u32[]{:S(2)}) async-start(f32[16,128,128]{2,1,0:T(8,128)} %get-tuple-element.24), calls=%async_computation.5 | async-start | bytes 2097152 | tf_op jit(solution)/shard_map/all_to_all | solution.py:218
  94.9 7.2 %reduce-scatter.3.cloned.1.call-done = f32[128,128]{1,0:T(8,128)} async-done(((f32[1024,128]{1,0:T(8,128)}), f32[128,128]{1,0:T(8,128)}) %reduce-scatter.3.cloned.1.call-update) | async-done | bytes 65552 | tf_op jit(solution)/shard_map/reduce_scatter | solution.py:255
  102.1 6.5 %all-to-all-done.3.refs_0_ = f32[16,128,128]{2,1,0:T(8,128)S(1)} async-done(((f32[16,128,128]{2,1,0:T(8,128)}), f32[16,128,128]{2,1,0:T(8,128)S(1)}, u32[]{:S(2)}, u32[]{:S(2)}) %all-to-all-start.3) | async-done | bytes 1048608 | tf_op jit(solution)/shard_map/all_to_all | solution.py:218
  109.6 19.2 %all_to_all.46.refs_0_ = f32[16,128,128]{2,1,0:T(8,128)S(1)} all-to-all(f32[16,128,128]{2,1,0:T(8,128)S(1)} %subtract.3), channel_id=1, replica_groups=mesh['z'=8,'core'=2,'x'=4,'y'=4] {'x','y'}, dimensions={0} | all-to-all | bytes 2097152 | tf_op jit(solution)/shard_map/all_to_all | solution.py:218
  128.8 3.7 %solve.5 = (f32[128,128]{1,0:T(8,128)S(1)}, f32[16,128,128]{2,1,0:T(8,128)}) custom-call(f32[16,128,128]{2,1,0:T(8,128)S(1)} %all_to_all.46.refs_0_, f32[4,128,2048]{2,1,0:T(8,128)} %refs_1_.7, f32[5,2048,128]{2,1,0:T(8,128)} %all-gather.5.cloned.1.call-done.refs_2_.refs_3_.refs_4_, f32[5,2048,128]{2,1,0:T(8,128)} %all-gather.5.cloned.1.call-done.refs_2_.refs_3_.refs_4_, ...), custom_call_target="tpu_custom_call" | custom-call | tf_op jit(solution)/shard_map/solve/pallas_call | solution.py:162
  132.5 4.9 %all-to-all-start.5 = ((f32[16,128,128]{2,1,0:T(8,128)}), f32[16,128,128]{2,1,0:T(8,128)S(1)}, u32[]{:S(2)}, u32[]{:S(2)}) async-start(f32[16,128,128]{2,1,0:T(8,128)} %get-tuple-element.26), calls=%async_computation.7 | async-start | bytes 2097152 | tf_op jit(solution)/shard_map/all_to_all | solution.py:218
  137.4 5.7 %reduce-scatter.5.cloned.1.call-done = f32[256,128]{1,0:T(8,128)} async-done(((f32[2048,128]{1,0:T(8,128)}), f32[256,128]{1,0:T(8,128)}) %reduce-scatter.5.cloned.1.call-update) | async-done | bytes 131088 | tf_op jit(solution)/shard_map/reduce_scatter | solution.py:255
  143.1 8.1 %all-to-all-done.5.refs_0_ = f32[16,128,128]{2,1,0:T(8,128)S(1)} async-done(((f32[16,128,128]{2,1,0:T(8,128)}), f32[16,128,128]{2,1,0:T(8,128)S(1)}, u32[]{:S(2)}, u32[]{:S(2)}) %all-to-all-start.5) | async-done | bytes 1048608 | tf_op jit(solution)/shard_map/all_to_all | solution.py:218
  152.3 18.8 %all_to_all.47.refs_0_ = f32[16,128,128]{2,1,0:T(8,128)S(1)} all-to-all(f32[16,128,128]{2,1,0:T(8,128)S(1)} %subtract.4), channel_id=1, replica_groups=mesh['z'=8,'core'=2,'x'=4,'y'=4] {'x','y'}, dimensions={0} | all-to-all | bytes 2097152 | tf_op jit(solution)/shard_map/all_to_all | solution.py:218
  171.1 3.2 %solve.6 = (f32[128,128]{1,0:T(8,128)S(1)}, f32[16,128,128]{2,1,0:T(8,128)S(1)}) custom-call(f32[16,128,128]{2,1,0:T(8,128)S(1)} %all_to_all.47.refs_0_, f32[4,128,2048]{2,1,0:T(8,128)} %refs_1_.7, f32[5,2048,128]{2,1,0:T(8,128)} %all-gather.5.cloned.1.call-done.refs_2_.refs_3_.refs_4_, f32[5,2048,128]{2,1,0:T(8,128)} %all-gather.5.cloned.1.call-done.refs_2_.refs_3_.refs_4_, ...), custom_call_target="tpu_custom_call" | custom-call | tf_op jit(solution)/shard_map/solve/pallas_call | solution.py:162
  174.3 17.7 %all_to_all.48.refs_0_ = f32[16,128,128]{2,1,0:T(8,128)S(1)} all-to-all(f32[16,128,128]{2,1,0:T(8,128)S(1)} %get-tuple-element.28), channel_id=1, replica_groups=mesh['z'=8,'core'=2,'x'=4,'y'=4] {'x','y'}, dimensions={0} | all-to-all | bytes 2097152 | tf_op jit(solution)/shard_map/all_to_all | solution.py:218
  193.1 5.0 %all-to-all-start.8 = ((f32[16,128,128]{2,1,0:T(8,128)}), f32[16,128,128]{2,1,0:T(8,128)S(1)}, u32[]{:S(2)}, u32[]{:S(2)}) async-start(f32[16,128,128]{2,1,0:T(8,128)} %subtract.5), calls=%async_computation.10 | async-start | bytes 2097152 | tf_op jit(solution)/shard_map/all_to_all | solution.py:218
  198.8 11.2 %all-to-all-done.8.refs_0_ = f32[16,128,128]{2,1,0:T(8,128)S(1)} async-done(((f32[16,128,128]{2,1,0:T(8,128)}), f32[16,128,128]{2,1,0:T(8,128)S(1)}, u32[]{:S(2)}, u32[]{:S(2)}) %all-to-all-start.8) | async-done | bytes 1048608 | tf_op jit(solution)/shard_map/all_to_all | solution.py:218
  210.1 2.4 %solve.7 = f32[4,128,128]{2,1,0:T(8,128)} custom-call(f32[16,128,128]{2,1,0:T(8,128)S(1)} %all-to-all-done.8.refs_0_, f32[4,128,2048]{2,1,0:T(8,128)} %refs_1_.7, f32[128,128]{1,0:T(8,128)S(1)} %get-tuple-element.25.refs_4_.refs_5_.refs_2_, f32[128,128]{1,0:T(8,128)S(1)} %get-tuple-element.27.refs_6_.refs_3_, f32[128,128]{1,0:T(8,128)S(1)} %get-tuple-element.29.refs_4_), custom_call_target="tpu_custom_call" | custom-call | tf_op jit(solution)/shard_map/solve/pallas_call | solution.py:162
  (48 shorter events, 12.8 us)
Async XLA Ops:
  8.0 0.7 copy-start.5
  8.7 0.7 copy-start.6
  9.3 12.5 %copy-start.7 = (f32[512,4,128]{2,1,0:T(4,128)S(1)}, f32[512,4,128]{2,1,0:T(4,128)}, u32[]{:S(2)}) copy-start(f32[512,4,128]{2,1,0:T(4,128)} %param.7) | copy-start | bytes 3145732
  9.9 16.2 %all-to-all-start = ((s32[16,2,128]{2,1,0:T(2,128)}), s32[16,2,128]{2,1,0:T(2,128)S(1)}, u32[]{:S(2)}, u32[]{:S(2)}) async-start(s32[16,2,128]{2,1,0:T(2,128)} %pair.1), calls=%async_computation | async-start | bytes 32768 | tf_op jit(solution)/shard_map/all_to_all | solution.py:241
  18.5 52.7 %all-gather.3.cloned.1.call-start = ((), (), s32[]{:S(2)}) async-start(), calls=%async_computation.13 | async-start | bytes 1114112 | tf_op jit(solution)/shard_map/all_gather | solution.py:228
  20.1 82.1 %reduce-scatter.3.cloned.1.call-start = ((), (), s32[]{:S(2)}) async-start(), calls=%async_computation.11 | async-start | bytes 589824 | tf_op jit(solution)/shard_map/reduce_scatter | solution.py:255
  29.5 2.0 collective-permute-start
  36.5 25.0 %collective-permute-start.1 = (f32[8,384,128]{2,1,0:T(8,128)S(1)}, f32[8,384,128]{2,1,0:T(8,128)S(1)}, u32[]{:S(2)}, u32[]{:S(2)}) collective-permute-start(f32[8,384,128]{2,1,0:T(8,128)S(1)} %get-tuple-element.20), channel_id=1, source_target_pairs={{0,16},{16,0},{1,17},{17,1},{2,18},{18,2},{3,19},{19,3},{4,20},{20... | collective-permute-start | bytes 4718600 | tf_op jit(solution)/shard_map/ppermute | solution.py:254
  61.5 1.4 copy-start.2
  62.9 65.9 %all-gather.5.cloned.1.call-start = ((), (), s32[]{:S(2)}) async-start(), calls=%async_computation.14 | async-start | bytes 5570560 | tf_op jit(solution)/shard_map/all_gather | solution.py:228
  63.7 22.3 %all-to-all-start.2 = ((f32[16,128,128]{2,1,0:T(8,128)}), f32[16,128,128]{2,1,0:T(8,128)S(1)}, u32[]{:S(2)}, u32[]{:S(2)}) async-start(f32[16,128,128]{2,1,0:T(8,128)} %get-tuple-element.23), calls=%async_computation.4 | async-start | bytes 2097152 | tf_op jit(solution)/shard_map/all_to_all | solution.py:218
  89.4 19.2 %all-to-all-start.3 = ((f32[16,128,128]{2,1,0:T(8,128)}), f32[16,128,128]{2,1,0:T(8,128)S(1)}, u32[]{:S(2)}, u32[]{:S(2)}) async-start(f32[16,128,128]{2,1,0:T(8,128)} %get-tuple-element.24), calls=%async_computation.5 | async-start | bytes 2097152 | tf_op jit(solution)/shard_map/all_to_all | solution.py:218
  94.3 48.8 %reduce-scatter.5.cloned.1.call-start = ((), (), s32[]{:S(2)}) async-start(), calls=%async_computation.12 | async-start | bytes 1179648 | tf_op jit(solution)/shard_map/reduce_scatter | solution.py:255
  108.6 0.8 copy-start.3
  132.5 18.8 %all-to-all-start.5 = ((f32[16,128,128]{2,1,0:T(8,128)}), f32[16,128,128]{2,1,0:T(8,128)S(1)}, u32[]{:S(2)}, u32[]{:S(2)}) async-start(f32[16,128,128]{2,1,0:T(8,128)} %get-tuple-element.26), calls=%async_computation.7 | async-start | bytes 2097152 | tf_op jit(solution)/shard_map/all_to_all | solution.py:218
  151.3 0.9 copy-start
  174.2 17.7 %copy-start.1 = (f32[256,128]{1,0:T(8,128)S(1)}, f32[256,128]{1,0:T(8,128)}, u32[]{:S(2)}) copy-start(f32[256,128]{1,0:T(8,128)} %reduce-scatter.5.cloned.1.call-done) | copy-start | bytes 393220
  193.1 5.0 %copy-start.4 = (f32[128,128]{1,0:T(8,128)S(1)}, f32[128,128]{1,0:T(8,128)}, u32[]{:S(2)}) copy-start(f32[128,128]{1,0:T(8,128)} %reduce-scatter.3.cloned.1.call-done) | copy-start | bytes 196612
  193.1 17.0 %all-to-all-start.8 = ((f32[16,128,128]{2,1,0:T(8,128)}), f32[16,128,128]{2,1,0:T(8,128)S(1)}, u32[]{:S(2)}, u32[]{:S(2)}) async-start(f32[16,128,128]{2,1,0:T(8,128)} %subtract.5), calls=%async_computation.10 | async-start | bytes 2097152 | tf_op jit(solution)/shard_map/all_to_all | solution.py:218
Sparse Core Ops, SparseCore 0:
  21.9 42.4 all-gather.2
  66.3 44.6 all-gather.4
Sparse Core Ops, SparseCore 1:
  63.0 39.1 reduce-scatter.2
  104.7 38.4 reduce-scatter.4

commit v5 on v3

--- a/solution.py
+++ b/solution.py
@@ -17,6 +17,7 @@
 BF16 = jnp.bfloat16
 SMEM = pl.BlockSpec(memory_space=pltpu.SMEM)
 VMEM = pl.BlockSpec(memory_space=pltpu.VMEM)
+HBM = pl.BlockSpec(memory_space=pltpu.HBM)
 PARAMS = pltpu.CompilerParams(vmem_limit_bytes=LIMIT)
 
 
@@ -68,38 +69,116 @@
     )(here, index, rows, after)
 
 
-def remain_kernel(block, *refs):
-    terms = refs[0]
+def in_hbm(array):
+    return pltpu.with_memory_space_constraint(array, pltpu.HBM)
+
+
+def added(terms):
     total = terms[0]
     for part in range(1, terms.shape[0]):
         total += terms[part]
-    if block is None:
-        refs[1][...] = total
-    else:
-        total = refs[1][block] - total
+    return total
+
+
+def first_kernel(terms, total_ref, copies):
+    total = added(terms)
+    total_ref[...] = total
     for owner in range(GROUP):
-        refs[2][owner] = total
-
-
-def spread(terms, minuend=None, block=None):
-    copies = jax.ShapeDtypeStruct((GROUP, SIDE, SIDE), F32)
-    if minuend is None:
-        return pl.pallas_call(
-            functools.partial(remain_kernel, None),
-            out_shape=(jax.ShapeDtypeStruct((SIDE, SIDE), F32), copies),
-            in_specs=[VMEM],
-            out_specs=(VMEM, VMEM),
-            compiler_params=PARAMS,
-            name="sum_first",
-        )(terms)
-    return pl.pallas_call(
-        functools.partial(remain_kernel, block),
-        out_shape=copies,
-        in_specs=[VMEM, VMEM],
+        copies[owner] = total
+
+
+def spread_first(terms):
+    return pl.pallas_call(
+        first_kernel,
+        out_shape=(
+            jax.ShapeDtypeStruct((SIDE, SIDE), F32),
+            jax.ShapeDtypeStruct((GROUP, SIDE, SIDE), F32),
+        ),
+        in_specs=[VMEM],
+        out_specs=(VMEM, VMEM),
+        compiler_params=PARAMS,
+        name="sum_first",
+    )(terms)
+
+
+def subtract_kernel(block, terms, minuend, copies, held, sem):
+    fetch = pltpu.make_async_copy(minuend.at[block], held, sem.at[0])
+    fetch.start()
+    total = added(terms)
+    fetch.wait()
+    total = held[...] - total
+    for owner in range(GROUP):
+        copies[owner] = total
+
+
+def spread(terms, minuend, block):
+    return pl.pallas_call(
+        functools.partial(subtract_kernel, block),
+        out_shape=jax.ShapeDtypeStruct((GROUP, SIDE, SIDE), F32),
+        in_specs=[VMEM, HBM],
         out_specs=VMEM,
+        scratch_shapes=[pltpu.VMEM((SIDE, SIDE), F32), pltpu.SemaphoreType.DMA((1,))],
         compiler_params=PARAMS,
         name="subtract",
-    )(terms, minuend)
+    )(terms, in_hbm(minuend))
+
+
+def first_block_kernel(blocks, out, sem):
+    copy = pltpu.make_async_copy(blocks.at[0:1], out, sem.at[0])
+    copy.start()
+    copy.wait()
+
+
+def first_block(blocks):
+    return pl.pallas_call(
+        first_block_kernel,
+        out_shape=jax.ShapeDtypeStruct((1,) + blocks.shape[1:], F32),
+        in_specs=[HBM],
+        out_specs=HBM,
+        scratch_shapes=[pltpu.SemaphoreType.DMA((1,))],
+        compiler_params=PARAMS,
+        name="first_block",
+    )(in_hbm(blocks))
+
+
+def pair_kernel(sire, dam, after, pair, held, sems):
+    copies = [
+        pltpu.make_async_copy(sire, held.at[0:1], sems.at[0]),
+        pltpu.make_async_copy(dam, held.at[1:2], sems.at[1]),
+    ]
+    for copy in copies:
+        copy.start()
+    for copy in copies:
+        copy.wait()
+    for owner in range(GROUP):
+        pair[owner] = held[...]
+
+
+def pair_copies(sire, dam, after):
+    return pl.pallas_call(
+        pair_kernel,
+        out_shape=jax.ShapeDtypeStruct((GROUP, 2, SIDE), jnp.int32),
+        in_specs=[HBM, HBM, pl.BlockSpec(memory_space=pl.ANY)],
+        out_specs=VMEM,
+        scratch_shapes=[pltpu.VMEM((2, SIDE), jnp.int32), pltpu.SemaphoreType.DMA((2,))],
+        compiler_params=PARAMS,
+        name="pair",
+    )(in_hbm(sire), in_hbm(dam), after)
+
+
+def add_kernel(one, other, after, out):
+    out[...] = one[...] + other[...]
+
+
+def add(one, other, after):
+    return pl.pallas_call(
+        add_kernel,
+        out_shape=jax.ShapeDtypeStruct(one.shape, F32),
+        in_specs=[VMEM, VMEM, pl.BlockSpec(memory_space=pl.ANY)],
+        out_specs=VMEM,
+        compiler_params=PARAMS,
+        name="add",
+    )(one, other, after)
 
 
 def solve_kernel(target, last, places, *refs):
@@ -204,11 +283,10 @@
     def gathered(some):
         return pltpu.with_memory_space_constraint(lax.all_gather(some, ROW, axis=1, tiled=True), pltpu.HBM)
 
-    start = gathered(factor_blocks[:1])
     inverses = pltpu.with_memory_space_constraint(inverses, pltpu.HBM)
-
-    pair = jnp.stack([sire_index, dam_index])
-    index = lax.all_to_all(jnp.broadcast_to(pair[None], (GROUP, 2, SIDE)), ROW, 0, 0)
+    first = first_block(factor_blocks)
+    start = gathered(first)
+    index = lax.all_to_all(pair_copies(sire_index[None], dam_index[None], first), ROW, 0, 0)
 
     def rows_of(first, count):
         rows = relatives[:, first : first + count, :].reshape(old_dev, count * SIDE).T
@@ -216,26 +294,27 @@
 
     keep, give = select(1, here, index, rows_of(0, 1), here)
     first_terms = keep + lax.ppermute(give, "core", swap)
-    relation0, copies = spread(lax.all_to_all(first_terms, "z", 0, 0))
-
-    rest = gathered(hold(factor_blocks, relation0))
+    relation0, copies = spread_first(lax.all_to_all(first_terms, "z", 0, 0))
+
+    whole = to_group(copies)
+    rest = gathered(hold(factor_blocks, whole))
 
     keep, give = select(blocks - 1, here, index, rows_of(1, blocks - 1), first_terms)
-    terms = keep + lax.ppermute(give, "core", swap)
+    terms = add(keep, lax.ppermute(give, "core", swap), relation0)
     later = lax.psum_scatter(terms.reshape(-1, SIDE), "z", scatter_dimension=0, tiled=True)
     later = later.reshape(blocks - 1, SIDE, SIDE)
 
     solved = []
     for target in range(blocks):
         if target > 0:
-            copies = spread(to_group(terms), later, target - 1)
+            whole = to_group(spread(to_group(terms), later, target - 1))
         first = target * (target + 1) // 2
         factors = [(rest, first + source - 1) for source in range(target + 1)]
         if target == 0:
             factors = [(start, 0)]
         if target + 1 == blocks:
             factors = []
-        own, terms = solve(target, to_group(copies), inverses, factors, solved)
+        own, terms = solve(target, whole, inverses, factors, solved)
         solved.append(own)
     relationship = jnp.concatenate([relation0[None], later])
     return relationship, solved[-1]

time: 214 us -> 224 us (1.047)
  blocking collectives: 110 us -> 142 us
  waiting for transfers between devices: 35.8 us -> 18.7 us
  starting transfers between devices: 21.6 us -> 14.2 us
  Pallas kernels: 22 us -> 29.2 us
  local copies, waits for them, and re-layouts: 5.13 us -> 2.12 us
    all_to_all x5 -> x6, blocking collectives: 85.8 us -> 121 us  [to_group(): return lax.all_to_all(parts, COL, 0, 0)]
    all_to_all x2 -> x1, waiting for transfers between devices: 27.2 us -> 11.9 us  [to_group(): return lax.all_to_all(parts, COL, 0, 0)]
    all_to_all x2 -> x1, starting transfers between devices: 12.5 us -> 5.05 us  [to_group(): return lax.all_to_all(parts, COL, 0, 0)]
    pallas_call x4 -> x7, Pallas kernels: 2.55 us -> 9.68 us  [the longest x3 3.85 us: spread(): pl.pallas_call(functools.partial(subtract_kernel, block), out_shape=jax.S...]
    all_to_all x1, blocking collectives: 24 us -> 20.5 us  [per_device(): relation0, copies = spread_first(lax.all_to_all(first_terms, 'z', 0, 0))]
    ppermute x1, waiting for transfers between devices: 3.27 us -> 0.01 us  [per_device(): terms = add(keep, lax.ppermute(give, 'core', swap), relation0)]
  transfers between devices with their start and end apart: 8 -> 7, of which waited for: 5 -> 3; matrix products, arithmetic and copies ran while one was open for 3% -> 1% of each run, Pallas kernels for 6% -> 7%
where the time goes in v5:
time: 224 us; the launch traced here: 223 us
  blocking collectives  142 us (63%)
  Pallas kernels  29.2 us (13%)
  waiting for transfers between devices  18.7 us (8%)
  between operations  15.7 us (7%)
  starting transfers between devices  14.2 us (6%)
    all_to_all x6, blocking collectives, to_group(): return lax.all_to_all(parts, COL, 0, 0)  121 us
    all_to_all x1, blocking collectives, per_device(): relation0, copies = spread_first(lax.all_to_all(first_terms, 'z', 0, 0))  20.5 us
    all_to_all x1, waiting for transfers between devices, to_group(): return lax.all_to_all(parts, COL, 0, 0)  11.9 us
    pallas_call x4, Pallas kernels, solve(): pl.pallas_call(functools.partial(solve_kernel, target, last, tuple((block...  10.4 us
    all_to_all x1, starting transfers between devices, per_device(): lax.all_to_all(pair_copies(sire_index[None], dam_index[None], first), ROW...  8.58 us
    pallas_call x2, Pallas kernels, select(): pl.pallas_call(functools.partial(select_kernel, count), out_shape=(shape,...  8.29 us
    all_to_all x1, waiting for transfers between devices, per_device(): lax.all_to_all(pair_copies(sire_index[None], dam_index[None], first), ROW...  5.24 us
    all_to_all x1, starting transfers between devices, to_group(): return lax.all_to_all(parts, COL, 0, 0)  5.05 us
  transfers between devices with their start and end apart: 7, of which 3 were waited for; matrix products, arithmetic and copies ran while one was open for 1% of the time, Pallas kernels for 7%

profile of v5, /device:TPU:8, one launch (start us, length us, event | category | flops | bytes accessed | tf_op | source)
XLA Modules:
  0.0 222.8 jit_solution(9387001216489450293)
XLA Ops:
  8.1 3.1 %first_block.1.after = f32[1,128,128]{2,1,0:T(8,128)} custom-call(f32[6,128,128]{2,1,0:T(8,128)} %blocks.3), custom_call_target="tpu_custom_call" | custom-call | tf_op jit(solution)/shard_map/first_block/pallas_call | solution.py:133
  11.2 1.3 pair.1
  12.5 8.6 %all-to-all-start = ((s32[16,2,128]{2,1,0:T(2,128)}), s32[16,2,128]{2,1,0:T(2,128)S(1)}, u32[]{:S(2)}, u32[]{:S(2)}) async-start(s32[16,2,128]{2,1,0:T(2,128)} %pair.1), calls=%async_computation | async-start | bytes 32768 | tf_op jit(solution)/shard_map/all_to_all | solution.py:289
  21.1 1.4 slice.6
  23.5 5.2 %all-to-all-done.index = s32[16,2,128]{2,1,0:T(2,128)S(1)} async-done(((s32[16,2,128]{2,1,0:T(2,128)}), s32[16,2,128]{2,1,0:T(2,128)S(1)}, u32[]{:S(2)}, u32[]{:S(2)}) %all-to-all-start) | async-done | bytes 16416 | tf_op jit(solution)/shard_map/all_to_all | solution.py:289
  28.7 3.3 %select.2 = (f32[8,128,128]{2,1,0:T(8,128)S(1)}, f32[8,128,128]{2,1,0:T(8,128)S(1)}) custom-call(s32[4]{0:T(128)S(1)} %pad_add_fusion.here.after, s32[16,2,128]{2,1,0:T(2,128)S(1)} %all-to-all-done.index, bf16[384,512]{1,0:T(8,128)(2,1)S(1)} %pad_maximum_fusion.1.rows, s32[4]{0:T(128)S(1)} %pad_add_fusion.here.after), custom_call_target="tpu_custom_call" | custom-call | flops 805306368 | bytes 1048576 | tf_op jit(solution)/shard_map/select/pallas_call | solution.py:59
  32.5 1.5 collective-permute-done
  34.1 5.0 %select.3 = (f32[8,384,128]{2,1,0:T(8,128)S(1)}, f32[8,384,128]{2,1,0:T(8,128)S(1)}) custom-call(s32[4]{0:T(128)S(1)} %pad_add_fusion.here.after, s32[16,2,128]{2,1,0:T(2,128)S(1)} %all-to-all-done.index, bf16[1152,512]{1,0:T(8,128)(2,1)S(1)} %pad_maximum_fusion.rows, f32[8,128,128]{2,1,0:T(8,128)S(1)} %add.10.after), custom_call_target="tpu_custom_call" | custom-call | flops 2415919104 | bytes 3145728 | tf_op jit(solution)/shard_map/select/pallas_call | solution.py:59
  39.3 20.5 %all_to_all.45.terms = f32[8,128,128]{2,1,0:T(8,128)S(1)} all-to-all(f32[8,128,128]{2,1,0:T(8,128)S(1)} %add.10.after), channel_id=1, replica_groups=mesh['z'=8,'core'=2,'x'=4,'y'=4] {'z'}, dimensions={0} | all-to-all | bytes 1048576 | tf_op jit(solution)/shard_map/all_to_all | solution.py:297
  60.0 1.3 add.16
  61.4 22.8 %all_to_all.46.refs_0_.after = f32[16,128,128]{2,1,0:T(8,128)S(1)} all-to-all(f32[16,128,128]{2,1,0:T(8,128)S(1)} %get-tuple-element.19), channel_id=1, replica_groups=mesh['z'=8,'core'=2,'x'=4,'y'=4] {'x','y'}, dimensions={0} | all-to-all | bytes 2097152 | tf_op jit(solution)/shard_map/all_to_all | solution.py:274
  85.1 2.2 %solve.4 = (f32[128,128]{1,0:T(8,128)S(1)}, f32[16,128,128]{2,1,0:T(8,128)S(1)}) custom-call(f32[16,128,128]{2,1,0:T(8,128)S(1)} %all_to_all.46.refs_0_.after, f32[4,128,2048]{2,1,0:T(8,128)} %refs_1_.7, f32[1,2048,128]{2,1,0:T(8,128)} %all-gather.3.cloned.1.call-done.refs_2_), custom_call_target="tpu_custom_call" | custom-call | tf_op jit(solution)/shard_map/solve/pallas_call | solution.py:241
  87.3 19.9 %all_to_all.47.terms = f32[16,128,128]{2,1,0:T(8,128)S(1)} all-to-all(f32[16,128,128]{2,1,0:T(8,128)S(1)} %get-tuple-element.20), channel_id=1, replica_groups=mesh['z'=8,'core'=2,'x'=4,'y'=4] {'x','y'}, dimensions={0} | all-to-all | bytes 2097152 | tf_op jit(solution)/shard_map/all_to_all | solution.py:274
  107.2 1.0 subtract.3
  108.2 18.3 %all_to_all.48.refs_0_ = f32[16,128,128]{2,1,0:T(8,128)S(1)} all-to-all(f32[16,128,128]{2,1,0:T(8,128)S(1)} %subtract.3), channel_id=1, replica_groups=mesh['z'=8,'core'=2,'x'=4,'y'=4] {'x','y'}, dimensions={0} | all-to-all | bytes 2097152 | tf_op jit(solution)/shard_map/all_to_all | solution.py:274
  126.5 2.6 %solve.5 = (f32[128,128]{1,0:T(8,128)S(1)}, f32[16,128,128]{2,1,0:T(8,128)S(1)}) custom-call(f32[16,128,128]{2,1,0:T(8,128)S(1)} %all_to_all.48.refs_0_, f32[4,128,2048]{2,1,0:T(8,128)} %refs_1_.7, f32[5,2048,128]{2,1,0:T(8,128)} %all-gather.5.cloned.1.call-done.refs_2_.refs_3_.refs_4_, f32[5,2048,128]{2,1,0:T(8,128)} %all-gather.5.cloned.1.call-done.refs_2_.refs_3_.refs_4_, ...), custom_call_target="tpu_custom_call" | custom-call | tf_op jit(solution)/shard_map/solve/pallas_call | solution.py:241
  129.1 22.0 %all_to_all.49.terms = f32[16,128,128]{2,1,0:T(8,128)S(1)} all-to-all(f32[16,128,128]{2,1,0:T(8,128)S(1)} %get-tuple-element.22), channel_id=1, replica_groups=mesh['z'=8,'core'=2,'x'=4,'y'=4] {'x','y'}, dimensions={0} | all-to-all | bytes 2097152 | tf_op jit(solution)/shard_map/all_to_all | solution.py:274
  152.1 19.6 %all_to_all.50.refs_0_ = f32[16,128,128]{2,1,0:T(8,128)S(1)} all-to-all(f32[16,128,128]{2,1,0:T(8,128)S(1)} %subtract.4), channel_id=1, replica_groups=mesh['z'=8,'core'=2,'x'=4,'y'=4] {'x','y'}, dimensions={0} | all-to-all | bytes 2097152 | tf_op jit(solution)/shard_map/all_to_all | solution.py:274
  171.7 3.2 %solve.6 = (f32[128,128]{1,0:T(8,128)S(1)}, f32[16,128,128]{2,1,0:T(8,128)S(1)}) custom-call(f32[16,128,128]{2,1,0:T(8,128)S(1)} %all_to_all.50.refs_0_, f32[4,128,2048]{2,1,0:T(8,128)} %refs_1_.7, f32[5,2048,128]{2,1,0:T(8,128)} %all-gather.5.cloned.1.call-done.refs_2_.refs_3_.refs_4_, f32[5,2048,128]{2,1,0:T(8,128)} %all-gather.5.cloned.1.call-done.refs_2_.refs_3_.refs_4_, ...), custom_call_target="tpu_custom_call" | custom-call | tf_op jit(solution)/shard_map/solve/pallas_call | solution.py:241
  174.9 18.4 %all_to_all.51.terms = f32[16,128,128]{2,1,0:T(8,128)S(1)} all-to-all(f32[16,128,128]{2,1,0:T(8,128)S(1)} %get-tuple-element.24), channel_id=1, replica_groups=mesh['z'=8,'core'=2,'x'=4,'y'=4] {'x','y'}, dimensions={0} | all-to-all | bytes 2097152 | tf_op jit(solution)/shard_map/all_to_all | solution.py:274
  193.3 1.9 subtract.5
  195.3 5.0 %all-to-all-start.8 = ((f32[16,128,128]{2,1,0:T(8,128)}), f32[16,128,128]{2,1,0:T(8,128)S(1)}, u32[]{:S(2)}, u32[]{:S(2)}) async-start(f32[16,128,128]{2,1,0:T(8,128)} %subtract.5), calls=%async_computation.9 | async-start | bytes 2097152 | tf_op jit(solution)/shard_map/all_to_all | solution.py:274
  201.1 11.9 %all-to-all-done.8.refs_0_ = f32[16,128,128]{2,1,0:T(8,128)S(1)} async-done(((f32[16,128,128]{2,1,0:T(8,128)}), f32[16,128,128]{2,1,0:T(8,128)S(1)}, u32[]{:S(2)}, u32[]{:S(2)}) %all-to-all-start.8) | async-done | bytes 1048608 | tf_op jit(solution)/shard_map/all_to_all | solution.py:274
  212.9 2.4 %solve.7 = f32[4,128,128]{2,1,0:T(8,128)} custom-call(f32[16,128,128]{2,1,0:T(8,128)S(1)} %all-to-all-done.8.refs_0_, f32[4,128,2048]{2,1,0:T(8,128)} %refs_1_.7, f32[128,128]{1,0:T(8,128)S(1)} %get-tuple-element.21.refs_4_.refs_5_.refs_2_, f32[128,128]{1,0:T(8,128)S(1)} %get-tuple-element.23.refs_6_.refs_3_, f32[128,128]{1,0:T(8,128)S(1)} %get-tuple-element.25.refs_4_), custom_call_target="tpu_custom_call" | custom-call | tf_op jit(solution)/shard_map/solve/pallas_call | solution.py:241
  (32 shorter events, 4.4 us)
Async XLA Ops:
  8.0 14.9 %copy-start.2 = (f32[512,4,128]{2,1,0:T(4,128)S(1)}, f32[512,4,128]{2,1,0:T(4,128)}, u32[]{:S(2)}) copy-start(f32[512,4,128]{2,1,0:T(4,128)} %param.7) | copy-start | bytes 3145732
  8.0 77.0 %all-gather.3.cloned.1.call-start = ((), (), s32[]{:S(2)}) async-start(), calls=%async_computation.11 | async-start | bytes 1114112 | tf_op jit(solution)/shard_map/all_gather | solution.py:284
  12.5 16.2 %all-to-all-start = ((s32[16,2,128]{2,1,0:T(2,128)}), s32[16,2,128]{2,1,0:T(2,128)S(1)}, u32[]{:S(2)}, u32[]{:S(2)}) async-start(s32[16,2,128]{2,1,0:T(2,128)} %pair.1), calls=%async_computation | async-start | bytes 32768 | tf_op jit(solution)/shard_map/all_to_all | solution.py:289
  21.1 86.2 %reduce-scatter.2.cloned.1.call-start = ((), (), s32[]{:S(2)}) async-start(), calls=%async_computation.10 | async-start | bytes 1769472 | tf_op jit(solution)/shard_map/reduce_scatter | solution.py:304
  32.0 2.0 collective-permute-start
  39.1 20.9 %collective-permute-start.1 = (f32[8,384,128]{2,1,0:T(8,128)S(1)}, f32[8,384,128]{2,1,0:T(8,128)S(1)}, u32[]{:S(2)}, u32[]{:S(2)}) collective-permute-start(f32[8,384,128]{2,1,0:T(8,128)S(1)} %get-tuple-element.18), channel_id=1, source_target_pairs={{0,16},{16,0},{1,17},{17,1},{2,18},{18,2},{3,19},{19,3},{4,20},{20... | collective-permute-start | bytes 4718600 | tf_op jit(solution)/shard_map/ppermute | solution.py:303
  61.3 22.9 %copy-start = (f32[6,128,128]{2,1,0:T(8,128)S(1)}, f32[6,128,128]{2,1,0:T(8,128)}, u32[]{:S(2)}) copy-start(f32[6,128,128]{2,1,0:T(8,128)} %blocks.3) | copy-start | bytes 1179652
  61.3 65.2 %all-gather.5.cloned.1.call-start = ((), (), s32[]{:S(2)}) async-start(), calls=%async_computation.12 | async-start | bytes 5570560 | tf_op jit(solution)/shard_map/all_gather | solution.py:284
  195.3 5.1 %copy-start.1 = (f32[384,128]{1,0:T(8,128)S(1)}, f32[384,128]{1,0:T(8,128)}, u32[]{:S(2)}) copy-start(f32[384,128]{1,0:T(8,128)} %reduce-scatter.2.cloned.1.call-done) | copy-start | bytes 589828
  195.3 17.6 %all-to-all-start.8 = ((f32[16,128,128]{2,1,0:T(8,128)}), f32[16,128,128]{2,1,0:T(8,128)S(1)}, u32[]{:S(2)}, u32[]{:S(2)}) async-start(f32[16,128,128]{2,1,0:T(8,128)} %subtract.5), calls=%async_computation.9 | async-start | bytes 2097152 | tf_op jit(solution)/shard_map/all_to_all | solution.py:274
Sparse Core Ops, SparseCore 0:
  11.3 43.3 all-gather.2
  85.1 40.1 all-gather.4
Sparse Core Ops, SparseCore 1:
  61.4 42.1 reduce-scatter.1

commit v6 on v5

--- a/solution.py
+++ b/solution.py
@@ -134,7 +134,7 @@
         first_block_kernel,
         out_shape=jax.ShapeDtypeStruct((1,) + blocks.shape[1:], F32),
         in_specs=[HBM],
-        out_specs=HBM,
+        out_specs=VMEM,
         scratch_shapes=[pltpu.SemaphoreType.DMA((1,))],
         compiler_params=PARAMS,
         name="first_block",
@@ -297,7 +297,7 @@
     relation0, copies = spread_first(lax.all_to_all(first_terms, "z", 0, 0))
 
     whole = to_group(copies)
-    rest = gathered(hold(factor_blocks, whole))
+    rest = gathered(hold(factor_blocks, relation0))
 
     keep, give = select(blocks - 1, here, index, rows_of(1, blocks - 1), first_terms)
     terms = add(keep, lax.ppermute(give, "core", swap), relation0)

time: 224 us -> 225 us (level)
  blocking collectives: 142 us -> 116 us
  waiting for transfers between devices: 18.7 us -> 37.8 us
  starting transfers between devices: 14.2 us -> 21.6 us
    all_to_all x6 -> x5, blocking collectives: 121 us -> 95.2 us  [to_group(): return lax.all_to_all(parts, COL, 0, 0)]
    all_to_all x1 -> x2, waiting for transfers between devices: 11.9 us -> 27.5 us  [to_group(): return lax.all_to_all(parts, COL, 0, 0)]
    all_to_all x1 -> x2, starting transfers between devices: 5.05 us -> 12.4 us  [to_group(): return lax.all_to_all(parts, COL, 0, 0)]
    reduce_scatter x1, waiting for transfers between devices: 0.01 us -> 3.51 us  [per_device(): lax.psum_scatter(terms.reshape(-1, SIDE), 'z', scatter_dimension=0, tiled...]
  transfers between devices with their start and end apart: 7 -> 8, of which waited for: 3 -> 5; matrix products, arithmetic and copies ran while one was open for 1% -> 1% of each run, Pallas kernels for 7% -> 7%
where the time goes in v6:
time: 225 us; the launch traced here: 224 us
  blocking collectives  116 us (52%)
  waiting for transfers between devices  37.8 us (17%)
  Pallas kernels  28.7 us (13%)
  starting transfers between devices  21.6 us (10%)
  between operations  15.7 us (7%)
  local copies, waits for them, and re-layouts  3.04 us (1%)
    all_to_all x5, blocking collectives, to_group(): return lax.all_to_all(parts, COL, 0, 0)  95.2 us
    all_to_all x2, waiting for transfers between devices, to_group(): return lax.all_to_all(parts, COL, 0, 0)  27.5 us
    all_to_all x1, blocking collectives, per_device(): relation0, copies = spread_first(lax.all_to_all(first_terms, 'z', 0, 0))  20.8 us
    all_to_all x2, starting transfers between devices, to_group(): return lax.all_to_all(parts, COL, 0, 0)  12.4 us
    pallas_call x4, Pallas kernels, solve(): pl.pallas_call(functools.partial(solve_kernel, target, last, tuple((block...  10.4 us
    all_to_all x1, starting transfers between devices, per_device(): lax.all_to_all(pair_copies(sire_index[None], dam_index[None], first), ROW...  8.58 us
    pallas_call x2, Pallas kernels, select(): pl.pallas_call(functools.partial(select_kernel, count), out_shape=(shape,...  8.27 us
    all_to_all x1, waiting for transfers between devices, per_device(): lax.all_to_all(pair_copies(sire_index[None], dam_index[None], first), ROW...  5.24 us
  transfers between devices with their start and end apart: 8, of which 5 were waited for; matrix products, arithmetic and copies ran while one was open for 1% of the time, Pallas kernels for 7%

profile of v6, /device:TPU:8, one launch (start us, length us, event | category | flops | bytes accessed | tf_op | source)
XLA Modules:
  0.0 224.0 jit_solution(2842786108688878238)
XLA Ops:
  8.1 1.6 first_block.1.after
  11.0 8.6 %all-to-all-start = ((s32[16,2,128]{2,1,0:T(2,128)}), s32[16,2,128]{2,1,0:T(2,128)S(1)}, u32[]{:S(2)}, u32[]{:S(2)}) async-start(s32[16,2,128]{2,1,0:T(2,128)} %pair.1), calls=%async_computation | async-start | bytes 32768 | tf_op jit(solution)/shard_map/all_to_all | solution.py:289
  19.6 1.4 slice.6
  21.9 5.2 %all-to-all-done.index = s32[16,2,128]{2,1,0:T(2,128)S(1)} async-done(((s32[16,2,128]{2,1,0:T(2,128)}), s32[16,2,128]{2,1,0:T(2,128)S(1)}, u32[]{:S(2)}, u32[]{:S(2)}) %all-to-all-start) | async-done | bytes 16416 | tf_op jit(solution)/shard_map/all_to_all | solution.py:289
  27.2 3.3 %select.2 = (f32[8,128,128]{2,1,0:T(8,128)S(1)}, f32[8,128,128]{2,1,0:T(8,128)S(1)}) custom-call(s32[4]{0:T(128)S(1)} %pad_add_fusion.here.after, s32[16,2,128]{2,1,0:T(2,128)S(1)} %all-to-all-done.index, bf16[384,512]{1,0:T(8,128)(2,1)S(1)} %pad_maximum_fusion.1.rows, s32[4]{0:T(128)S(1)} %pad_add_fusion.here.after), custom_call_target="tpu_custom_call" | custom-call | flops 805306368 | bytes 1048576 | tf_op jit(solution)/shard_map/select/pallas_call | solution.py:59
  31.0 1.5 collective-permute-done
  32.6 4.9 %select.3 = (f32[8,384,128]{2,1,0:T(8,128)S(1)}, f32[8,384,128]{2,1,0:T(8,128)S(1)}) custom-call(s32[4]{0:T(128)S(1)} %pad_add_fusion.here.after, s32[16,2,128]{2,1,0:T(2,128)S(1)} %all-to-all-done.index, bf16[1152,512]{1,0:T(8,128)(2,1)S(1)} %pad_maximum_fusion.rows, f32[8,128,128]{2,1,0:T(8,128)S(1)} %add.10.after), custom_call_target="tpu_custom_call" | custom-call | flops 2415919104 | bytes 3145728 | tf_op jit(solution)/shard_map/select/pallas_call | solution.py:59
  37.7 20.8 %all_to_all.45.terms = f32[8,128,128]{2,1,0:T(8,128)S(1)} all-to-all(f32[8,128,128]{2,1,0:T(8,128)S(1)} %add.10.after), channel_id=1, replica_groups=mesh['z'=8,'core'=2,'x'=4,'y'=4] {'z'}, dimensions={0} | all-to-all | bytes 1048576 | tf_op jit(solution)/shard_map/all_to_all | solution.py:297
  59.7 1.3 add.16
  62.8 7.4 %all-to-all-start.2 = ((f32[16,128,128]{2,1,0:T(8,128)}), f32[16,128,128]{2,1,0:T(8,128)S(1)}, u32[]{:S(2)}, u32[]{:S(2)}) async-start(f32[16,128,128]{2,1,0:T(8,128)} %get-tuple-element.19), calls=%async_computation.3 | async-start | bytes 2097152 | tf_op jit(solution)/shard_map/all_to_all | solution.py:274
  70.2 16.6 %all-to-all-done.2.refs_0_ = f32[16,128,128]{2,1,0:T(8,128)S(1)} async-done(((f32[16,128,128]{2,1,0:T(8,128)}), f32[16,128,128]{2,1,0:T(8,128)S(1)}, u32[]{:S(2)}, u32[]{:S(2)}) %all-to-all-start.2) | async-done | bytes 1048608 | tf_op jit(solution)/shard_map/all_to_all | solution.py:274
  86.8 2.3 %solve.4 = (f32[128,128]{1,0:T(8,128)S(1)}, f32[16,128,128]{2,1,0:T(8,128)S(1)}) custom-call(f32[16,128,128]{2,1,0:T(8,128)S(1)} %all-to-all-done.2.refs_0_, f32[4,128,2048]{2,1,0:T(8,128)} %refs_1_.7, f32[1,2048,128]{2,1,0:T(8,128)} %all-gather.3.cloned.1.call-done.refs_2_), custom_call_target="tpu_custom_call" | custom-call | tf_op jit(solution)/shard_map/solve/pallas_call | solution.py:241
  89.1 18.9 %all_to_all.46.terms = f32[16,128,128]{2,1,0:T(8,128)S(1)} all-to-all(f32[16,128,128]{2,1,0:T(8,128)S(1)} %get-tuple-element.20), channel_id=1, replica_groups=mesh['z'=8,'core'=2,'x'=4,'y'=4] {'x','y'}, dimensions={0} | all-to-all | bytes 2097152 | tf_op jit(solution)/shard_map/all_to_all | solution.py:274
  108.0 3.5 %reduce-scatter.2.cloned.1.call-done = f32[384,128]{1,0:T(8,128)} async-done(((f32[3072,128]{1,0:T(8,128)}), f32[384,128]{1,0:T(8,128)}) %reduce-scatter.2.cloned.1.call-update) | async-done | bytes 196624 | tf_op jit(solution)/shard_map/reduce_scatter | solution.py:304
  112.5 22.6 %all_to_all.47.refs_0_ = f32[16,128,128]{2,1,0:T(8,128)S(1)} all-to-all(f32[16,128,128]{2,1,0:T(8,128)S(1)} %subtract.3), channel_id=1, replica_groups=mesh['z'=8,'core'=2,'x'=4,'y'=4] {'x','y'}, dimensions={0} | all-to-all | bytes 2097152 | tf_op jit(solution)/shard_map/all_to_all | solution.py:274
  135.1 2.6 %solve.5 = (f32[128,128]{1,0:T(8,128)S(1)}, f32[16,128,128]{2,1,0:T(8,128)S(1)}) custom-call(f32[16,128,128]{2,1,0:T(8,128)S(1)} %all_to_all.47.refs_0_, f32[4,128,2048]{2,1,0:T(8,128)} %refs_1_.7, f32[5,2048,128]{2,1,0:T(8,128)} %all-gather.5.cloned.1.call-done.refs_2_.refs_3_.refs_4_, f32[5,2048,128]{2,1,0:T(8,128)} %all-gather.5.cloned.1.call-done.refs_2_.refs_3_.refs_4_, ...), custom_call_target="tpu_custom_call" | custom-call | tf_op jit(solution)/shard_map/solve/pallas_call | solution.py:241
  137.7 19.1 %all_to_all.48.terms = f32[16,128,128]{2,1,0:T(8,128)S(1)} all-to-all(f32[16,128,128]{2,1,0:T(8,128)S(1)} %get-tuple-element.22), channel_id=1, replica_groups=mesh['z'=8,'core'=2,'x'=4,'y'=4] {'x','y'}, dimensions={0} | all-to-all | bytes 2097152 | tf_op jit(solution)/shard_map/all_to_all | solution.py:274
  157.8 17.9 %all_to_all.49.refs_0_ = f32[16,128,128]{2,1,0:T(8,128)S(1)} all-to-all(f32[16,128,128]{2,1,0:T(8,128)S(1)} %subtract.4), channel_id=1, replica_groups=mesh['z'=8,'core'=2,'x'=4,'y'=4] {'x','y'}, dimensions={0} | all-to-all | bytes 2097152 | tf_op jit(solution)/shard_map/all_to_all | solution.py:274
  175.7 3.2 %solve.6 = (f32[128,128]{1,0:T(8,128)S(1)}, f32[16,128,128]{2,1,0:T(8,128)S(1)}) custom-call(f32[16,128,128]{2,1,0:T(8,128)S(1)} %all_to_all.49.refs_0_, f32[4,128,2048]{2,1,0:T(8,128)} %refs_1_.7, f32[5,2048,128]{2,1,0:T(8,128)} %all-gather.5.cloned.1.call-done.refs_2_.refs_3_.refs_4_, f32[5,2048,128]{2,1,0:T(8,128)} %all-gather.5.cloned.1.call-done.refs_2_.refs_3_.refs_4_, ...), custom_call_target="tpu_custom_call" | custom-call | tf_op jit(solution)/shard_map/solve/pallas_call | solution.py:241
  178.9 16.6 %all_to_all.50.terms = f32[16,128,128]{2,1,0:T(8,128)S(1)} all-to-all(f32[16,128,128]{2,1,0:T(8,128)S(1)} %get-tuple-element.24), channel_id=1, replica_groups=mesh['z'=8,'core'=2,'x'=4,'y'=4] {'x','y'}, dimensions={0} | all-to-all | bytes 2097152 | tf_op jit(solution)/shard_map/all_to_all | solution.py:274
  195.5 2.0 subtract.5
  197.5 5.0 %all-to-all-start.8 = ((f32[16,128,128]{2,1,0:T(8,128)}), f32[16,128,128]{2,1,0:T(8,128)S(1)}, u32[]{:S(2)}, u32[]{:S(2)}) async-start(f32[16,128,128]{2,1,0:T(8,128)} %subtract.5), calls=%async_computation.9 | async-start | bytes 2097152 | tf_op jit(solution)/shard_map/all_to_all | solution.py:274
  203.3 10.9 %all-to-all-done.8.refs_0_ = f32[16,128,128]{2,1,0:T(8,128)S(1)} async-done(((f32[16,128,128]{2,1,0:T(8,128)}), f32[16,128,128]{2,1,0:T(8,128)S(1)}, u32[]{:S(2)}, u32[]{:S(2)}) %all-to-all-start.8) | async-done | bytes 1048608 | tf_op jit(solution)/shard_map/all_to_all | solution.py:274
  214.2 2.4 %solve.7 = f32[4,128,128]{2,1,0:T(8,128)} custom-call(f32[16,128,128]{2,1,0:T(8,128)S(1)} %all-to-all-done.8.refs_0_, f32[4,128,2048]{2,1,0:T(8,128)} %refs_1_.7, f32[128,128]{1,0:T(8,128)S(1)} %get-tuple-element.21.refs_4_.refs_5_.refs_2_, f32[128,128]{1,0:T(8,128)S(1)} %get-tuple-element.23.refs_6_.refs_3_, f32[128,128]{1,0:T(8,128)S(1)} %get-tuple-element.25.refs_4_), custom_call_target="tpu_custom_call" | custom-call | tf_op jit(solution)/shard_map/solve/pallas_call | solution.py:241
  (33 shorter events, 8.6 us)
Async XLA Ops:
  8.0 13.3 %copy-start.2 = (f32[512,4,128]{2,1,0:T(4,128)S(1)}, f32[512,4,128]{2,1,0:T(4,128)}, u32[]{:S(2)}) copy-start(f32[512,4,128]{2,1,0:T(4,128)} %param.7) | copy-start | bytes 3145732
  8.0 62.2 %all-gather.3.cloned.1.call-start = ((), (), s32[]{:S(2)}) async-start(), calls=%async_computation.11 | async-start | bytes 1114112 | tf_op jit(solution)/shard_map/all_gather | solution.py:284
  11.0 16.2 %all-to-all-start = ((s32[16,2,128]{2,1,0:T(2,128)}), s32[16,2,128]{2,1,0:T(2,128)S(1)}, u32[]{:S(2)}, u32[]{:S(2)}) async-start(s32[16,2,128]{2,1,0:T(2,128)} %pair.1), calls=%async_computation | async-start | bytes 32768 | tf_op jit(solution)/shard_map/all_to_all | solution.py:289
  19.5 92.0 %reduce-scatter.2.cloned.1.call-start = ((), (), s32[]{:S(2)}) async-start(), calls=%async_computation.10 | async-start | bytes 1769472 | tf_op jit(solution)/shard_map/reduce_scatter | solution.py:304
  30.5 2.0 collective-permute-start
  37.5 22.2 %collective-permute-start.1 = (f32[8,384,128]{2,1,0:T(8,128)S(1)}, f32[8,384,128]{2,1,0:T(8,128)S(1)}, u32[]{:S(2)}, u32[]{:S(2)}) collective-permute-start(f32[8,384,128]{2,1,0:T(8,128)S(1)} %get-tuple-element.18), channel_id=1, source_target_pairs={{0,16},{16,0},{1,17},{17,1},{2,18},{18,2},{3,19},{19,3},{4,20},{20... | collective-permute-start | bytes 4718600 | tf_op jit(solution)/shard_map/ppermute | solution.py:303
  61.0 1.0 copy-start
  61.1 74.0 %all-gather.5.cloned.1.call-start = ((), (), s32[]{:S(2)}) async-start(), calls=%async_computation.12 | async-start | bytes 5570560 | tf_op jit(solution)/shard_map/all_gather | solution.py:284
  62.8 24.0 %all-to-all-start.2 = ((f32[16,128,128]{2,1,0:T(8,128)}), f32[16,128,128]{2,1,0:T(8,128)S(1)}, u32[]{:S(2)}, u32[]{:S(2)}) async-start(f32[16,128,128]{2,1,0:T(8,128)} %get-tuple-element.19), calls=%async_computation.3 | async-start | bytes 2097152 | tf_op jit(solution)/shard_map/all_to_all | solution.py:274
  197.5 5.1 %copy-start.1 = (f32[384,128]{1,0:T(8,128)S(1)}, f32[384,128]{1,0:T(8,128)}, u32[]{:S(2)}) copy-start(f32[384,128]{1,0:T(8,128)} %reduce-scatter.2.cloned.1.call-done) | copy-start | bytes 589828
  197.5 16.7 %all-to-all-start.8 = ((f32[16,128,128]{2,1,0:T(8,128)}), f32[16,128,128]{2,1,0:T(8,128)S(1)}, u32[]{:S(2)}, u32[]{:S(2)}) async-start(f32[16,128,128]{2,1,0:T(8,128)} %subtract.5), calls=%async_computation.9 | async-start | bytes 2097152 | tf_op jit(solution)/shard_map/all_to_all | solution.py:274
Sparse Core Ops, SparseCore 0:
  11.2 43.1 all-gather.2
  63.8 50.9 all-gather.4
Sparse Core Ops, SparseCore 1:
  61.2 50.3 reduce-scatter.1

commit v7 on v6

--- a/solution.py
+++ b/solution.py
@@ -164,21 +164,6 @@
         compiler_params=PARAMS,
         name="pair",
     )(in_hbm(sire), in_hbm(dam), after)
-
-
-def add_kernel(one, other, after, out):
-    out[...] = one[...] + other[...]
-
-
-def add(one, other, after):
-    return pl.pallas_call(
-        add_kernel,
-        out_shape=jax.ShapeDtypeStruct(one.shape, F32),
-        in_specs=[VMEM, VMEM, pl.BlockSpec(memory_space=pl.ANY)],
-        out_specs=VMEM,
-        compiler_params=PARAMS,
-        name="add",
-    )(one, other, after)
 
 
 def solve_kernel(target, last, places, *refs):
@@ -300,7 +285,7 @@
     rest = gathered(hold(factor_blocks, relation0))
 
     keep, give = select(blocks - 1, here, index, rows_of(1, blocks - 1), first_terms)
-    terms = add(keep, lax.ppermute(give, "core", swap), relation0)
+    terms = keep + lax.ppermute(give, "core", swap)
     later = lax.psum_scatter(terms.reshape(-1, SIDE), "z", scatter_dimension=0, tiled=True)
     later = later.reshape(blocks - 1, SIDE, SIDE)
 

time: 225 us -> 218 us (0.969)
  blocking collectives: 116 us -> 110 us
    all_to_all x5, blocking collectives: 95.2 us -> 86.2 us  [to_group(): return lax.all_to_all(parts, COL, 0, 0)]
    reduce_scatter x1, waiting for transfers between devices: 3.51 us -> 0.01 us  [per_device(): lax.psum_scatter(terms.reshape(-1, SIDE), 'z', scatter_dimension=0, tiled...]
    ppermute x1, waiting for transfers between devices: 0.01 us -> 3.27 us  [per_device(): terms = keep + lax.ppermute(give, 'core', swap)]
    all_to_all x1, blocking collectives: 20.8 us -> 23.6 us  [per_device(): relation0, copies = spread_first(lax.all_to_all(first_terms, 'z', 0, 0))]
  transfers between devices with their start and end apart: 8 -> 8, of which waited for: 5 -> 5; matrix products, arithmetic and copies ran while one was open for 1% -> 2% of each run, Pallas kernels for 7% -> 7%
where the time goes in v7:
time: 218 us; the launch traced here: 217 us
  blocking collectives  110 us (50%)
  waiting for transfers between devices  37.6 us (17%)
  Pallas kernels  27.3 us (13%)
  starting transfers between devices  21.7 us (10%)
  between operations  15.7 us (7%)
  other arithmetic  2.57 us (1%)
    all_to_all x5, blocking collectives, to_group(): return lax.all_to_all(parts, COL, 0, 0)  86.2 us
    all_to_all x2, waiting for transfers between devices, to_group(): return lax.all_to_all(parts, COL, 0, 0)  27.5 us
    all_to_all x1, blocking collectives, per_device(): relation0, copies = spread_first(lax.all_to_all(first_terms, 'z', 0, 0))  23.6 us
    all_to_all x2, starting transfers between devices, to_group(): return lax.all_to_all(parts, COL, 0, 0)  12.5 us
    pallas_call x4, Pallas kernels, solve(): pl.pallas_call(functools.partial(solve_kernel, target, last, tuple((block...  10.4 us
    all_to_all x1, starting transfers between devices, per_device(): lax.all_to_all(pair_copies(sire_index[None], dam_index[None], first), ROW...  8.58 us
    pallas_call x2, Pallas kernels, select(): pl.pallas_call(functools.partial(select_kernel, count), out_shape=(shape,...  8.27 us
    all_to_all x1, waiting for transfers between devices, per_device(): lax.all_to_all(pair_copies(sire_index[None], dam_index[None], first), ROW...  5.24 us
  transfers between devices with their start and end apart: 8, of which 5 were waited for; matrix products, arithmetic and copies ran while one was open for 2% of the time, Pallas kernels for 7%

profile of v7, /device:TPU:8, one launch (start us, length us, event | category | flops | bytes accessed | tf_op | source)
XLA Modules:
  0.0 216.8 jit_solution(17566426515711346943)
XLA Ops:
  8.1 1.6 first_block.1.after
  11.0 8.6 %all-to-all-start = ((s32[16,2,128]{2,1,0:T(2,128)}), s32[16,2,128]{2,1,0:T(2,128)S(1)}, u32[]{:S(2)}, u32[]{:S(2)}) async-start(s32[16,2,128]{2,1,0:T(2,128)} %pair.1), calls=%async_computation | async-start | bytes 32768 | tf_op jit(solution)/shard_map/all_to_all | solution.py:274
  19.6 1.4 slice.6
  21.9 5.2 %all-to-all-done.index = s32[16,2,128]{2,1,0:T(2,128)S(1)} async-done(((s32[16,2,128]{2,1,0:T(2,128)}), s32[16,2,128]{2,1,0:T(2,128)S(1)}, u32[]{:S(2)}, u32[]{:S(2)}) %all-to-all-start) | async-done | bytes 16416 | tf_op jit(solution)/shard_map/all_to_all | solution.py:274
  27.2 3.3 %select.2 = (f32[8,128,128]{2,1,0:T(8,128)S(1)}, f32[8,128,128]{2,1,0:T(8,128)S(1)}) custom-call(s32[4]{0:T(128)S(1)} %pad_add_fusion.here.after, s32[16,2,128]{2,1,0:T(2,128)S(1)} %all-to-all-done.index, bf16[384,512]{1,0:T(8,128)(2,1)S(1)} %pad_maximum_fusion.1.rows, s32[4]{0:T(128)S(1)} %pad_add_fusion.here.after), custom_call_target="tpu_custom_call" | custom-call | flops 805306368 | bytes 1048576 | tf_op jit(solution)/shard_map/select/pallas_call | solution.py:59
  31.0 1.5 collective-permute-done
  32.6 4.9 %select.3 = (f32[8,384,128]{2,1,0:T(8,128)S(1)}, f32[8,384,128]{2,1,0:T(8,128)S(1)}) custom-call(s32[4]{0:T(128)S(1)} %pad_add_fusion.here.after, s32[16,2,128]{2,1,0:T(2,128)S(1)} %all-to-all-done.index, bf16[1152,512]{1,0:T(8,128)(2,1)S(1)} %pad_maximum_fusion.rows, f32[8,128,128]{2,1,0:T(8,128)S(1)} %add.12.after), custom_call_target="tpu_custom_call" | custom-call | flops 2415919104 | bytes 3145728 | tf_op jit(solution)/shard_map/select/pallas_call | solution.py:59
  37.7 3.3 %collective-permute-done.1 = f32[8,384,128]{2,1,0:T(8,128)S(1)} collective-permute-done((f32[8,384,128]{2,1,0:T(8,128)S(1)}, f32[8,384,128]{2,1,0:T(8,128)S(1)}, u32[]{:S(2)}, u32[]{:S(2)}) %collective-permute-start.1) | collective-permute-done | bytes 1572896 | tf_op jit(solution)/shard_map/ppermute | solution.py:288
  41.0 1.4 add.13
  42.5 23.6 %all_to_all.45.terms = f32[8,128,128]{2,1,0:T(8,128)S(1)} all-to-all(f32[8,128,128]{2,1,0:T(8,128)S(1)} %add.12.after), channel_id=1, replica_groups=mesh['z'=8,'core'=2,'x'=4,'y'=4] {'z'}, dimensions={0} | all-to-all | bytes 1048576 | tf_op jit(solution)/shard_map/all_to_all | solution.py:282
  68.0 7.5 %all-to-all-start.2 = ((f32[16,128,128]{2,1,0:T(8,128)}), f32[16,128,128]{2,1,0:T(8,128)S(1)}, u32[]{:S(2)}, u32[]{:S(2)}) async-start(f32[16,128,128]{2,1,0:T(8,128)} %get-tuple-element.19), calls=%async_computation.3 | async-start | bytes 2097152 | tf_op jit(solution)/shard_map/all_to_all | solution.py:259
  75.5 16.6 %all-to-all-done.2.refs_0_ = f32[16,128,128]{2,1,0:T(8,128)S(1)} async-done(((f32[16,128,128]{2,1,0:T(8,128)}), f32[16,128,128]{2,1,0:T(8,128)S(1)}, u32[]{:S(2)}, u32[]{:S(2)}) %all-to-all-start.2) | async-done | bytes 1048608 | tf_op jit(solution)/shard_map/all_to_all | solution.py:259
  92.1 2.3 %solve.4 = (f32[128,128]{1,0:T(8,128)S(1)}, f32[16,128,128]{2,1,0:T(8,128)S(1)}) custom-call(f32[16,128,128]{2,1,0:T(8,128)S(1)} %all-to-all-done.2.refs_0_, f32[4,128,2048]{2,1,0:T(8,128)} %refs_1_.7, f32[1,2048,128]{2,1,0:T(8,128)} %all-gather.3.cloned.1.call-done.refs_2_), custom_call_target="tpu_custom_call" | custom-call | tf_op jit(solution)/shard_map/solve/pallas_call | solution.py:226
  94.4 19.0 %all_to_all.46.terms = f32[16,128,128]{2,1,0:T(8,128)S(1)} all-to-all(f32[16,128,128]{2,1,0:T(8,128)S(1)} %get-tuple-element.20), channel_id=1, replica_groups=mesh['z'=8,'core'=2,'x'=4,'y'=4] {'x','y'}, dimensions={0} | all-to-all | bytes 2097152 | tf_op jit(solution)/shard_map/all_to_all | solution.py:259
  114.3 18.1 %all_to_all.47.refs_0_ = f32[16,128,128]{2,1,0:T(8,128)S(1)} all-to-all(f32[16,128,128]{2,1,0:T(8,128)S(1)} %subtract.3), channel_id=1, replica_groups=mesh['z'=8,'core'=2,'x'=4,'y'=4] {'x','y'}, dimensions={0} | all-to-all | bytes 2097152 | tf_op jit(solution)/shard_map/all_to_all | solution.py:259
  132.4 2.6 %solve.5 = (f32[128,128]{1,0:T(8,128)S(1)}, f32[16,128,128]{2,1,0:T(8,128)S(1)}) custom-call(f32[16,128,128]{2,1,0:T(8,128)S(1)} %all_to_all.47.refs_0_, f32[4,128,2048]{2,1,0:T(8,128)} %refs_1_.7, f32[5,2048,128]{2,1,0:T(8,128)} %all-gather.5.cloned.1.call-done.refs_2_.refs_3_.refs_4_, f32[5,2048,128]{2,1,0:T(8,128)} %all-gather.5.cloned.1.call-done.refs_2_.refs_3_.refs_4_, ...), custom_call_target="tpu_custom_call" | custom-call | tf_op jit(solution)/shard_map/solve/pallas_call | solution.py:226
  135.0 16.8 %all_to_all.48.terms = f32[16,128,128]{2,1,0:T(8,128)S(1)} all-to-all(f32[16,128,128]{2,1,0:T(8,128)S(1)} %get-tuple-element.22), channel_id=1, replica_groups=mesh['z'=8,'core'=2,'x'=4,'y'=4] {'x','y'}, dimensions={0} | all-to-all | bytes 2097152 | tf_op jit(solution)/shard_map/all_to_all | solution.py:259
  152.8 16.2 %all_to_all.49.refs_0_ = f32[16,128,128]{2,1,0:T(8,128)S(1)} all-to-all(f32[16,128,128]{2,1,0:T(8,128)S(1)} %subtract.4), channel_id=1, replica_groups=mesh['z'=8,'core'=2,'x'=4,'y'=4] {'x','y'}, dimensions={0} | all-to-all | bytes 2097152 | tf_op jit(solution)/shard_map/all_to_all | solution.py:259
  168.9 3.2 %solve.6 = (f32[128,128]{1,0:T(8,128)S(1)}, f32[16,128,128]{2,1,0:T(8,128)S(1)}) custom-call(f32[16,128,128]{2,1,0:T(8,128)S(1)} %all_to_all.49.refs_0_, f32[4,128,2048]{2,1,0:T(8,128)} %refs_1_.7, f32[5,2048,128]{2,1,0:T(8,128)} %all-gather.5.cloned.1.call-done.refs_2_.refs_3_.refs_4_, f32[5,2048,128]{2,1,0:T(8,128)} %all-gather.5.cloned.1.call-done.refs_2_.refs_3_.refs_4_, ...), custom_call_target="tpu_custom_call" | custom-call | tf_op jit(solution)/shard_map/solve/pallas_call | solution.py:226
  172.1 16.2 %all_to_all.50.terms = f32[16,128,128]{2,1,0:T(8,128)S(1)} all-to-all(f32[16,128,128]{2,1,0:T(8,128)S(1)} %get-tuple-element.24), channel_id=1, replica_groups=mesh['z'=8,'core'=2,'x'=4,'y'=4] {'x','y'}, dimensions={0} | all-to-all | bytes 2097152 | tf_op jit(solution)/shard_map/all_to_all | solution.py:259
  188.3 2.0 subtract.5
  190.2 5.0 %all-to-all-start.8 = ((f32[16,128,128]{2,1,0:T(8,128)}), f32[16,128,128]{2,1,0:T(8,128)S(1)}, u32[]{:S(2)}, u32[]{:S(2)}) async-start(f32[16,128,128]{2,1,0:T(8,128)} %subtract.5), calls=%async_computation.9 | async-start | bytes 2097152 | tf_op jit(solution)/shard_map/all_to_all | solution.py:259
  196.0 10.9 %all-to-all-done.8.refs_0_ = f32[16,128,128]{2,1,0:T(8,128)S(1)} async-done(((f32[16,128,128]{2,1,0:T(8,128)}), f32[16,128,128]{2,1,0:T(8,128)S(1)}, u32[]{:S(2)}, u32[]{:S(2)}) %all-to-all-start.8) | async-done | bytes 1048608 | tf_op jit(solution)/shard_map/all_to_all | solution.py:259
  206.9 2.4 %solve.7 = f32[4,128,128]{2,1,0:T(8,128)} custom-call(f32[16,128,128]{2,1,0:T(8,128)S(1)} %all-to-all-done.8.refs_0_, f32[4,128,2048]{2,1,0:T(8,128)} %refs_1_.7, f32[128,128]{1,0:T(8,128)S(1)} %get-tuple-element.21.refs_4_.refs_5_.refs_2_, f32[128,128]{1,0:T(8,128)S(1)} %get-tuple-element.23.refs_6_.refs_3_, f32[128,128]{1,0:T(8,128)S(1)} %get-tuple-element.25.refs_4_), custom_call_target="tpu_custom_call" | custom-call | tf_op jit(solution)/shard_map/solve/pallas_call | solution.py:226
  (33 shorter events, 7.7 us)
Async XLA Ops:
  8.0 13.3 %copy-start.2 = (f32[512,4,128]{2,1,0:T(4,128)S(1)}, f32[512,4,128]{2,1,0:T(4,128)}, u32[]{:S(2)}) copy-start(f32[512,4,128]{2,1,0:T(4,128)} %param.7) | copy-start | bytes 3145732
  8.0 67.5 %all-gather.3.cloned.1.call-start = ((), (), s32[]{:S(2)}) async-start(), calls=%async_computation.11 | async-start | bytes 1114112 | tf_op jit(solution)/shard_map/all_gather | solution.py:269
  11.0 16.2 %all-to-all-start = ((s32[16,2,128]{2,1,0:T(2,128)}), s32[16,2,128]{2,1,0:T(2,128)S(1)}, u32[]{:S(2)}, u32[]{:S(2)}) async-start(s32[16,2,128]{2,1,0:T(2,128)} %pair.1), calls=%async_computation | async-start | bytes 32768 | tf_op jit(solution)/shard_map/all_to_all | solution.py:274
  19.5 93.8 %reduce-scatter.2.cloned.1.call-start = ((), (), s32[]{:S(2)}) async-start(), calls=%async_computation.10 | async-start | bytes 1769472 | tf_op jit(solution)/shard_map/reduce_scatter | solution.py:289
  30.5 2.0 collective-permute-start
  37.5 3.5 %collective-permute-start.1 = (f32[8,384,128]{2,1,0:T(8,128)S(1)}, f32[8,384,128]{2,1,0:T(8,128)S(1)}, u32[]{:S(2)}, u32[]{:S(2)}) collective-permute-start(f32[8,384,128]{2,1,0:T(8,128)S(1)} %get-tuple-element.18), channel_id=1, source_target_pairs={{0,16},{16,0},{1,17},{17,1},{2,18},{18,2},{3,19},{19,3},{4,20},{20... | collective-permute-start | bytes 4718600 | tf_op jit(solution)/shard_map/ppermute | solution.py:288
  42.4 24.8 %copy-start = (f32[6,128,128]{2,1,0:T(8,128)S(1)}, f32[6,128,128]{2,1,0:T(8,128)}, u32[]{:S(2)}) copy-start(f32[6,128,128]{2,1,0:T(8,128)} %blocks.3) | copy-start | bytes 1179652
  42.4 90.0 %all-gather.5.cloned.1.call-start = ((), (), s32[]{:S(2)}) async-start(), calls=%async_computation.12 | async-start | bytes 5570560 | tf_op jit(solution)/shard_map/all_gather | solution.py:269
  68.0 24.1 %all-to-all-start.2 = ((f32[16,128,128]{2,1,0:T(8,128)}), f32[16,128,128]{2,1,0:T(8,128)S(1)}, u32[]{:S(2)}, u32[]{:S(2)}) async-start(f32[16,128,128]{2,1,0:T(8,128)} %get-tuple-element.19), calls=%async_computation.3 | async-start | bytes 2097152 | tf_op jit(solution)/shard_map/all_to_all | solution.py:259
  190.2 5.1 %copy-start.1 = (f32[384,128]{1,0:T(8,128)S(1)}, f32[384,128]{1,0:T(8,128)}, u32[]{:S(2)}) copy-start(f32[384,128]{1,0:T(8,128)} %reduce-scatter.2.cloned.1.call-done) | copy-start | bytes 589828
  190.2 16.7 %all-to-all-start.8 = ((f32[16,128,128]{2,1,0:T(8,128)}), f32[16,128,128]{2,1,0:T(8,128)S(1)}, u32[]{:S(2)}, u32[]{:S(2)}) async-start(f32[16,128,128]{2,1,0:T(8,128)} %subtract.5), calls=%async_computation.9 | async-start | bytes 2097152 | tf_op jit(solution)/shard_map/all_to_all | solution.py:259
Sparse Core Ops, SparseCore 0:
  11.2 42.2 all-gather.2
  68.1 42.3 all-gather.4
Sparse Core Ops, SparseCore 1:
  42.5 44.3 reduce-scatter.1

commit v8 on v3

--- a/solution.py
+++ b/solution.py
@@ -70,13 +70,18 @@
 
 def remain_kernel(block, *refs):
     terms = refs[0]
+    if block is not None:
+        held, sem = refs[3:]
+        fetch = pltpu.make_async_copy(refs[1].at[block], held, sem.at[0])
+        fetch.start()
     total = terms[0]
     for part in range(1, terms.shape[0]):
         total += terms[part]
     if block is None:
         refs[1][...] = total
     else:
-        total = refs[1][block] - total
+        fetch.wait()
+        total = held[...] - total
     for owner in range(GROUP):
         refs[2][owner] = total
 
@@ -95,11 +100,12 @@
     return pl.pallas_call(
         functools.partial(remain_kernel, block),
         out_shape=copies,
-        in_specs=[VMEM, VMEM],
+        in_specs=[VMEM, pl.BlockSpec(memory_space=pltpu.HBM)],
         out_specs=VMEM,
+        scratch_shapes=[pltpu.VMEM((SIDE, SIDE), F32), pltpu.SemaphoreType.DMA((1,))],
         compiler_params=PARAMS,
         name="subtract",
-    )(terms, minuend)
+    )(terms, pltpu.with_memory_space_constraint(minuend, pltpu.HBM))
 
 
 def solve_kernel(target, last, places, *refs):

time: 214 us -> 216 us (level)
  Pallas kernels: 22 us -> 24.5 us
    pallas_call x3, Pallas kernels: 1.38 us -> 3.85 us  [spread(): pl.pallas_call(functools.partial(remain_kernel, block), out_shape=copies,...]
where the time goes in v8:
time: 216 us; the launch traced here: 215 us
  blocking collectives  110 us (51%)
  waiting for transfers between devices  35.8 us (17%)
  Pallas kernels  24.5 us (11%)
  starting transfers between devices  21.8 us (10%)
  between operations  15.7 us (7%)
  local copies, waits for them, and re-layouts  4.21 us (2%)
  other arithmetic  3.34 us (2%)
    all_to_all x5, blocking collectives, to_group(): return lax.all_to_all(parts, COL, 0, 0)  85.7 us
    all_to_all x2, waiting for transfers between devices, to_group(): return lax.all_to_all(parts, COL, 0, 0)  27.2 us
    all_to_all x1, blocking collectives, per_device(): relation0, copies = spread(lax.all_to_all(first_terms, 'z', 0, 0))  24 us
    all_to_all x2, starting transfers between devices, to_group(): return lax.all_to_all(parts, COL, 0, 0)  12.6 us
    pallas_call x4, Pallas kernels, solve(): pl.pallas_call(functools.partial(solve_kernel, target, last, tuple((block...  10.4 us
    all_to_all x1, starting transfers between devices, per_device(): lax.all_to_all(jnp.broadcast_to(pair[None], (GROUP, 2, SIDE)), ROW, 0, 0)  8.57 us
    pallas_call x2, Pallas kernels, select(): pl.pallas_call(functools.partial(select_kernel, count), out_shape=(shape,...  8.27 us
  transfers between devices with their start and end apart: 8, of which 5 were waited for; matrix products, arithmetic and copies ran while one was open for 3% of the time, Pallas kernels for 6%

profile of v8, /device:TPU:8, one launch (start us, length us, event | category | flops | bytes accessed | tf_op | source)
XLA Modules:
  0.0 214.9 jit_solution(17864862327431804541)
XLA Ops:
  9.4 8.6 %all-to-all-start = ((s32[16,2,128]{2,1,0:T(2,128)}), s32[16,2,128]{2,1,0:T(2,128)S(1)}, u32[]{:S(2)}, u32[]{:S(2)}) async-start(s32[16,2,128]{2,1,0:T(2,128)} %broadcast_in_dim.4), calls=%async_computation | async-start | bytes 32768 | tf_op jit(solution)/shard_map/all_to_all | solution.py:217
  18.0 1.5 slice.11
  19.6 1.4 slice.9
  21.9 3.7 %all-to-all-done.index = s32[16,2,128]{2,1,0:T(2,128)S(1)} async-done(((s32[16,2,128]{2,1,0:T(2,128)}), s32[16,2,128]{2,1,0:T(2,128)S(1)}, u32[]{:S(2)}, u32[]{:S(2)}) %all-to-all-start) | async-done | bytes 16416 | tf_op jit(solution)/shard_map/all_to_all | solution.py:217
  25.6 3.3 %select.2 = (f32[8,128,128]{2,1,0:T(8,128)S(1)}, f32[8,128,128]{2,1,0:T(8,128)S(1)}) custom-call(s32[4]{0:T(128)S(1)} %pad_add_fusion.1.here.after, s32[16,2,128]{2,1,0:T(2,128)S(1)} %all-to-all-done.index, bf16[384,512]{1,0:T(8,128)(2,1)S(1)} %pad_maximum_fusion.1.rows, s32[4]{0:T(128)S(1)} %pad_add_fusion.1.here.after), custom_call_target="tpu_custom_call" | custom-call | flops 805306368 | bytes 1048576 | tf_op jit(solution)/shard_map/select/pallas_call | solution.py:58
  29.4 1.5 collective-permute-done
  31.0 4.9 %select.3 = (f32[8,384,128]{2,1,0:T(8,128)S(1)}, f32[8,384,128]{2,1,0:T(8,128)S(1)}) custom-call(s32[4]{0:T(128)S(1)} %pad_add_fusion.1.here.after, s32[16,2,128]{2,1,0:T(2,128)S(1)} %all-to-all-done.index, bf16[1152,512]{1,0:T(8,128)(2,1)S(1)} %pad_maximum_fusion.rows, f32[8,128,128]{2,1,0:T(8,128)S(1)} %add.12.after), custom_call_target="tpu_custom_call" | custom-call | flops 2415919104 | bytes 3145728 | tf_op jit(solution)/shard_map/select/pallas_call | solution.py:58
  36.2 3.3 %collective-permute-done.1 = f32[8,384,128]{2,1,0:T(8,128)S(1)} collective-permute-done((f32[8,384,128]{2,1,0:T(8,128)S(1)}, f32[8,384,128]{2,1,0:T(8,128)S(1)}, u32[]{:S(2)}, u32[]{:S(2)}) %collective-permute-start.1) | collective-permute-done | bytes 1572896 | tf_op jit(solution)/shard_map/ppermute | solution.py:230
  39.4 1.4 add.13
  40.9 24.0 %all_to_all.45.refs_0_ = f32[8,128,128]{2,1,0:T(8,128)S(1)} all-to-all(f32[8,128,128]{2,1,0:T(8,128)S(1)} %add.12.after), channel_id=1, replica_groups=mesh['z'=8,'core'=2,'x'=4,'y'=4] {'z'}, dimensions={0} | all-to-all | bytes 1048576 | tf_op jit(solution)/shard_map/all_to_all | solution.py:225
  66.8 7.6 %all-to-all-start.2 = ((f32[16,128,128]{2,1,0:T(8,128)}), f32[16,128,128]{2,1,0:T(8,128)S(1)}, u32[]{:S(2)}, u32[]{:S(2)}) async-start(f32[16,128,128]{2,1,0:T(8,128)} %get-tuple-element.19), calls=%async_computation.3 | async-start | bytes 2097152 | tf_op jit(solution)/shard_map/all_to_all | solution.py:201
  74.5 16.3 %all-to-all-done.2.refs_0_ = f32[16,128,128]{2,1,0:T(8,128)S(1)} async-done(((f32[16,128,128]{2,1,0:T(8,128)}), f32[16,128,128]{2,1,0:T(8,128)S(1)}, u32[]{:S(2)}, u32[]{:S(2)}) %all-to-all-start.2) | async-done | bytes 1048608 | tf_op jit(solution)/shard_map/all_to_all | solution.py:201
  90.8 2.3 %solve.4 = (f32[128,128]{1,0:T(8,128)S(1)}, f32[16,128,128]{2,1,0:T(8,128)S(1)}) custom-call(f32[16,128,128]{2,1,0:T(8,128)S(1)} %all-to-all-done.2.refs_0_, f32[4,128,2048]{2,1,0:T(8,128)} %refs_1_.7, f32[1,2048,128]{2,1,0:T(8,128)} %all-gather.3.cloned.1.call-done.refs_2_), custom_call_target="tpu_custom_call" | custom-call | tf_op jit(solution)/shard_map/solve/pallas_call | solution.py:168
  93.1 18.7 %all_to_all.46.refs_0_ = f32[16,128,128]{2,1,0:T(8,128)S(1)} all-to-all(f32[16,128,128]{2,1,0:T(8,128)S(1)} %get-tuple-element.20), channel_id=1, replica_groups=mesh['z'=8,'core'=2,'x'=4,'y'=4] {'x','y'}, dimensions={0} | all-to-all | bytes 2097152 | tf_op jit(solution)/shard_map/all_to_all | solution.py:201
  112.8 18.0 %all_to_all.47.refs_0_ = f32[16,128,128]{2,1,0:T(8,128)S(1)} all-to-all(f32[16,128,128]{2,1,0:T(8,128)S(1)} %subtract.3), channel_id=1, replica_groups=mesh['z'=8,'core'=2,'x'=4,'y'=4] {'x','y'}, dimensions={0} | all-to-all | bytes 2097152 | tf_op jit(solution)/shard_map/all_to_all | solution.py:201
  130.7 2.6 %solve.5 = (f32[128,128]{1,0:T(8,128)S(1)}, f32[16,128,128]{2,1,0:T(8,128)S(1)}) custom-call(f32[16,128,128]{2,1,0:T(8,128)S(1)} %all_to_all.47.refs_0_, f32[4,128,2048]{2,1,0:T(8,128)} %refs_1_.7, f32[5,2048,128]{2,1,0:T(8,128)} %all-gather.5.cloned.1.call-done.refs_2_.refs_3_.refs_4_, f32[5,2048,128]{2,1,0:T(8,128)} %all-gather.5.cloned.1.call-done.refs_2_.refs_3_.refs_4_, ...), custom_call_target="tpu_custom_call" | custom-call | tf_op jit(solution)/shard_map/solve/pallas_call | solution.py:168
  133.3 16.7 %all_to_all.48.refs_0_ = f32[16,128,128]{2,1,0:T(8,128)S(1)} all-to-all(f32[16,128,128]{2,1,0:T(8,128)S(1)} %get-tuple-element.22), channel_id=1, replica_groups=mesh['z'=8,'core'=2,'x'=4,'y'=4] {'x','y'}, dimensions={0} | all-to-all | bytes 2097152 | tf_op jit(solution)/shard_map/all_to_all | solution.py:201
  150.9 16.2 %all_to_all.49.refs_0_ = f32[16,128,128]{2,1,0:T(8,128)S(1)} all-to-all(f32[16,128,128]{2,1,0:T(8,128)S(1)} %subtract.4), channel_id=1, replica_groups=mesh['z'=8,'core'=2,'x'=4,'y'=4] {'x','y'}, dimensions={0} | all-to-all | bytes 2097152 | tf_op jit(solution)/shard_map/all_to_all | solution.py:201
  167.1 3.2 %solve.6 = (f32[128,128]{1,0:T(8,128)S(1)}, f32[16,128,128]{2,1,0:T(8,128)S(1)}) custom-call(f32[16,128,128]{2,1,0:T(8,128)S(1)} %all_to_all.49.refs_0_, f32[4,128,2048]{2,1,0:T(8,128)} %refs_1_.7, f32[5,2048,128]{2,1,0:T(8,128)} %all-gather.5.cloned.1.call-done.refs_2_.refs_3_.refs_4_, f32[5,2048,128]{2,1,0:T(8,128)} %all-gather.5.cloned.1.call-done.refs_2_.refs_3_.refs_4_, ...), custom_call_target="tpu_custom_call" | custom-call | tf_op jit(solution)/shard_map/solve/pallas_call | solution.py:168
  170.3 16.2 %all_to_all.50.refs_0_ = f32[16,128,128]{2,1,0:T(8,128)S(1)} all-to-all(f32[16,128,128]{2,1,0:T(8,128)S(1)} %get-tuple-element.24), channel_id=1, replica_groups=mesh['z'=8,'core'=2,'x'=4,'y'=4] {'x','y'}, dimensions={0} | all-to-all | bytes 2097152 | tf_op jit(solution)/shard_map/all_to_all | solution.py:201
  186.4 2.0 subtract.5
  188.4 5.0 %all-to-all-start.8 = ((f32[16,128,128]{2,1,0:T(8,128)}), f32[16,128,128]{2,1,0:T(8,128)S(1)}, u32[]{:S(2)}, u32[]{:S(2)}) async-start(f32[16,128,128]{2,1,0:T(8,128)} %subtract.5), calls=%async_computation.9 | async-start | bytes 2097152 | tf_op jit(solution)/shard_map/all_to_all | solution.py:201
  194.2 10.9 %all-to-all-done.8.refs_0_ = f32[16,128,128]{2,1,0:T(8,128)S(1)} async-done(((f32[16,128,128]{2,1,0:T(8,128)}), f32[16,128,128]{2,1,0:T(8,128)S(1)}, u32[]{:S(2)}, u32[]{:S(2)}) %all-to-all-start.8) | async-done | bytes 1048608 | tf_op jit(solution)/shard_map/all_to_all | solution.py:201
  205.1 2.4 %solve.7 = f32[4,128,128]{2,1,0:T(8,128)} custom-call(f32[16,128,128]{2,1,0:T(8,128)S(1)} %all-to-all-done.8.refs_0_, f32[4,128,2048]{2,1,0:T(8,128)} %refs_1_.7, f32[128,128]{1,0:T(8,128)S(1)} %get-tuple-element.21.refs_4_.refs_5_.refs_2_, f32[128,128]{1,0:T(8,128)S(1)} %get-tuple-element.23.refs_6_.refs_3_, f32[128,128]{1,0:T(8,128)S(1)} %get-tuple-element.25.refs_4_), custom_call_target="tpu_custom_call" | custom-call | tf_op jit(solution)/shard_map/solve/pallas_call | solution.py:168
  (34 shorter events, 7.7 us)
Async XLA Ops:
  8.0 13.3 %copy-start.2 = (f32[512,4,128]{2,1,0:T(4,128)S(1)}, f32[512,4,128]{2,1,0:T(4,128)}, u32[]{:S(2)}) copy-start(f32[512,4,128]{2,1,0:T(4,128)} %param.7) | copy-start | bytes 3145732
  9.4 16.2 %all-to-all-start = ((s32[16,2,128]{2,1,0:T(2,128)}), s32[16,2,128]{2,1,0:T(2,128)S(1)}, u32[]{:S(2)}, u32[]{:S(2)}) async-start(s32[16,2,128]{2,1,0:T(2,128)} %broadcast_in_dim.4), calls=%async_computation | async-start | bytes 32768 | tf_op jit(solution)/shard_map/all_to_all | solution.py:217
  18.0 56.5 %all-gather.3.cloned.1.call-start = ((), (), s32[]{:S(2)}) async-start(), calls=%async_computation.11 | async-start | bytes 1114112 | tf_op jit(solution)/shard_map/all_gather | solution.py:211
  19.5 92.3 %reduce-scatter.2.cloned.1.call-start = ((), (), s32[]{:S(2)}) async-start(), calls=%async_computation.10 | async-start | bytes 1769472 | tf_op jit(solution)/shard_map/reduce_scatter | solution.py:231
  28.9 2.0 collective-permute-start
  36.0 3.5 %collective-permute-start.1 = (f32[8,384,128]{2,1,0:T(8,128)S(1)}, f32[8,384,128]{2,1,0:T(8,128)S(1)}, u32[]{:S(2)}, u32[]{:S(2)}) collective-permute-start(f32[8,384,128]{2,1,0:T(8,128)S(1)} %get-tuple-element.18), channel_id=1, source_target_pairs={{0,16},{16,0},{1,17},{17,1},{2,18},{18,2},{3,19},{19,3},{4,20},{20... | collective-permute-start | bytes 4718600 | tf_op jit(solution)/shard_map/ppermute | solution.py:230
  40.8 25.2 %copy-start = (f32[6,128,128]{2,1,0:T(8,128)S(1)}, f32[6,128,128]{2,1,0:T(8,128)}, u32[]{:S(2)}) copy-start(f32[6,128,128]{2,1,0:T(8,128)} %blocks.1) | copy-start | bytes 1179652
  40.8 89.9 %all-gather.5.cloned.1.call-start = ((), (), s32[]{:S(2)}) async-start(), calls=%async_computation.12 | async-start | bytes 5570560 | tf_op jit(solution)/shard_map/all_gather | solution.py:211
  66.8 23.9 %all-to-all-start.2 = ((f32[16,128,128]{2,1,0:T(8,128)}), f32[16,128,128]{2,1,0:T(8,128)S(1)}, u32[]{:S(2)}, u32[]{:S(2)}) async-start(f32[16,128,128]{2,1,0:T(8,128)} %get-tuple-element.19), calls=%async_computation.3 | async-start | bytes 2097152 | tf_op jit(solution)/shard_map/all_to_all | solution.py:201
  188.4 5.1 %copy-start.1 = (f32[384,128]{1,0:T(8,128)S(1)}, f32[384,128]{1,0:T(8,128)}, u32[]{:S(2)}) copy-start(f32[384,128]{1,0:T(8,128)} %reduce-scatter.2.cloned.1.call-done) | copy-start | bytes 589828
  188.4 16.7 %all-to-all-start.8 = ((f32[16,128,128]{2,1,0:T(8,128)}), f32[16,128,128]{2,1,0:T(8,128)S(1)}, u32[]{:S(2)}, u32[]{:S(2)}) async-start(f32[16,128,128]{2,1,0:T(8,128)} %subtract.5), calls=%async_computation.9 | async-start | bytes 2097152 | tf_op jit(solution)/shard_map/all_to_all | solution.py:201
Sparse Core Ops, SparseCore 0:
  21.2 46.5 all-gather.2
  69.6 44.0 all-gather.4
Sparse Core Ops, SparseCore 1:
  40.9 43.3 reduce-scatter.1

commit v9 on v3

--- a/solution.py
+++ b/solution.py
@@ -107,7 +107,8 @@
     count = 0 if last else target + 1
     factors = refs[2 : 2 + count]
     before = refs[2 + count : 2 + count + target]
-    solved = refs[2 + count + target]
+    extra = 2 if last else 0
+    solved = refs[2 + count + target + extra]
     held_inverse, held, sems = refs[-3:]
     fetch = pltpu.make_async_copy(inverse_ref.at[target], held_inverse, sems.at[0])
     fetch.start()
@@ -127,6 +128,8 @@
         for source in range(target):
             solved[source] = before[source][...]
         solved[target] = own
+        refs[-4][0] = refs[2 + target][...]
+        refs[-4][1:] = refs[3 + target][...]
         return
     solved[...] = own
     terms = refs[-4]
@@ -151,18 +154,19 @@
                 terms[pl.ds(part * 4, 4)] += term
 
 
-def solve(target, whole, inverses, factors, before):
+def solve(target, whole, inverses, factors, before, relation):
     last = target + 1 == inverses.shape[0]
     count = len(factors)
     one = jax.ShapeDtypeStruct((SIDE, SIDE), F32)
     out_shape = (one, jax.ShapeDtypeStruct((GROUP, SIDE, SIDE), F32))
     if last:
-        out_shape = (jax.ShapeDtypeStruct((target + 1, SIDE, SIDE), F32),)
+        before = [*before, *relation]
+        out_shape = (jax.ShapeDtypeStruct((target + 1, SIDE, SIDE), F32),) * 2
     hbm = pl.BlockSpec(memory_space=pltpu.HBM)
     out = pl.pallas_call(
         functools.partial(solve_kernel, target, last, tuple(block for _, block in factors)),
         out_shape=out_shape,
-        in_specs=[VMEM, hbm] + [hbm] * count + [VMEM] * target,
+        in_specs=[VMEM, hbm] + [hbm] * count + [VMEM] * len(before),
         out_specs=(VMEM,) * len(out_shape),
         scratch_shapes=[
             pltpu.VMEM((SIDE, GROUP * SIDE), F32),
@@ -172,7 +176,7 @@
         compiler_params=PARAMS,
         name="solve",
     )(whole, inverses, *[array for array, _ in factors], *before)
-    return (out[0], None) if last else out
+    return out
 
 
 def hold_kernel(blocks, after, out):
@@ -235,10 +239,9 @@
             factors = [(start, 0)]
         if target + 1 == blocks:
             factors = []
-        own, terms = solve(target, to_group(copies), inverses, factors, solved)
+        own, terms = solve(target, to_group(copies), inverses, factors, solved, (relation0, later))
         solved.append(own)
-    relationship = jnp.concatenate([relation0[None], later])
-    return relationship, solved[-1]
+    return terms, solved[-1]
 
 
 def solution(mesh):

time: 214 us -> 213 us (level)
  blocking collectives: 110 us -> 126 us
  waiting for transfers between devices: 35.8 us -> 24.9 us
  starting transfers between devices: 21.6 us -> 16.7 us
    all_to_all x5 -> x6, blocking collectives: 85.8 us -> 102 us  [to_group(): return lax.all_to_all(parts, COL, 0, 0)]
    all_to_all x2 -> x1, waiting for transfers between devices: 27.2 us -> 16.3 us  [to_group(): return lax.all_to_all(parts, COL, 0, 0)]
    all_to_all x2 -> x1, starting transfers between devices: 12.5 us -> 7.59 us  [to_group(): return lax.all_to_all(parts, COL, 0, 0)]
  transfers between devices with their start and end apart: 8 -> 7, of which waited for: 5 -> 4; matrix products, arithmetic and copies ran while one was open for 3% -> 3% of each run, Pallas kernels for 6% -> 6%
where the time goes in v9:
time: 213 us; the launch traced here: 212 us
  blocking collectives  126 us (59%)
  waiting for transfers between devices  24.9 us (12%)
  Pallas kernels  21 us (10%)
  starting transfers between devices  16.7 us (8%)
  between operations  15.7 us (7%)
  local copies, waits for them, and re-layouts  5.13 us (2%)
  other arithmetic  2.62 us (1%)
    all_to_all x6, blocking collectives, to_group(): return lax.all_to_all(parts, COL, 0, 0)  102 us
    all_to_all x1, blocking collectives, per_device(): relation0, copies = spread(lax.all_to_all(first_terms, 'z', 0, 0))  24 us
    all_to_all x1, waiting for transfers between devices, to_group(): return lax.all_to_all(parts, COL, 0, 0)  16.3 us
    pallas_call x4, Pallas kernels, solve(): pl.pallas_call(functools.partial(solve_kernel, target, last, tuple((block...  10.5 us
    all_to_all x1, starting transfers between devices, per_device(): lax.all_to_all(jnp.broadcast_to(pair[None], (GROUP, 2, SIDE)), ROW, 0, 0)  8.57 us
    pallas_call x2, Pallas kernels, select(): pl.pallas_call(functools.partial(select_kernel, count), out_shape=(shape,...  8.27 us
    all_to_all x1, starting transfers between devices, to_group(): return lax.all_to_all(parts, COL, 0, 0)  7.59 us
  transfers between devices with their start and end apart: 7, of which 4 were waited for; matrix products, arithmetic and copies ran while one was open for 3% of the time, Pallas kernels for 6%

profile of v9, /device:TPU:8, one launch (start us, length us, event | category | flops | bytes accessed | tf_op | source)
XLA Modules:
  0.0 212.0 jit_solution(17923837793062929409)
XLA Ops:
  9.4 8.6 %all-to-all-start = ((s32[16,2,128]{2,1,0:T(2,128)}), s32[16,2,128]{2,1,0:T(2,128)S(1)}, u32[]{:S(2)}, u32[]{:S(2)}) async-start(s32[16,2,128]{2,1,0:T(2,128)} %broadcast_in_dim.2), calls=%async_computation | async-start | bytes 32768 | tf_op jit(solution)/shard_map/all_to_all | solution.py:215
  18.0 1.5 slice.10
  19.6 1.4 slice.9
  21.9 3.7 %all-to-all-done.index = s32[16,2,128]{2,1,0:T(2,128)S(1)} async-done(((s32[16,2,128]{2,1,0:T(2,128)}), s32[16,2,128]{2,1,0:T(2,128)S(1)}, u32[]{:S(2)}, u32[]{:S(2)}) %all-to-all-start) | async-done | bytes 16416 | tf_op jit(solution)/shard_map/all_to_all | solution.py:215
  25.6 3.3 %select.2 = (f32[8,128,128]{2,1,0:T(8,128)S(1)}, f32[8,128,128]{2,1,0:T(8,128)S(1)}) custom-call(s32[4]{0:T(128)S(1)} %pad_add_fusion.1.here.after, s32[16,2,128]{2,1,0:T(2,128)S(1)} %all-to-all-done.index, bf16[384,512]{1,0:T(8,128)(2,1)S(1)} %pad_maximum_fusion.1.rows, s32[4]{0:T(128)S(1)} %pad_add_fusion.1.here.after), custom_call_target="tpu_custom_call" | custom-call | flops 805306368 | bytes 1048576 | tf_op jit(solution)/shard_map/select/pallas_call | solution.py:58
  29.4 1.5 collective-permute-done
  31.0 4.9 %select.3 = (f32[8,384,128]{2,1,0:T(8,128)S(1)}, f32[8,384,128]{2,1,0:T(8,128)S(1)}) custom-call(s32[4]{0:T(128)S(1)} %pad_add_fusion.1.here.after, s32[16,2,128]{2,1,0:T(2,128)S(1)} %all-to-all-done.index, bf16[1152,512]{1,0:T(8,128)(2,1)S(1)} %pad_maximum_fusion.rows, f32[8,128,128]{2,1,0:T(8,128)S(1)} %add.12.after), custom_call_target="tpu_custom_call" | custom-call | flops 2415919104 | bytes 3145728 | tf_op jit(solution)/shard_map/select/pallas_call | solution.py:58
  36.2 3.3 %collective-permute-done.1 = f32[8,384,128]{2,1,0:T(8,128)S(1)} collective-permute-done((f32[8,384,128]{2,1,0:T(8,128)S(1)}, f32[8,384,128]{2,1,0:T(8,128)S(1)}, u32[]{:S(2)}, u32[]{:S(2)}) %collective-permute-start.1) | collective-permute-done | bytes 1572896 | tf_op jit(solution)/shard_map/ppermute | solution.py:228
  39.4 1.4 add.13
  40.9 24.0 %all_to_all.45.refs_0_ = f32[8,128,128]{2,1,0:T(8,128)S(1)} all-to-all(f32[8,128,128]{2,1,0:T(8,128)S(1)} %add.12.after), channel_id=1, replica_groups=mesh['z'=8,'core'=2,'x'=4,'y'=4] {'z'}, dimensions={0} | all-to-all | bytes 1048576 | tf_op jit(solution)/shard_map/all_to_all | solution.py:223
  64.9 1.2 sum_first.1
  66.8 7.6 %all-to-all-start.2 = ((f32[16,128,128]{2,1,0:T(8,128)}), f32[16,128,128]{2,1,0:T(8,128)S(1)}, u32[]{:S(2)}, u32[]{:S(2)}) async-start(f32[16,128,128]{2,1,0:T(8,128)} %get-tuple-element.18), calls=%async_computation.2 | async-start | bytes 2097152 | tf_op jit(solution)/shard_map/all_to_all | solution.py:199
  74.5 16.3 %all-to-all-done.2.refs_0_ = f32[16,128,128]{2,1,0:T(8,128)S(1)} async-done(((f32[16,128,128]{2,1,0:T(8,128)}), f32[16,128,128]{2,1,0:T(8,128)S(1)}, u32[]{:S(2)}, u32[]{:S(2)}) %all-to-all-start.2) | async-done | bytes 1048608 | tf_op jit(solution)/shard_map/all_to_all | solution.py:199
  90.8 2.3 %solve.4 = (f32[128,128]{1,0:T(8,128)S(1)}, f32[16,128,128]{2,1,0:T(8,128)S(1)}) custom-call(f32[16,128,128]{2,1,0:T(8,128)S(1)} %all-to-all-done.2.refs_0_, f32[4,128,2048]{2,1,0:T(8,128)} %refs_1_.7, f32[1,2048,128]{2,1,0:T(8,128)} %all-gather.3.cloned.1.call-done.refs_2_), custom_call_target="tpu_custom_call" | custom-call | tf_op jit(solution)/shard_map/solve/pallas_call | solution.py:166
  93.1 18.7 %all_to_all.46.refs_0_ = f32[16,128,128]{2,1,0:T(8,128)S(1)} all-to-all(f32[16,128,128]{2,1,0:T(8,128)S(1)} %get-tuple-element.19), channel_id=1, replica_groups=mesh['z'=8,'core'=2,'x'=4,'y'=4] {'x','y'}, dimensions={0} | all-to-all | bytes 2097152 | tf_op jit(solution)/shard_map/all_to_all | solution.py:199
  111.8 0.9 copy-done
  112.8 18.0 %all_to_all.47.refs_0_ = f32[16,128,128]{2,1,0:T(8,128)S(1)} all-to-all(f32[16,128,128]{2,1,0:T(8,128)S(1)} %subtract.3), channel_id=1, replica_groups=mesh['z'=8,'core'=2,'x'=4,'y'=4] {'x','y'}, dimensions={0} | all-to-all | bytes 2097152 | tf_op jit(solution)/shard_map/all_to_all | solution.py:199
  130.8 2.6 %solve.5 = (f32[128,128]{1,0:T(8,128)S(1)}, f32[16,128,128]{2,1,0:T(8,128)S(1)}) custom-call(f32[16,128,128]{2,1,0:T(8,128)S(1)} %all_to_all.47.refs_0_, f32[4,128,2048]{2,1,0:T(8,128)} %refs_1_.7, f32[5,2048,128]{2,1,0:T(8,128)} %all-gather.5.cloned.1.call-done.refs_2_.refs_3_.refs_4_, f32[5,2048,128]{2,1,0:T(8,128)} %all-gather.5.cloned.1.call-done.refs_2_.refs_3_.refs_4_, ...), custom_call_target="tpu_custom_call" | custom-call | tf_op jit(solution)/shard_map/solve/pallas_call | solution.py:166
  133.4 16.8 %all_to_all.48.refs_0_ = f32[16,128,128]{2,1,0:T(8,128)S(1)} all-to-all(f32[16,128,128]{2,1,0:T(8,128)S(1)} %get-tuple-element.24), channel_id=1, replica_groups=mesh['z'=8,'core'=2,'x'=4,'y'=4] {'x','y'}, dimensions={0} | all-to-all | bytes 2097152 | tf_op jit(solution)/shard_map/all_to_all | solution.py:199
  150.3 16.2 %all_to_all.49.refs_0_ = f32[16,128,128]{2,1,0:T(8,128)S(1)} all-to-all(f32[16,128,128]{2,1,0:T(8,128)S(1)} %subtract.4), channel_id=1, replica_groups=mesh['z'=8,'core'=2,'x'=4,'y'=4] {'x','y'}, dimensions={0} | all-to-all | bytes 2097152 | tf_op jit(solution)/shard_map/all_to_all | solution.py:199
  166.5 3.2 %solve.6 = (f32[128,128]{1,0:T(8,128)S(1)}, f32[16,128,128]{2,1,0:T(8,128)S(1)}) custom-call(f32[16,128,128]{2,1,0:T(8,128)S(1)} %all_to_all.49.refs_0_, f32[4,128,2048]{2,1,0:T(8,128)} %refs_1_.7, f32[5,2048,128]{2,1,0:T(8,128)} %all-gather.5.cloned.1.call-done.refs_2_.refs_3_.refs_4_, f32[5,2048,128]{2,1,0:T(8,128)} %all-gather.5.cloned.1.call-done.refs_2_.refs_3_.refs_4_, ...), custom_call_target="tpu_custom_call" | custom-call | tf_op jit(solution)/shard_map/solve/pallas_call | solution.py:166
  169.7 16.2 %all_to_all.50.refs_0_ = f32[16,128,128]{2,1,0:T(8,128)S(1)} all-to-all(f32[16,128,128]{2,1,0:T(8,128)S(1)} %get-tuple-element.26), channel_id=1, replica_groups=mesh['z'=8,'core'=2,'x'=4,'y'=4] {'x','y'}, dimensions={0} | all-to-all | bytes 2097152 | tf_op jit(solution)/shard_map/all_to_all | solution.py:199
  186.0 16.1 %all_to_all.51.refs_0_ = f32[16,128,128]{2,1,0:T(8,128)S(1)} all-to-all(f32[16,128,128]{2,1,0:T(8,128)S(1)} %subtract.5), channel_id=1, replica_groups=mesh['z'=8,'core'=2,'x'=4,'y'=4] {'x','y'}, dimensions={0} | all-to-all | bytes 2097152 | tf_op jit(solution)/shard_map/all_to_all | solution.py:199
  202.1 2.4 %solve.7 = (f32[4,128,128]{2,1,0:T(8,128)}, f32[4,128,128]{2,1,0:T(8,128)}) custom-call(f32[16,128,128]{2,1,0:T(8,128)S(1)} %all_to_all.51.refs_0_, f32[4,128,2048]{2,1,0:T(8,128)} %refs_1_.7, f32[128,128]{1,0:T(8,128)S(1)} %get-tuple-element.23.refs_4_.refs_5_.refs_2_, f32[128,128]{1,0:T(8,128)S(1)} %get-tuple-element.25.refs_6_.refs_3_, ...), custom_call_target="tpu_custom_call" | custom-call | tf_op jit(solution)/shard_map/solve/pallas_call | solution.py:166
  (34 shorter events, 4.3 us)
Async XLA Ops:
  8.0 13.3 %copy-start.3 = (f32[512,4,128]{2,1,0:T(4,128)S(1)}, f32[512,4,128]{2,1,0:T(4,128)}, u32[]{:S(2)}) copy-start(f32[512,4,128]{2,1,0:T(4,128)} %param.7) | copy-start | bytes 3145732
  9.4 16.2 %all-to-all-start = ((s32[16,2,128]{2,1,0:T(2,128)}), s32[16,2,128]{2,1,0:T(2,128)S(1)}, u32[]{:S(2)}, u32[]{:S(2)}) async-start(s32[16,2,128]{2,1,0:T(2,128)} %broadcast_in_dim.2), calls=%async_computation | async-start | bytes 32768 | tf_op jit(solution)/shard_map/all_to_all | solution.py:215
  18.0 56.5 %all-gather.3.cloned.1.call-start = ((), (), s32[]{:S(2)}) async-start(), calls=%async_computation.10 | async-start | bytes 1114112 | tf_op jit(solution)/shard_map/all_gather | solution.py:209
  19.5 92.3 %reduce-scatter.2.cloned.1.call-start = ((), (), s32[]{:S(2)}) async-start(), calls=%async_computation.11 | async-start | bytes 1769472 | tf_op jit(solution)/shard_map/reduce_scatter | solution.py:229
  28.9 2.0 collective-permute-start
  36.0 3.5 %collective-permute-start.1 = (f32[8,384,128]{2,1,0:T(8,128)S(1)}, f32[8,384,128]{2,1,0:T(8,128)S(1)}, u32[]{:S(2)}, u32[]{:S(2)}) collective-permute-start(f32[8,384,128]{2,1,0:T(8,128)S(1)} %get-tuple-element.21), channel_id=1, source_target_pairs={{0,16},{16,0},{1,17},{17,1},{2,18},{18,2},{3,19},{19,3},{4,20},{20... | collective-permute-start | bytes 4718600 | tf_op jit(solution)/shard_map/ppermute | solution.py:228
  40.8 25.2 %copy-start.2 = (f32[6,128,128]{2,1,0:T(8,128)S(1)}, f32[6,128,128]{2,1,0:T(8,128)}, u32[]{:S(2)}) copy-start(f32[6,128,128]{2,1,0:T(8,128)} %blocks.1) | copy-start | bytes 1179652
  40.8 90.0 %all-gather.5.cloned.1.call-start = ((), (), s32[]{:S(2)}) async-start(), calls=%async_computation.12 | async-start | bytes 5570560 | tf_op jit(solution)/shard_map/all_gather | solution.py:209
  66.8 23.9 %all-to-all-start.2 = ((f32[16,128,128]{2,1,0:T(8,128)}), f32[16,128,128]{2,1,0:T(8,128)S(1)}, u32[]{:S(2)}, u32[]{:S(2)}) async-start(f32[16,128,128]{2,1,0:T(8,128)} %get-tuple-element.18), calls=%async_computation.2 | async-start | bytes 2097152 | tf_op jit(solution)/shard_map/all_to_all | solution.py:199
  111.8 0.9 copy-start
  133.4 16.8 %copy-start.1 = (f32[384,128]{1,0:T(8,128)S(1)}, f32[384,128]{1,0:T(8,128)}, u32[]{:S(2)}) copy-start(f32[384,128]{1,0:T(8,128)} %reduce-scatter.2.cloned.1.call-done) | copy-start | bytes 589828
Sparse Core Ops, SparseCore 0:
  21.2 46.4 all-gather.2
  69.6 44.1 all-gather.4
Sparse Core Ops, SparseCore 1:
  40.9 43.4 reduce-scatter.1
